TPU v7x, 32 devices: a whole 2x2x4 slice. The times are simulated.
32 devices in a mesh: ev: 4 (over x, core), gx: 2 (over y), gy: 4 (over z).
Axes of the slice: x: 2, y: 2, z: 4, core: 2. Of those that a mesh axis runs over, the one named last changes fastest.
Arguments:
- adjoint_now: float32 [8, 3, 16, 32, 128], P('ev', None, 'gx', 'gy'), may hold values from -6 to 6
- adjoint_prev: float32 [8, 3, 16, 32, 128], P('ev', None, 'gx', 'gy'), may hold values from -6 to 6
- forward: bfloat16 [8, 4, 3, 16, 32, 128], P('ev', None, None, 'gx', 'gy'), may hold values from -6 to 6
- medium: float32 [4, 16, 32, 128], P(None, 'gx', 'gy'), may hold values from 0.5 to 2
- drm_cells: int32 [2, 4, 128], P('gx', 'gy'), may hold values from 0 to 8191, as said below
- drm_force: float32 [8, 2, 3, 2, 4, 128], P('ev', None, None, 'gx', 'gy'), may hold values from -320 to 320
Outputs:
- adjoint_mid: float32 [8, 3, 16, 32, 128], P('ev', None, 'gx', 'gy')
- adjoint_next: float32 [8, 3, 16, 32, 128], P('ev', None, 'gx', 'gy')
- grad_shear: float32 [16, 32, 128], P('gx', 'gy', 'ev')
- grad_density: float32 [16, 32, 128], P('gx', 'gy', 'ev')
Inputs may be any that keep to these rules, and one draw needn't show every extreme that they name: `drm_cells`: each entry is the local flat index (x * 8 + y) * 128 + z of a cell of its own tile that lies within 2 cells of the grid's bottom or of one of the grid's outer lateral faces; entries may repeat.
All inputs are finite; a program needn't handle non-finite values.
Results may differ from a plain program's by a relative error of at most 0.0011.
Values may be sent and summed in bfloat16 or wider, within the bound.
No kernel may reach another device: no remote copies, remote signals or barrier semaphores. Data moves between devices by JAX's collectives and lax.ppermute only.
A program may use at most 128 MiB of HBM per device.

v0:
```python
import jax
import jax.numpy as jnp
from jax import lax
from jax.sharding import PartitionSpec as P

STEP_FACTOR = 0.01
UNITS = ((1, 0, 0), (0, 1, 0), (0, 0, 1))


def with_halo(cells, sides, width):
    for axis, dim in sides:
        count = lax.axis_size(axis)
        ends = count - 1
        head = lax.slice_in_dim(cells, 0, width, axis=dim)
        tail = lax.slice_in_dim(cells, cells.shape[dim] - width, cells.shape[dim], axis=dim)
        cells = jnp.concatenate(
            [
                lax.ppermute(tail, axis, [(i, (i + 1) % count) for i in range(ends)]),
                cells,
                lax.ppermute(head, axis, [((i + 1) % count, i) for i in range(ends)]),
            ],
            axis=dim,
        )
    return cells


def offset(array, shift_x, shift_y, shift_z):
    size_x, size_y, size_z = array.shape[-3:]
    return array[
        ...,
        1 + shift_x : size_x - 1 + shift_x,
        1 + shift_y : size_y - 1 + shift_y,
        1 + shift_z : size_z - 1 + shift_z,
    ]


def negate(vector):
    return tuple((-entry for entry in vector))


def operate(field, medium):
    field_pad = jnp.pad(field, ((0, 0), (0, 0), (0, 0), (0, 0), (1, 1)))
    medium_pad = jnp.pad(medium, ((0, 0), (0, 0), (0, 0), (1, 1)))
    shear = medium_pad[0]
    lame = medium_pad[1]
    inverse = medium_pad[3]
    bulk = lame + shear
    inverse_here = offset(inverse, 0, 0, 0)
    results = []
    for component in range(3):
        displaced = field_pad[:, component]
        total = jnp.zeros(displaced.shape[:1] + inverse_here.shape, jnp.float32)
        for direction in range(3):
            upper = UNITS[direction]
            lower = negate(upper)
            modulus = lame + 2.0 * shear if direction == component else shear
            here = offset(modulus, 0, 0, 0)
            face_up = 0.5 * (here + offset(modulus, *upper))
            face_down = 0.5 * (offset(modulus, *lower) + here)
            if direction == 2:
                face_up = face_up * 0.5 * (inverse_here + offset(inverse, *upper))
                face_down = face_down * 0.5 * (offset(inverse, *lower) + inverse_here)
            centre = offset(displaced, 0, 0, 0)
            term = face_up * (offset(displaced, *upper) - centre) - face_down * (
                centre - offset(displaced, *lower)
            )
            if direction == 2:
                term = term * inverse_here
            total = total + term
        for other in range(3):
            if other == component:
                continue
            partner = field_pad[:, other]
            values = []
            for sign in (1, -1):
                shift = tuple((sign * entry for entry in UNITS[component]))
                plus = tuple((shift[index] + UNITS[other][index] for index in range(3)))
                minus = tuple((shift[index] - UNITS[other][index] for index in range(3)))
                slope = 0.5 * (offset(partner, *plus) - offset(partner, *minus))
                if other == 2:
                    slope = slope * offset(inverse, *shift)
                values.append(slope * offset(bulk, *shift))
            term = 0.5 * (values[0] - values[1])
            if component == 2:
                term = term * inverse_here
            total = total + term
        results.append(total)
    return jnp.stack(results, axis=1)


def operate_each(field, medium):

    def single(event_field):
        return operate(event_field[None], medium)[0]

    return lax.map(single, field)


def shear_term(adjoint_rim, forward_rim, inverse_own):
    adjoint_pad = jnp.pad(adjoint_rim, ((0, 0), (0, 0), (0, 0), (0, 0), (1, 1)))
    forward_pad = jnp.pad(forward_rim, ((0, 0), (0, 0), (0, 0), (0, 0), (1, 1)))
    total = jnp.zeros(inverse_own.shape, jnp.float32)
    for direction in range(3):
        upper = UNITS[direction]
        lower = negate(upper)
        slope_a = 0.5 * (offset(adjoint_pad, *upper) - offset(adjoint_pad, *lower))
        slope_f = 0.5 * (offset(forward_pad, *upper) - offset(forward_pad, *lower))
        product = jnp.sum(slope_a * slope_f, axis=(0, 1))
        if direction == 2:
            product = product * inverse_own * inverse_own
        total = total - product
    return total


def density_term(adjoint_own, newer, middle, older):
    second = (
        newer.astype(jnp.float32) - 2.0 * middle.astype(jnp.float32) + older.astype(jnp.float32)
    )
    return -jnp.sum(adjoint_own * second, axis=(0, 1))


def body(adjoint_now, adjoint_prev, forward, medium, drm_cells, drm_force):
    events_here, _, width_x, width_y, depth = adjoint_now.shape
    cells = drm_cells[0, 0]
    force_values = drm_force[:, :, :, 0, 0, :]
    forces = jnp.zeros((events_here, 2, 3, width_x * width_y * depth), jnp.float32)
    forces = forces.at[:, :, :, cells].add(force_values)
    forces = forces.reshape(events_here, 2, 3, width_x, width_y, depth)
    buoyancy = medium[2]
    inverse_own = medium[3]
    rim_width = 1
    medium_rim = with_halo(medium.astype(jnp.bfloat16), (("gx", 1), ("gy", 2)), rim_width).astype(
        medium.dtype
    )
    forward_rim = with_halo(forward[:, 1:3], (("gx", 3), ("gy", 4)), 1)
    shear_total = jnp.zeros((width_x, width_y, depth), jnp.float32)
    density_total = jnp.zeros((width_x, width_y, depth), jnp.float32)
    current = adjoint_now
    previous = adjoint_prev
    for step in range(2):
        current_rim = with_halo(current, (("gx", 2), ("gy", 3)), 1)
        shear_total = shear_total + shear_term(
            current_rim, forward_rim[:, step].astype(jnp.float32), inverse_own
        )
        density_total = density_total + density_term(
            current, forward[:, step], forward[:, step + 1], forward[:, step + 2]
        )
        applied = operate_each(current_rim, medium_rim)
        following = 2.0 * current - previous + STEP_FACTOR * buoyancy * (applied + forces[:, step])
        previous, current = (current, following)
    totals = (shear_total, density_total)
    whole = lax.psum((totals[0], totals[1]), "ev")
    piece = depth // lax.axis_size("ev")
    start = lax.axis_index("ev") * piece
    shares = tuple((lax.dynamic_slice_in_dim(item, start, piece, 2) for item in whole))
    scale = 1.0 / (events_here * lax.axis_size("ev"))
    return (previous, current, shares[0] * scale, shares[1] * scale)


def solution(mesh):
    in_specs = (
        P("ev", None, "gx", "gy", None),
        P("ev", None, "gx", "gy", None),
        P("ev", None, None, "gx", "gy", None),
        P(None, "gx", "gy", None),
        P("gx", "gy", None),
        P("ev", None, None, "gx", "gy", None),
    )
    out_specs = (
        P("ev", None, "gx", "gy", None),
        P("ev", None, "gx", "gy", None),
        P("gx", "gy", "ev"),
        P("gx", "gy", "ev"),
    )
    return jax.shard_map(body, mesh=mesh, in_specs=in_specs, out_specs=out_specs, check_vma=False)
```

profile of v0, /device:TPU:0, one launch (start us, length us, event | category | flops | bytes accessed | tf_op | source)
XLA Modules:
  0.0 179.0 jit_solution(5548861196468526104)
XLA Ops:
  7.2 0.9 convert_element_type.59
  8.1 4.9 %collective-permute-start = (bf16[4,1,8,128]{3,2,1,0:T(8,128)(2,1)S(1)}, bf16[4,1,8,128]{3,2,1,0:T(8,128)(2,1)S(1)}, u32[]{:S(2)}, u32[]{:S(2)}) collective-permute-start(bf16[4,1,8,128]{3,2,1,0:T(8,128)(2,1)S(1)} %get-tuple-element.216), channel_id=1, source_target_pairs={{0,4},{1,5},{2,6},{3,7},{8,12},{9,13},{10,14},{11,15},{16,20},{17,... | collective-permute-start | bytes 24584 | tf_op jit(solution)/shard_map/ppermute | solution.py:18
  13.0 1.3 collective-permute-start.1
  15.1 4.5 %collective-permute-start.4 = (f32[2,3,1,8,128]{4,3,2,1,0:T(8,128)S(1)}, f32[2,3,1,8,128]{4,3,2,1,0:T(8,128)S(1)}, u32[]{:S(2)}, u32[]{:S(2)}) collective-permute-start(f32[2,3,1,8,128]{4,3,2,1,0:T(8,128)S(1)} %get-tuple-element.213), channel_id=1, source_target_pairs={{0,4},{1,5},{2,6},{3,7},{8,12},{9,13},{10,14},{11,15},{16,20},{17,... | collective-permute-start | bytes 73736 | tf_op jit(solution)/shard_map/ppermute | solution.py:18
  19.6 1.3 collective-permute-start.5
  21.7 4.5 %collective-permute-start.12 = (bf16[2,2,3,1,8,128]{5,4,3,2,0,1:T(8,128)(2,1)S(1)}, bf16[2,2,3,1,8,128]{5,4,3,2,0,1:T(8,128)(2,1)S(1)}, u32[]{:S(2)}, u32[]{:S(2)}) collective-permute-start(bf16[2,2,3,1,8,128]{5,4,3,2,0,1:T(8,128)(2,1)S(1)} %copy.34), channel_id=1, source_target_pairs={{0,4},{1,5},{2,6},{3,7},{8,12},{9,13},{10,14},{11,15},{16,20},{17,... | collective-permute-start | bytes 73736 | tf_op jit(solution)/shard_map/ppermute | solution.py:18
  26.3 0.9 copy.31
  27.8 6.0 %broadcast_in_dim.365 = f32[2,2,3,8192]{2,1,3,0:T(2,128)} broadcast(f32[]{:T(128)} %constant.107.clone.1), dimensions={} | broadcast | bytes 393220 | tf_op jit(solution)/shard_map/broadcast_in_dim | solution.py:126
  33.8 13.3 %scatter_fusion = f32[2,2,3,8192]{2,1,3,0:T(2,128)} fusion(f32[2,2,3,8192]{2,1,3,0:T(2,128)} %broadcast_in_dim.365, s32[128]{0:T(128)S(1)} %fusion.291, f32[128,2,2,3]{3,2,1,0:T(2,128)S(1)} %bitcast.498), kind=kCustom, calls=%fused_computation | custom fusion | flops 1536 | bytes 18944 | tf_op jit(solution)/shard_map/scatter-add | solution.py:127
  47.1 20.8 %fusion.297 = (f32[2,1,3,8,8,128]{2,1,5,4,3,0:T(1,128)}, f32[2,1,3,8,8,128]{2,1,5,4,3,0:T(1,128)}) fusion(f32[2,2,3,8,8,128]{2,1,5,4,3,0:T(2,128)} %bitcast.497), kind=kLoop, calls=%fused_computation.474 | loop fusion | bytes 786432 | tf_op jit(solution)/shard_map/slice | solution.py:149
  68.0 3.7 %collective-permute-start.2 = (bf16[4,10,1,128]{3,2,1,0:T(2,128)(2,1)S(1)}, bf16[4,10,1,128]{3,2,1,0:T(2,128)(2,1)S(1)}, u32[]{:S(2)}, u32[]{:S(2)}) collective-permute-start(bf16[4,10,1,128]{3,2,1,0:T(2,128)(2,1)S(1)} %get-tuple-element.214), channel_id=1, source_target_pairs={{0,1},{1,2},{2,3},{4,5},{5,6},{6,7},{8,9},{9,10},{10,11},{12,13},{... | collective-permute-start | bytes 30728 | tf_op jit(solution)/shard_map/ppermute | solution.py:18
  71.7 1.3 collective-permute-start.3
  73.0 10.3 %copy.32 = f32[2,1,3,8,8,128]{5,4,3,2,0,1:T(8,128)S(1)} copy(f32[2,1,3,8,8,128]{2,1,5,4,3,0:T(1,128)} %get-tuple-element.198) | data formatting | bytes 393216
  83.4 10.3 %copy.33 = f32[2,1,3,8,8,128]{5,4,3,2,0,1:T(8,128)S(1)} copy(f32[2,1,3,8,8,128]{2,1,5,4,3,0:T(1,128)} %get-tuple-element.197) | data formatting | bytes 393216
  93.7 1.4 collective-permute-start.13
  95.4 5.1 %collective-permute-start.6 = (f32[2,3,10,1,128]{4,3,2,1,0:T(1,128)S(1)}, f32[2,3,10,1,128]{4,3,2,1,0:T(1,128)}, u32[]{:S(2)}, u32[]{:S(2)}) collective-permute-start(f32[2,3,10,1,128]{4,3,2,1,0:T(1,128)S(1)} %get-tuple-element.207), channel_id=1, source_target_pairs={{0,1},{1,2},{2,3},{4,5},{5,6},{6,7},{8,9},{9,10},{10,11},{12,13},{... | collective-permute-start | bytes 92168 | tf_op jit(solution)/shard_map/ppermute | solution.py:18
  100.6 1.3 collective-permute-start.7
  102.0 4.5 %collective-permute-start.14 = (bf16[2,2,3,10,1,128]{5,4,3,2,0,1:T(2,128)(2,1)S(1)}, bf16[2,2,3,10,1,128]{5,4,3,2,0,1:T(2,128)(2,1)S(1)}, u32[]{:S(2)}, u32[]{:S(2)}) collective-permute-start(bf16[2,2,3,10,1,128]{5,4,3,2,0,1:T(2,128)(2,1)S(1)} %get-tuple-element.203), channel_id=1, source_target_pairs={{0,1},{1,2},{2,3},{4,5},{5,6},{6,7},{8,9},{9,10},{10,11},{12,13},{... | collective-permute-start | bytes 92168 | tf_op jit(solution)/shard_map/ppermute | solution.py:18
  106.6 1.3 collective-permute-start.15
  108.5 0.8 pad_maximum_fusion
  109.4 2.9 %while.26 = (s32[]{:T(128)}, f32[2,3,8,8,128]{4,3,2,1,0:T(8,128)S(1)}, f32[4,10,10,128]{3,2,1,0:T(8,128)S(1)}, f32[2,3,10,10,128]{4,3,2,1,0:T(8,128)S(1)}, s32[]{:T(128)}) while((s32[]{:T(128)}, f32[2,3,8,8,128]{4,3,2,1,0:T(8,128)S(1)}, f32[4,10,10,128]{3,2,1,0:T(8,128)S(1)}, f32[2,3,10,10,128]{4,3,2,1,0:T(8,128)S(1)}, s32[]{:T(128)}) %tuple.103), condition=%wide.region_1.2_spmd, body=%wide.region_0.0_spmd.sunk | while | flops 1349722 | bytes 4412965 | solution.py:96
  112.5 4.5 %collective-permute-start.8 = (f32[2,3,1,8,128]{4,3,2,1,0:T(8,128)S(1)}, f32[2,3,1,8,128]{4,3,2,1,0:T(8,128)S(1)}, u32[]{:S(2)}, u32[]{:S(2)}) collective-permute-start(f32[2,3,1,8,128]{4,3,2,1,0:T(8,128)S(1)} %get-tuple-element.210), channel_id=1, source_target_pairs={{0,4},{1,5},{2,6},{3,7},{8,12},{9,13},{10,14},{11,15},{16,20},{17,... | collective-permute-start | bytes 73736 | tf_op jit(solution)/shard_map/ppermute | solution.py:18
  117.1 1.3 collective-permute-start.9
  118.8 4.0 %collective-permute-done.9 = f32[2,3,1,8,128]{4,3,2,1,0:T(8,128)S(1)} collective-permute-done((f32[2,3,1,8,128]{4,3,2,1,0:T(8,128)S(1)}, f32[2,3,1,8,128]{4,3,2,1,0:T(8,128)S(1)}, u32[]{:S(2)}, u32[]{:S(2)}) %collective-permute-start.9) | collective-permute-done | bytes 24608 | tf_op jit(solution)/shard_map/ppermute | solution.py:20
  122.8 4.5 %collective-permute-start.10 = (f32[2,3,10,1,128]{4,3,2,1,0:T(1,128)S(1)}, f32[2,3,10,1,128]{4,3,2,1,0:T(1,128)S(1)}, u32[]{:S(2)}, u32[]{:S(2)}) collective-permute-start(f32[2,3,10,1,128]{4,3,2,1,0:T(1,128)S(1)} %get-tuple-element.205), channel_id=1, source_target_pairs={{0,1},{1,2},{2,3},{4,5},{5,6},{6,7},{8,9},{9,10},{10,11},{12,13},{... | collective-permute-start | bytes 92168 | tf_op jit(solution)/shard_map/ppermute | solution.py:18
  127.4 1.3 collective-permute-start.11
  129.3 3.9 %collective-permute-done.11 = f32[2,3,10,1,128]{4,3,2,1,0:T(1,128)S(1)} collective-permute-done((f32[2,3,10,1,128]{4,3,2,1,0:T(1,128)S(1)}, f32[2,3,10,1,128]{4,3,2,1,0:T(1,128)S(1)}, u32[]{:S(2)}, u32[]{:S(2)}) %collective-permute-start.11) | collective-permute-done | bytes 30752 | tf_op jit(solution)/shard_map/ppermute | solution.py:20
  133.9 2.9 %while.27 = (s32[]{:T(128)}, f32[2,3,8,8,128]{4,3,2,1,0:T(8,128)S(1)}, f32[4,10,10,128]{3,2,1,0:T(8,128)S(1)}, f32[2,3,10,10,128]{4,3,2,1,0:T(8,128)S(1)}, s32[]{:T(128)}) while((s32[]{:T(128)}, f32[2,3,8,8,128]{4,3,2,1,0:T(8,128)S(1)}, f32[4,10,10,128]{3,2,1,0:T(8,128)S(1)}, f32[2,3,10,10,128]{4,3,2,1,0:T(8,128)S(1)}, s32[]{:T(128)}) %tuple.112), condition=%wide.region_4.5_spmd, body=%wide.region_3.4_spmd.sunk | while | flops 1349722 | bytes 4412965 | solution.py:96
  136.9 1.2 fusion.271
  138.0 1.9 %fusion.281 = (f32[8,8,128]{2,1,0:T(8,128)S(1)}, f32[8,8,128]{2,1,0:T(8,128)S(1)}, f32[8,8,128]{2,1,0:T(8,128)S(1)}, f32[2,3,8,8,128]{4,3,2,1,0:T(8,128)}) fusion(f32[2,3,10,10,128]{4,3,2,1,0:T(8,128)S(1)} %get-tuple-element.200, f32[2,3,8,8,128]{4,3,2,1,0:T(8,128)S(1)} %copy-done.1, f32[2,3,1,8,128]{4,3,2,1,0:T(8,128)} %copy-done.8, ...), kind=kLoop, calls=%fused_computation.439 | loop fusion | flops 1302528 | bytes 3239936 | tf_op jit(solution)/shard_map/reduce_sum | solution.py:108
  140.6 30.1 %all-reduce.11.cloned.1.call-done = (f32[8,8,128]{2,1,0:T(8,128)}, f32[8,8,128]{2,1,0:T(8,128)}) async-done(((f32[8,8,128]{2,1,0:T(8,128)}, f32[8,8,128]{2,1,0:T(8,128)}), (f32[8,8,128]{2,1,0:T(8,128)}, f32[8,8,128]{2,1,0:T(8,128)})) %all-reduce.11.cloned.1.call-update) | async-done | bytes 65552 | tf_op jit(solution)/shard_map/psum | solution.py:152
  170.6 1.5 dynamic-slice_multiply_fusion
  (95 shorter events, 11.4 us)
Async XLA Ops:
  7.2 163.5 %all-reduce.11.cloned.1.call-start = ((), (), s32[]{:S(2)}) async-start(), calls=%async_computation | async-start | bytes 131072 | tf_op jit(solution)/shard_map/psum | solution.py:152
  8.1 59.8 %collective-permute-start = (bf16[4,1,8,128]{3,2,1,0:T(8,128)(2,1)S(1)}, bf16[4,1,8,128]{3,2,1,0:T(8,128)(2,1)S(1)}, u32[]{:S(2)}, u32[]{:S(2)}) collective-permute-start(bf16[4,1,8,128]{3,2,1,0:T(8,128)(2,1)S(1)} %get-tuple-element.216), channel_id=1, source_target_pairs={{0,4},{1,5},{2,6},{3,7},{8,12},{9,13},{10,14},{11,15},{16,20},{17,... | collective-permute-start | bytes 24584 | tf_op jit(solution)/shard_map/ppermute | solution.py:18
  13.0 55.0 %collective-permute-start.1 = (bf16[4,1,8,128]{3,2,1,0:T(8,128)(2,1)S(1)}, bf16[4,1,8,128]{3,2,1,0:T(8,128)(2,1)S(1)}, u32[]{:S(2)}, u32[]{:S(2)}) collective-permute-start(bf16[4,1,8,128]{3,2,1,0:T(8,128)(2,1)S(1)} %get-tuple-element.217), channel_id=1, source_target_pairs={{4,0},{5,1},{6,2},{7,3},{12,8},{13,9},{14,10},{15,11},{20,16},{21,... | collective-permute-start | bytes 24584 | tf_op jit(solution)/shard_map/ppermute | solution.py:20
  15.1 80.2 %collective-permute-start.4 = (f32[2,3,1,8,128]{4,3,2,1,0:T(8,128)S(1)}, f32[2,3,1,8,128]{4,3,2,1,0:T(8,128)S(1)}, u32[]{:S(2)}, u32[]{:S(2)}) collective-permute-start(f32[2,3,1,8,128]{4,3,2,1,0:T(8,128)S(1)} %get-tuple-element.213), channel_id=1, source_target_pairs={{0,4},{1,5},{2,6},{3,7},{8,12},{9,13},{10,14},{11,15},{16,20},{17,... | collective-permute-start | bytes 73736 | tf_op jit(solution)/shard_map/ppermute | solution.py:18
  19.6 75.7 %collective-permute-start.5 = (f32[2,3,1,8,128]{4,3,2,1,0:T(8,128)S(1)}, f32[2,3,1,8,128]{4,3,2,1,0:T(8,128)S(1)}, u32[]{:S(2)}, u32[]{:S(2)}) collective-permute-start(f32[2,3,1,8,128]{4,3,2,1,0:T(8,128)S(1)} %get-tuple-element.212), channel_id=1, source_target_pairs={{4,0},{5,1},{6,2},{7,3},{12,8},{13,9},{14,10},{15,11},{20,16},{21,... | collective-permute-start | bytes 73736 | tf_op jit(solution)/shard_map/ppermute | solution.py:20
  21.7 80.1 %collective-permute-start.12 = (bf16[2,2,3,1,8,128]{5,4,3,2,0,1:T(8,128)(2,1)S(1)}, bf16[2,2,3,1,8,128]{5,4,3,2,0,1:T(8,128)(2,1)S(1)}, u32[]{:S(2)}, u32[]{:S(2)}) collective-permute-start(bf16[2,2,3,1,8,128]{5,4,3,2,0,1:T(8,128)(2,1)S(1)} %copy.34), channel_id=1, source_target_pairs={{0,4},{1,5},{2,6},{3,7},{8,12},{9,13},{10,14},{11,15},{16,20},{17,... | collective-permute-start | bytes 73736 | tf_op jit(solution)/shard_map/ppermute | solution.py:18
  47.1 25.9 %copy-start.3 = (f32[4,8,8,128]{3,2,1,0:T(8,128)S(1)}, f32[4,8,8,128]{3,2,1,0:T(8,128)}, u32[]{:S(2)}) copy-start(f32[4,8,8,128]{3,2,1,0:T(8,128)} %param.13) | copy-start | bytes 393220
  67.9 27.3 %copy-start.1 = (f32[2,3,8,8,128]{4,3,2,1,0:T(8,128)S(1)}, f32[2,3,8,8,128]{4,3,2,1,0:T(8,128)}, u32[]{:S(2)}) copy-start(f32[2,3,8,8,128]{4,3,2,1,0:T(8,128)} %param.10) | copy-start | bytes 589828
  68.0 33.9 %copy-start.2 = (bf16[2,4,3,8,8,128]{5,4,3,2,1,0:T(8,128)(2,1)S(1)}, bf16[2,4,3,8,8,128]{5,4,3,2,1,0:T(8,128)(2,1)}, u32[]{:S(2)}) copy-start(bf16[2,4,3,8,8,128]{5,4,3,2,1,0:T(8,128)(2,1)} %param.12) | copy-start | bytes 1179652
  68.0 25.7 %collective-permute-start.2 = (bf16[4,10,1,128]{3,2,1,0:T(2,128)(2,1)S(1)}, bf16[4,10,1,128]{3,2,1,0:T(2,128)(2,1)S(1)}, u32[]{:S(2)}, u32[]{:S(2)}) collective-permute-start(bf16[4,10,1,128]{3,2,1,0:T(2,128)(2,1)S(1)} %get-tuple-element.214), channel_id=1, source_target_pairs={{0,1},{1,2},{2,3},{4,5},{5,6},{6,7},{8,9},{9,10},{10,11},{12,13},{... | collective-permute-start | bytes 30728 | tf_op jit(solution)/shard_map/ppermute | solution.py:18
  71.7 23.4 %collective-permute-start.3 = (bf16[4,10,1,128]{3,2,1,0:T(2,128)(2,1)S(1)}, bf16[4,10,1,128]{3,2,1,0:T(2,128)(2,1)S(1)}, u32[]{:S(2)}, u32[]{:S(2)}) collective-permute-start(bf16[4,10,1,128]{3,2,1,0:T(2,128)(2,1)S(1)} %get-tuple-element.215), channel_id=1, source_target_pairs={{1,0},{2,1},{3,2},{5,4},{6,5},{7,6},{9,8},{10,9},{11,10},{13,12},{... | collective-permute-start | bytes 30728 | tf_op jit(solution)/shard_map/ppermute | solution.py:20
  93.7 18.6 %copy-start.4 = (f32[2,3,8,8,128]{4,3,2,1,0:T(8,128)S(1)}, f32[2,3,8,8,128]{4,3,2,1,0:T(8,128)}, u32[]{:S(2)}) copy-start(f32[2,3,8,8,128]{4,3,2,1,0:T(8,128)} %param.11) | copy-start | bytes 589828
  93.7 8.2 %collective-permute-start.13 = (bf16[2,2,3,1,8,128]{5,4,3,2,0,1:T(8,128)(2,1)S(1)}, bf16[2,2,3,1,8,128]{5,4,3,2,0,1:T(8,128)(2,1)S(1)}, u32[]{:S(2)}, u32[]{:S(2)}) collective-permute-start(bf16[2,2,3,1,8,128]{5,4,3,2,0,1:T(8,128)(2,1)S(1)} %copy.36), channel_id=1, source_target_pairs={{4,0},{5,1},{6,2},{7,3},{12,8},{13,9},{14,10},{15,11},{20,16},{21,... | collective-permute-start | bytes 73736 | tf_op jit(solution)/shard_map/ppermute | solution.py:20
  95.3 5.3 %copy-start.8 = (f32[2,3,1,8,128]{4,3,2,1,0:T(8,128)}, f32[2,3,1,8,128]{4,3,2,1,0:T(8,128)S(1)}, u32[]{:S(2)}) copy-start(f32[2,3,1,8,128]{4,3,2,1,0:T(8,128)S(1)} %collective-permute-done.4) | copy-start | bytes 73732
  95.3 5.2 %copy-start.9 = (f32[2,3,1,8,128]{4,3,2,1,0:T(8,128)}, f32[2,3,1,8,128]{4,3,2,1,0:T(8,128)S(1)}, u32[]{:S(2)}) copy-start(f32[2,3,1,8,128]{4,3,2,1,0:T(8,128)S(1)} %collective-permute-done.5) | copy-start | bytes 73732
  95.4 12.5 %collective-permute-start.6 = (f32[2,3,10,1,128]{4,3,2,1,0:T(1,128)S(1)}, f32[2,3,10,1,128]{4,3,2,1,0:T(1,128)}, u32[]{:S(2)}, u32[]{:S(2)}) collective-permute-start(f32[2,3,10,1,128]{4,3,2,1,0:T(1,128)S(1)} %get-tuple-element.207), channel_id=1, source_target_pairs={{0,1},{1,2},{2,3},{4,5},{5,6},{6,7},{8,9},{9,10},{10,11},{12,13},{... | collective-permute-start | bytes 92168 | tf_op jit(solution)/shard_map/ppermute | solution.py:18
  100.6 7.3 %collective-permute-start.7 = (f32[2,3,10,1,128]{4,3,2,1,0:T(1,128)S(1)}, f32[2,3,10,1,128]{4,3,2,1,0:T(1,128)S(1)}, u32[]{:S(2)}, u32[]{:S(2)}) collective-permute-start(f32[2,3,10,1,128]{4,3,2,1,0:T(1,128)S(1)} %get-tuple-element.208), channel_id=1, source_target_pairs={{1,0},{2,1},{3,2},{5,4},{6,5},{7,6},{9,8},{10,9},{11,10},{13,12},{... | collective-permute-start | bytes 92168 | tf_op jit(solution)/shard_map/ppermute | solution.py:20
  102.0 16.3 %collective-permute-start.14 = (bf16[2,2,3,10,1,128]{5,4,3,2,0,1:T(2,128)(2,1)S(1)}, bf16[2,2,3,10,1,128]{5,4,3,2,0,1:T(2,128)(2,1)S(1)}, u32[]{:S(2)}, u32[]{:S(2)}) collective-permute-start(bf16[2,2,3,10,1,128]{5,4,3,2,0,1:T(2,128)(2,1)S(1)} %get-tuple-element.203), channel_id=1, source_target_pairs={{0,1},{1,2},{2,3},{4,5},{5,6},{6,7},{8,9},{9,10},{10,11},{12,13},{... | collective-permute-start | bytes 92168 | tf_op jit(solution)/shard_map/ppermute | solution.py:18
  106.6 11.8 %collective-permute-start.15 = (bf16[2,2,3,10,1,128]{5,4,3,2,0,1:T(2,128)(2,1)S(1)}, bf16[2,2,3,10,1,128]{5,4,3,2,0,1:T(2,128)(2,1)S(1)}, u32[]{:S(2)}, u32[]{:S(2)}) collective-permute-start(bf16[2,2,3,10,1,128]{5,4,3,2,0,1:T(2,128)(2,1)S(1)} %get-tuple-element.204), channel_id=1, source_target_pairs={{1,0},{2,1},{3,2},{5,4},{6,5},{7,6},{9,8},{10,9},{11,10},{13,12},{... | collective-permute-start | bytes 92168 | tf_op jit(solution)/shard_map/ppermute | solution.py:20
  107.9 0.6 copy-start.5
  112.5 25.5 %copy-start = (f32[2,3,8,8,128]{4,3,2,1,0:T(8,128)}, f32[2,3,8,8,128]{4,3,2,1,0:T(8,128)S(1)}, u32[]{:S(2)}) copy-start(f32[2,3,8,8,128]{4,3,2,1,0:T(8,128)S(1)} %get-tuple-element.182) | copy-start | bytes 589828
  112.5 6.3 %collective-permute-start.8 = (f32[2,3,1,8,128]{4,3,2,1,0:T(8,128)S(1)}, f32[2,3,1,8,128]{4,3,2,1,0:T(8,128)S(1)}, u32[]{:S(2)}, u32[]{:S(2)}) collective-permute-start(f32[2,3,1,8,128]{4,3,2,1,0:T(8,128)S(1)} %get-tuple-element.210), channel_id=1, source_target_pairs={{0,4},{1,5},{2,6},{3,7},{8,12},{9,13},{10,14},{11,15},{16,20},{17,... | collective-permute-start | bytes 73736 | tf_op jit(solution)/shard_map/ppermute | solution.py:18
  117.1 5.7 %collective-permute-start.9 = (f32[2,3,1,8,128]{4,3,2,1,0:T(8,128)S(1)}, f32[2,3,1,8,128]{4,3,2,1,0:T(8,128)S(1)}, u32[]{:S(2)}, u32[]{:S(2)}) collective-permute-start(f32[2,3,1,8,128]{4,3,2,1,0:T(8,128)S(1)} %get-tuple-element.211), channel_id=1, source_target_pairs={{4,0},{5,1},{6,2},{7,3},{12,8},{13,9},{14,10},{15,11},{20,16},{21,... | collective-permute-start | bytes 73736 | tf_op jit(solution)/shard_map/ppermute | solution.py:20
  122.8 6.5 %collective-permute-start.10 = (f32[2,3,10,1,128]{4,3,2,1,0:T(1,128)S(1)}, f32[2,3,10,1,128]{4,3,2,1,0:T(1,128)S(1)}, u32[]{:S(2)}, u32[]{:S(2)}) collective-permute-start(f32[2,3,10,1,128]{4,3,2,1,0:T(1,128)S(1)} %get-tuple-element.205), channel_id=1, source_target_pairs={{0,1},{1,2},{2,3},{4,5},{5,6},{6,7},{8,9},{9,10},{10,11},{12,13},{... | collective-permute-start | bytes 92168 | tf_op jit(solution)/shard_map/ppermute | solution.py:18
  127.4 5.8 %collective-permute-start.11 = (f32[2,3,10,1,128]{4,3,2,1,0:T(1,128)S(1)}, f32[2,3,10,1,128]{4,3,2,1,0:T(1,128)S(1)}, u32[]{:S(2)}, u32[]{:S(2)}) collective-permute-start(f32[2,3,10,1,128]{4,3,2,1,0:T(1,128)S(1)} %get-tuple-element.206), channel_id=1, source_target_pairs={{1,0},{2,1},{3,2},{5,4},{6,5},{7,6},{9,8},{10,9},{11,10},{13,12},{... | collective-permute-start | bytes 92168 | tf_op jit(solution)/shard_map/ppermute | solution.py:20
  129.3 3.9 %copy-start.6 = (f32[2,3,10,1,128]{4,3,2,1,0:T(1,128)}, f32[2,3,10,1,128]{4,3,2,1,0:T(1,128)S(1)}, u32[]{:S(2)}) copy-start(f32[2,3,10,1,128]{4,3,2,1,0:T(1,128)S(1)} %collective-permute-done.10) | copy-start | bytes 92164
  133.2 0.6 copy-start.7
Sparse Core Ops, SparseCore 0:
  140.7 29.9 all-reduce.10
where the time goes:
time: 181 us; the launch traced here: 179 us
  local copies, waits for them, and re-layouts  52.9 us (29%)
  starting transfers between devices  46.9 us (26%)
  waiting for transfers between devices  38 us (21%)
  other arithmetic  26.5 us (15%)
  between operations  14.5 us (8%)
    ppermute x8, starting transfers between devices, with_halo(): lax.ppermute(tail, axis, [(i, (i + 1) % count) for i in range(ends)])  36.4 us
    psum x1, waiting for transfers between devices, body(): whole = lax.psum((totals[0], totals[1]), 'ev')  30.1 us
    unnamed x28, local copies, waits for them, and re-layouts  22 us
    slice x1, local copies, waits for them, and re-layouts, body(): forces[:, step]  20.8 us
    scatter-add x1, other arithmetic, body(): forces = forces.at[:, :, :, cells].add(force_values)  13.3 us
    ppermute x8, starting transfers between devices, with_halo(): lax.ppermute(head, axis, [((i + 1) % count, i) for i in range(ends)])  10.5 us
    ppermute x8, waiting for transfers between devices, with_halo(): lax.ppermute(head, axis, [((i + 1) % count, i) for i in range(ends)])  7.86 us
    broadcast_in_dim x1, local copies, waits for them, and re-layouts, body(): jnp.zeros((events_here, 2, 3, width_x * width_y * depth), jnp.float32)  6 us
  transfers between devices with their start and end apart: 17, of which 3 were waited for; matrix products, arithmetic and copies ran while one was open for 39% of the time, Pallas kernels for 0%

commit v1 on v0

v1 whole, which is shorter than its diff:
```python
import functools

import jax
import jax.numpy as jnp
from jax import lax
from jax.experimental import pallas as pl
from jax.experimental.pallas import tpu as pltpu
from jax.sharding import PartitionSpec as P

STEP_FACTOR = 0.01
F32, BF16 = jnp.float32, jnp.bfloat16
SHEAR, LAME, BUOY, INV = range(4)
ROWS = 16
FULL = pl.BlockSpec(memory_space=pltpu.VMEM)
VMEM_LIMIT = 40 * 1024 * 1024
PACK_LIMIT = 60 * 1024 * 1024


def rounds_of(count):
    return "AB"[: max(0, min(2, count - 1))]


def swap(values, axis, name):
    count = lax.axis_size(axis)
    first = "AB".index(name)
    pairs = []
    for low in range(first, count - 1, 2):
        pairs += [(low, low + 1), (low + 1, low)]
    return lax.ppermute(values, axis, pairs)


def upward(axis, name):
    even = lax.rem(lax.axis_index(axis), 2) == 0
    return even if name == "A" else jnp.logical_not(even)


def split(values):
    high = values.astype(BF16)
    low = (values - high.astype(F32)).astype(BF16)
    return jnp.concatenate([high, low], axis=0)


def join(tile):
    tile = tile.astype(F32)
    return tile[:8] + tile[8:]


def force_field(cells, force_rows, width):
    depth = 128
    count = cells.shape[1]
    place = lax.broadcasted_iota(jnp.int32, (width, count), 0)
    mask = place == cells // depth
    level = lax.broadcasted_iota(jnp.int32, (depth, count), 0)
    hot = jnp.where(level == lax.rem(cells, depth), 1.0, 0.0).astype(BF16)
    left = jnp.concatenate([jnp.where(mask, row, 0.0) for row in force_rows], axis=0)
    total = None
    for _ in range(3):
        part = left.astype(BF16)
        left = left - part.astype(F32)
        term = lax.dot_general(part, hot, (((1,), (1,)), ((), ())), preferred_element_type=F32)
        total = term if total is None else total + term
    return total


def pack_kernel(events, x_rounds, y_rounds, now_in, prev_in, fwd_in, med_in, cells, force, *refs):
    fields = 3 * events
    outs, (now, prev, fwd, med, stored, arrived) = refs[:-6], refs[-6:]
    base = outs[0]
    messages = outs[1:]
    copies = [(now_in, now), (prev_in, prev), (med_in, med)]
    for e in range(events):
        copies.append((fwd_in.at[pl.ds(e * 12 + 3, 6)], fwd.at[pl.ds(e * 6, 6)]))
    copies = [
        pltpu.make_async_copy(source, target, arrived.at[k])
        for k, (source, target) in enumerate(copies)
    ]
    for copy in copies:
        copy.start()
    rows = [force[e, 0, c, 0] for e in range(events) for c in range(3)]
    pushed = force_field(cells[...], rows, 64)
    for copy in copies:
        copy.wait()
    for f in range(fields):
        base[f] = (
            2.0 * now[f] - prev[f] + STEP_FACTOR * med[BUOY] * pushed[f * 64 : (f + 1) * 64]
        )
        e, c = f // 3, f % 3
        for t in range(2):
            stored[f * 2 + t] = fwd[(e * 2 + t) * 3 + c].astype(F32).reshape(64, 128)

    def fill(message, pick):
        for f in range(fields):
            message[2 * f] = split(pick(now, f, 1))
            message[2 * f + 1] = split(pick(now, f, 2))
            message[2 * fields + f] = split(pick(base, f, 1))
            message[3 * fields + f] = jnp.concatenate(
                [pick(stored, 2 * f, 1), pick(stored, 2 * f + 1, 1)], axis=0
            ).astype(BF16)
        for k, m in enumerate((SHEAR, LAME, INV)):
            message[4 * fields + k] = jnp.concatenate(
                [pick(med, m, 1), pick(med, m, 2)], axis=0
            ).astype(BF16)
        edge = pick(med, BUOY, 1)
        message[4 * fields + 3] = jnp.concatenate([edge, edge], axis=0).astype(BF16)

    for k, name in enumerate(x_rounds):
        up = upward("gx", name)

        def pick_x(ref, index, ring, up=up):
            row = jnp.where(up, 8 - ring, ring - 1)
            return ref[index, pl.ds(pl.multiple_of(row * 8, 8), 8), :]

        fill(messages[k], pick_x)
    for k, name in enumerate(y_rounds):
        up = upward("gy", name)

        def pick_y(ref, index, ring, up=up):
            row = jnp.where(up, 8 - ring, ring - 1)
            return ref[index, pl.ds(row, 8, stride=8), :]

        fill(messages[len(x_rounds) + k], pick_y)


def corner_kernel(fields, x_rounds, y_rounds, *refs):
    sides = refs[: len(y_rounds)]
    outs = refs[len(y_rounds) : len(y_rounds) + len(x_rounds)]
    rows = refs[-1]
    for s, side in enumerate(sides):
        for k in range(3 * fields):
            rows[s, pl.ds(k * 8, 8), :] = join(side[k])
        for k in range(3):
            tile = side[4 * fields + k].astype(F32)
            rows[s, pl.ds((3 * fields + 2 * k) * 8, 16), :] = tile
        tile = side[4 * fields + 3].astype(F32)
        rows[s, pl.ds((3 * fields + 6) * 8, 16), :] = tile
        for k in range(3 * fields + 8, 32):
            rows[s, pl.ds(k * 8, 8), :] = jnp.zeros((8, 128), F32)
    for k, name in enumerate(x_rounds):
        up = upward("gx", name)
        for s in range(len(sides)):
            for ring in (1, 2):
                row = jnp.where(up, 8 - ring, ring - 1)
                outs[k][s, ring - 1] = rows[s, pl.ds(row, 32, stride=8), :]


def shift_z(values, step, lane, beyond=0.0):
    depth = values.shape[-1]
    moved = pltpu.roll(values, (-step) % depth, axis=values.ndim - 1)
    edge = depth - 1 if step > 0 else 0
    return jnp.where(lane == edge, beyond, moved)


def shift_y(values, step):
    return pltpu.roll(values, (-step) % ROWS, axis=0)


def row_of(ref, index, row):
    return ref[index, pl.ds(row * ROWS, ROWS), :]


def time_step(field, faces, first, last, emit):
    lane = lax.broadcasted_iota(jnp.int32, (ROWS, 128), 1)
    value = functools.cache(field)

    @functools.cache
    def ahead_y(c, row):
        return shift_y(value(c, row), 1)

    @functools.cache
    def ahead_z(c, row):
        return shift_z(value(c, row), 1, lane)

    @functools.cache
    def slope(d, row):
        if d == 0:
            return faces("cross", row) * (value(0, row + 1) - value(0, row - 1))
        if d == 1:
            return faces("cross", row) * (ahead_y(1, row) - shift_y(value(1, row), -1))
        return faces("cross_z", row) * (ahead_z(2, row) - shift_z(value(2, row), -1, lane))

    @functools.cache
    def flux_x(c, row):
        kind = "own_x" if c == 0 else "other_x"
        return faces(kind, row) * (value(c, row + 1) - value(c, row))

    for row in range(first, last + 1):
        results = []
        for c in range(3):
            total = flux_x(c, row) - flux_x(c, row - 1)
            flux = faces("own_y" if c == 1 else "other_y", row) * (ahead_y(c, row) - value(c, row))
            total = total + (flux - shift_y(flux, -1))
            flux = faces("own_z" if c == 2 else "other_z", row) * (ahead_z(c, row) - value(c, row))
            below = faces("own_low" if c == 2 else "other_low", row) * value(c, row)
            upright = flux - shift_z(flux, -1, lane, below)
            if c == 0:
                total = total + (
                    (slope(1, row + 1) + slope(2, row + 1))
                    - (slope(1, row - 1) + slope(2, row - 1))
                )
            elif c == 1:
                mixed = slope(0, row) + slope(2, row)
                total = total + (shift_y(mixed, 1) - shift_y(mixed, -1))
            else:
                mixed = slope(0, row) + slope(1, row)
                upright = upright + (shift_z(mixed, 1, lane) - shift_z(mixed, -1, lane))
            results.append(total + faces("inverse", row) * upright)
        emit(row, results)


def main_kernel(events, x_rounds, y_rounds, shares, *refs):
    fields = 3 * events
    now, base, fwd, med, cells, force = refs[:6]
    at = 6
    x_messages = refs[at : at + len(x_rounds)]
    at += len(x_rounds)
    y_messages = refs[at : at + len(y_rounds)]
    at += len(y_rounds)
    corners = refs[at : at + len(x_rounds)] if y_rounds else ()
    at += len(corners)
    mid, after, own_share = refs[at : at + 3]
    at += 3
    sent = refs[at : at + shares - 1]
    at += shares - 1
    here, then, start, stored, medium, coef, slabs = refs[at:]

    for f in range(fields):
        e, c = f // 3, f % 3
        for x in range(8):
            spot = pl.ds((x + 2) * ROWS, 8)
            here[f, spot, :] = now[f, pl.ds(x * 8, 8), :]
            start[f, spot, :] = base[f, pl.ds(x * 8, 8), :]
            for t in range(2):
                stored[2 * f + t, spot, :] = fwd[(e * 4 + t + 1) * 3 + c, x].astype(F32)
    for m in range(4):
        for x in range(8):
            medium[m, pl.ds((x + 2) * ROWS, 8), :] = med[m, pl.ds(x * 8, 8), :]

    def place(tile, put):
        for f in range(fields):
            put(here, f, 1, join(tile(2 * f)))
            put(here, f, 2, join(tile(2 * f + 1)))
            put(start, f, 1, join(tile(2 * fields + f)))
            both = tile(3 * fields + f).astype(F32)
            put(stored, 2 * f, 1, both[:8])
            put(stored, 2 * f + 1, 1, both[8:])
        for k, m in enumerate((SHEAR, LAME, INV)):
            both = tile(4 * fields + k).astype(F32)
            put(medium, m, 1, both[:8])
            put(medium, m, 2, both[8:])
        put(medium, BUOY, 1, tile(4 * fields + 3).astype(F32)[:8])

    def nothing(_):
        return jnp.zeros((16, 128), BF16)

    def x_row(up, ring):
        return jnp.where(up, 9 + ring, 2 - ring)

    def y_place(up, ring):
        return jnp.where(up, 7 + ring, ROWS - ring)

    for k, name in enumerate("AB"):
        up = upward("gx", name)

        def put_x(ref, index, ring, values, up=up):
            row = pl.multiple_of(x_row(up, ring) * ROWS, ROWS)
            ref[index, pl.ds(row, 8), :] = values

        if k < len(x_rounds):
            place(lambda i, k=k: x_messages[k][i], put_x)
        else:
            place(nothing, put_x)
    for k, name in enumerate("AB"):
        up = upward("gy", name)

        def put_y(ref, index, ring, values, up=up):
            ref[index, pl.ds(2 * ROWS + y_place(up, ring), 8, stride=ROWS), :] = values

        if k < len(y_rounds):
            place(lambda i, k=k: y_messages[k][i], put_y)
        else:
            place(nothing, put_y)
    for kx, name_x in enumerate("AB"):
        for ky, name_y in enumerate("AB"):
            up_x, up_y = upward("gx", name_x), upward("gy", name_y)
            for ring_x in (1, 2):
                for ring_y in (1, 2):
                    spot = x_row(up_x, ring_x) * ROWS + y_place(up_y, ring_y)

                    def move(ref, index, k):
                        if kx < len(x_rounds) and ky < len(y_rounds):
                            values = corners[kx][ky, ring_x - 1, pl.ds(k, 1), :]
                        else:
                            values = jnp.zeros((1, 128), F32)
                        ref[index, pl.ds(spot, 1), :] = values

                    for f in range(fields):
                        move(here, f, 2 * f + ring_y - 1)
                        if ring_x == 1 and ring_y == 1:
                            move(start, f, 2 * fields + f)
                    for k, m in enumerate((SHEAR, LAME, INV)):
                        move(medium, m, 3 * fields + 2 * k + ring_y - 1)
                    if ring_x == 1 and ring_y == 1:
                        move(medium, BUOY, 3 * fields + 6)

    names = (
        ("own_x", "other_x", "own_y", "other_y", "own_z", "other_z")
        + ("own_low", "other_low", "cross", "cross_z")
    )
    lane = lax.broadcasted_iota(jnp.int32, (ROWS, 128), 1)

    def wide(row):
        return row_of(medium, LAME, row) + 2.0 * row_of(medium, SHEAR, row)

    for row in range(12):
        shear, lame, inverse = (row_of(medium, m, row) for m in (SHEAR, LAME, INV))
        both = lame + 2.0 * shear
        values = {}
        if row < 11:
            values["own_x"] = 0.5 * (both + wide(row + 1))
            values["other_x"] = 0.5 * (shear + row_of(medium, SHEAR, row + 1))
        values["own_y"] = 0.5 * (both + shift_y(both, 1))
        values["other_y"] = 0.5 * (shear + shift_y(shear, 1))
        spacing = 0.25 * (inverse + shift_z(inverse, 1, lane))
        values["own_z"] = spacing * (both + shift_z(both, 1, lane))
        values["other_z"] = spacing * (shear + shift_z(shear, 1, lane))
        values["own_low"] = 0.25 * inverse * both
        values["other_low"] = 0.25 * inverse * shear
        values["cross"] = 0.25 * (lame + shear)
        values["cross_z"] = values["cross"] * inverse
        for name, value in values.items():
            coef[names.index(name), pl.ds(row * ROWS, ROWS), :] = value

    def faces(name, row):
        if name == "inverse":
            return row_of(medium, INV, row)
        return row_of(coef, names.index(name), row)

    for e in range(events):

        def emit(row, results, e=e):
            scale = STEP_FACTOR * row_of(medium, BUOY, row)
            for c in range(3):
                f = 3 * e + c
                value = row_of(start, f, row) + scale * results[c]
                then[f, pl.ds(row * ROWS, ROWS), :] = value
                if 2 <= row <= 9:
                    mid[f, pl.ds((row - 2) * 8, 8), :] = value[:8]

        time_step(lambda c, row, e=e: row_of(here, 3 * e + c, row), faces, 1, 10, emit)

    lane8 = lane[:8]
    grads = [[], []]
    for x in range(8):
        row = x + 2
        lateral = upright = density = None
        for t, ref in ((0, here), (1, then)):
            for f in range(fields):
                e, c = f // 3, f % 3

                def slopes(source, index):
                    mine = row_of(source, index, row)
                    along_x = row_of(source, index, row + 1) - row_of(source, index, row - 1)
                    along_y = shift_y(mine, 1) - shift_y(mine, -1)
                    own = mine[:8]
                    along_z = shift_z(own, 1, lane8) - shift_z(own, -1, lane8)
                    return own, along_x[:8], along_y[:8], along_z

                own, ax, ay, az = slopes(ref, f)
                middle, ux, uy, uz = slopes(stored, 2 * f + t)
                newer = fwd[(e * 4 + t) * 3 + c, x].astype(F32)
                older = fwd[(e * 4 + t + 2) * 3 + c, x].astype(F32)
                terms = (ax * ux + ay * uy, az * uz, own * (newer - 2.0 * middle + older))
                if lateral is None:
                    lateral, upright, density = terms
                else:
                    lateral, upright, density = (
                        lateral + terms[0],
                        upright + terms[1],
                        density + terms[2],
                    )
        inverse = med[INV, pl.ds(x * 8, 8), :]
        grads[0].append(-0.25 * (lateral + inverse * inverse * upright))
        grads[1].append(-density)
    grads = grads[0] + grads[1]
    piece = 128 // shares
    quarter = lane8 // piece
    per = len(grads) // shares
    for j in range(shares):
        for r in range(per):
            tile = None
            for g in range(shares):
                source = grads[r * shares + g]
                moved = pltpu.roll(source, ((g - j) * piece) % 128, axis=1) if g != j else source
                tile = moved if tile is None else jnp.where(quarter == g, moved, tile)
            slabs[j, pl.ds(r * 8, 8), :] = tile
    me = lax.axis_index("ev")
    own_share[...] = slabs[me]
    for m in range(1, shares):
        sent[m - 1][...] = slabs[me ^ m]

    rows = [force[e, 1, c, 0] for e in range(events) for c in range(3)]
    pushed = force_field(cells[...], rows, 64)
    for e in range(events):

        def emit(row, results, e=e):
            x = row - 2
            scale = STEP_FACTOR * med[BUOY, pl.ds(x * 8, 8), :]
            for c in range(3):
                f = 3 * e + c
                current = then[f, pl.ds(row * ROWS, 8), :]
                previous = now[f, pl.ds(x * 8, 8), :]
                extra = pushed[f * 64 + x * 8 : f * 64 + x * 8 + 8]
                after[f, pl.ds(x * 8, 8), :] = (
                    2.0 * current - previous + scale * (results[c][:8] + extra)
                )

        time_step(lambda c, row, e=e: row_of(then, 3 * e + c, row), faces, 2, 9, emit)


def finish_kernel(shares, scale, *refs):
    pieces, (shear, density) = refs[:shares], refs[shares:]
    total = pieces[0][...]
    for piece in pieces[1:]:
        total = total + piece[...]
    width = 128 // shares
    for v in range(16):
        g, r = v % shares, v // shares
        tile = total[r * 8 : (r + 1) * 8]
        if g:
            tile = pltpu.roll(tile, (-g * width) % 128, axis=1)
        out = shear if v < 8 else density
        out[pl.ds((v % 8) * 8, 8), :] = tile[:, :width] * scale


def call(kernel, outs, ins, scratch=(), name=None, limit=VMEM_LIMIT):
    return pl.pallas_call(
        kernel,
        out_shape=[jax.ShapeDtypeStruct(s, d) for s, d in outs],
        in_specs=[pl.BlockSpec(memory_space=m) for m in ins],
        scratch_shapes=[s if not isinstance(s, tuple) else pltpu.VMEM(*s) for s in scratch],
        compiler_params=pltpu.CompilerParams(vmem_limit_bytes=limit),
        name=name,
    )


def body(adjoint_now, adjoint_prev, forward, medium, drm_cells, drm_force):
    events, _, width_x, width_y, depth = adjoint_now.shape
    fields = 3 * events
    tile = width_x * width_y
    shares = lax.axis_size("ev")
    x_rounds, y_rounds = rounds_of(lax.axis_size("gx")), rounds_of(lax.axis_size("gy"))
    now = adjoint_now.reshape(fields, tile, depth)
    prev = adjoint_prev.reshape(fields, tile, depth)
    fwd = forward.reshape(events * 12, width_x, width_y, depth)
    med = medium.reshape(4, tile, depth)
    cells = drm_cells.reshape(1, -1)
    force = drm_force

    message = ((4 * fields + 4, 16, depth), BF16)
    base, *messages = call(
        functools.partial(pack_kernel, events, x_rounds, y_rounds),
        [((fields, tile, depth), F32)] + [message] * (len(x_rounds) + len(y_rounds)),
        [pltpu.HBM] * 4 + [pltpu.VMEM] * 2,
        [
            ((fields, tile, depth), F32),
            ((fields, tile, depth), F32),
            ((2 * fields, width_x, width_y, depth), BF16),
            ((4, tile, depth), F32),
            ((2 * fields, tile, depth), F32),
            pltpu.SemaphoreType.DMA((3 + events,)),
        ],
        "pack",
        PACK_LIMIT,
    )(now, prev, fwd, med, cells, force)
    y_messages = [swap(m, "gy", r) for m, r in zip(messages[len(x_rounds) :], y_rounds)]
    x_messages = [swap(m, "gx", r) for m, r in zip(messages, x_rounds)]
    corners = []
    if x_rounds and y_rounds:
        corners = call(
            functools.partial(corner_kernel, fields, x_rounds, y_rounds),
            [((len(y_rounds), 2, 32, depth), F32)] * len(x_rounds),
            [pltpu.VMEM] * len(y_rounds),
            [((len(y_rounds), 32 * 8, depth), F32)],
            "corners",
        )(*y_messages)
        corners = [swap(m, "gx", r) for m, r in zip(corners, x_rounds)]

    slab = ((16 // shares * 8, depth), F32)
    wide = ((fields, 12 * ROWS, depth), F32)
    mid, after, own_share, *sent = call(
        functools.partial(main_kernel, events, x_rounds, y_rounds, shares),
        [((fields, tile, depth), F32)] * 2 + [slab] * shares,
        [pltpu.VMEM] * (6 + len(x_messages) + len(y_messages) + len(corners)),
        [
            wide,
            wide,
            wide,
            ((2 * fields, 12 * ROWS, depth), F32),
            ((4, 12 * ROWS, depth), F32),
            ((10, 12 * ROWS, depth), F32),
            ((shares,) + slab[0], F32),
        ],
        "steps",
    )(now, base, fwd, med, cells, force, *x_messages, *y_messages, *corners)
    pieces = [own_share]
    for m in reversed(range(1, shares)):
        pairs = [(i, i ^ m) for i in range(shares)]
        pieces.append(lax.ppermute(sent[m - 1], "ev", pairs))
    shear, density = call(
        functools.partial(finish_kernel, shares, 1.0 / (events * shares)),
        [((tile, depth // shares), F32)] * 2,
        [pltpu.VMEM] * shares,
        name="finish",
    )(*pieces)
    shape = adjoint_now.shape
    grad = (width_x, width_y, depth // shares)
    return mid.reshape(shape), after.reshape(shape), shear.reshape(grad), density.reshape(grad)


def solution(mesh):
    in_specs = (
        P("ev", None, "gx", "gy", None),
        P("ev", None, "gx", "gy", None),
        P("ev", None, None, "gx", "gy", None),
        P(None, "gx", "gy", None),
        P("gx", "gy", None),
        P("ev", None, None, "gx", "gy", None),
    )
    out_specs = (
        P("ev", None, "gx", "gy", None),
        P("ev", None, "gx", "gy", None),
        P("gx", "gy", "ev"),
        P("gx", "gy", "ev"),
    )
    return jax.shard_map(body, mesh=mesh, in_specs=in_specs, out_specs=out_specs, check_vma=False)
```

time: 181 us -> 27.8 us (0.15)
  the two profiles are of different devices: /device:TPU:0 before, /device:TPU:9 now
where the time goes in v1:
time: 27.8 us; the launch traced here: 27.3 us
  starting transfers between devices  11 us (40%)
  Pallas kernels  8.73 us (31%)
  waiting for transfers between devices  5.81 us (21%)
  local copies, waits for them, and re-layouts  0.95 us (3%)
  between operations  0.73 us (3%)
    ppermute x4, starting transfers between devices, swap(): return lax.ppermute(values, axis, pairs)  7.16 us
    pallas_call x1, Pallas kernels, body(): call(functools.partial(main_kernel, events, x_rounds, y_rounds, shares),...  5.17 us
    ppermute x3, starting transfers between devices, body(): pieces.append(lax.ppermute(sent[m - 1], 'ev', pairs))  3.89 us
    ppermute x4, waiting for transfers between devices, swap(): return lax.ppermute(values, axis, pairs)  3.65 us
    pallas_call x1, Pallas kernels, body(): call(functools.partial(pack_kernel, events, x_rounds, y_rounds), [((field...  2.82 us
    ppermute x3, waiting for transfers between devices, body(): pieces.append(lax.ppermute(sent[m - 1], 'ev', pairs))  2.16 us
    unnamed x12, local copies, waits for them, and re-layouts  0.95 us
    pallas_call x1, Pallas kernels, body(): call(functools.partial(finish_kernel, shares, 1.0 / (events * shares)), [...  0.7 us
  transfers between devices with their start and end apart: 7, of which 4 were waited for; matrix products, arithmetic and copies ran while one was open for 0% of the time, Pallas kernels for 0%

profile of v1, /device:TPU:9, one launch (start us, length us, event | category | flops | bytes accessed | tf_op | source)
XLA Modules:
  0.0 27.3 jit_solution(15699949284319670694)
XLA Ops:
  0.6 0.0 copy-start
  0.6 0.0 copy-start.2
  0.7 2.8 %pack.1 = (f32[6,64,128]{2,1,0:T(8,128)}, bf16[28,16,128]{2,1,0:T(8,128)(2,1)}, bf16[28,16,128]{2,1,0:T(8,128)(2,1)}, bf16[28,16,128]{2,1,0:T(8,128)(2,1)}) custom-call(f32[6,64,128]{2,1,0:T(8,128)} %bitcast.11, f32[6,64,128]{2,1,0:T(8,128)} %bitcast.17, bf16[24,8,8,128]{3,2,1,0:T(8,128)(2,1)} %bitcast.9, f32[4,64,128]{2,1,0:T(8,128)} %bitcast.13, ...), custom_call_target="tpu_custom_call" | custom-call | tf_op jit(solution)/shard_map/pack/pallas_call | solution.py:460
  3.5 0.0 copy-start.1
  3.5 0.1 collective-permute-start.1
  3.6 4.5 %collective-permute-start.2 = (bf16[28,16,128]{2,1,0:T(8,128)(2,1)}, bf16[28,16,128]{2,1,0:T(8,128)(2,1)S(1)}, u32[]{:S(2)}, u32[]{:S(2)}) collective-permute-start(bf16[28,16,128]{2,1,0:T(8,128)(2,1)} %get-tuple-element.19), channel_id=1, source_target_pairs={{1,2},{2,1},{5,6},{6,5},{9,10},{10,9},{13,14},{14,13},{17,18},{18,... | collective-permute-start | bytes 344072 | tf_op jit(solution)/shard_map/ppermute | solution.py:29
  8.1 1.3 %collective-permute-start = (bf16[28,16,128]{2,1,0:T(8,128)(2,1)}, bf16[28,16,128]{2,1,0:T(8,128)(2,1)S(1)}, u32[]{:S(2)}, u32[]{:S(2)}) collective-permute-start(bf16[28,16,128]{2,1,0:T(8,128)(2,1)} %get-tuple-element.17), channel_id=1, source_target_pairs={{0,4},{4,0},{1,5},{5,1},{2,6},{6,2},{3,7},{7,3},{8,12},{12,8},{9,1... | collective-permute-start | bytes 344072 | tf_op jit(solution)/shard_map/ppermute | solution.py:29
  9.4 0.0 collective-permute-done.1.refs_0_.refs_7_
  9.4 1.4 %collective-permute-done.2.refs_1_.refs_8_ = bf16[28,16,128]{2,1,0:T(8,128)(2,1)S(1)} collective-permute-done((bf16[28,16,128]{2,1,0:T(8,128)(2,1)}, bf16[28,16,128]{2,1,0:T(8,128)(2,1)S(1)}, u32[]{:S(2)}, u32[]{:S(2)}) %collective-permute-start.2) | collective-permute-done | bytes 114720 | tf_op jit(solution)/shard_map/ppermute | solution.py:29
  10.8 0.0 copy-start.4
  10.9 0.0 copy-start.5
  10.9 1.3 %collective-permute-start.3 = (f32[2,2,32,128]{3,2,1,0:T(8,128)S(1)}, f32[2,2,32,128]{3,2,1,0:T(8,128)S(1)}, u32[]{:S(2)}, u32[]{:S(2)}) collective-permute-start(f32[2,2,32,128]{3,2,1,0:T(8,128)S(1)} %corners.1), channel_id=1, source_target_pairs={{0,4},{4,0},{1,5},{5,1},{2,6},{6,2},{3,7},{7,3},{8,12},{12,8},{9,1... | collective-permute-start | bytes 196616 | tf_op jit(solution)/shard_map/ppermute | solution.py:29
  12.2 0.0 collective-permute-done.refs_6_
  12.2 2.2 %collective-permute-done.3.refs_9_ = f32[2,2,32,128]{3,2,1,0:T(8,128)S(1)} collective-permute-done((f32[2,2,32,128]{3,2,1,0:T(8,128)S(1)}, f32[2,2,32,128]{3,2,1,0:T(8,128)S(1)}, u32[]{:S(2)}, u32[]{:S(2)}) %collective-permute-start.3) | collective-permute-done | bytes 65568 | tf_op jit(solution)/shard_map/ppermute | solution.py:29
  14.4 0.0 copy-done
  14.4 0.0 copy-done.2
  14.4 0.0 copy-done.1
  14.4 0.0 copy-done.4
  14.4 0.0 copy-done.5
  14.4 0.0 copy-start.3
  14.4 0.9 %copy-done.3 = f32[6,64,128]{2,1,0:T(8,128)S(1)} copy-done((f32[6,64,128]{2,1,0:T(8,128)S(1)}, f32[6,64,128]{2,1,0:T(8,128)}, u32[]{:S(2)}) %copy-start.3) | copy-done | bytes 196632
  15.3 5.2 %steps.1 = (f32[6,64,128]{2,1,0:T(8,128)}, f32[6,64,128]{2,1,0:T(8,128)}, f32[32,128]{1,0:T(8,128)S(1)}, f32[32,128]{1,0:T(8,128)S(1)}, f32[32,128]{1,0:T(8,128)S(1)}, /*index=5*/f32[32,128]{1,0:T(8,128)S(1)}) custom-call(f32[6,64,128]{2,1,0:T(8,128)S(1)} %bitcast.12, f32[6,64,128]{2,1,0:T(8,128)S(1)} %copy-done.3, bf16[24,8,8,128]{3,2,1,0:T(8,128)(2,1)S(1)} %bitcast.10, ...), custom_call_target="tpu_custom_call" | custom-call | tf_op jit(solution)/shard_map/steps/pallas_call | solution.py:490
  20.5 3.5 %collective-permute-start.4 = (f32[32,128]{1,0:T(8,128)S(1)}, f32[32,128]{1,0:T(8,128)S(1)}, u32[]{:S(2)}, u32[]{:S(2)}) collective-permute-start(f32[32,128]{1,0:T(8,128)S(1)} %get-tuple-element.23), channel_id=1, source_target_pairs={{0,24},{8,16},{16,8},{24,0},{1,25},{9,17},{17,9},{25,1},{2,26},{10... | collective-permute-start | bytes 49160 | tf_op jit(solution)/shard_map/ppermute | solution.py:508
  24.0 0.3 collective-permute-start.5
  24.2 0.2 collective-permute-start.6
  24.4 1.4 %collective-permute-done.4.refs_1_ = f32[32,128]{1,0:T(8,128)S(1)} collective-permute-done((f32[32,128]{1,0:T(8,128)S(1)}, f32[32,128]{1,0:T(8,128)S(1)}, u32[]{:S(2)}, u32[]{:S(2)}) %collective-permute-start.4) | collective-permute-done | bytes 16416 | tf_op jit(solution)/shard_map/ppermute | solution.py:508
  25.8 0.8 %collective-permute-done.5.refs_2_ = f32[32,128]{1,0:T(8,128)S(1)} collective-permute-done((f32[32,128]{1,0:T(8,128)S(1)}, f32[32,128]{1,0:T(8,128)S(1)}, u32[]{:S(2)}, u32[]{:S(2)}) %collective-permute-start.5) | collective-permute-done | bytes 16416 | tf_op jit(solution)/shard_map/ppermute | solution.py:508
  26.6 0.0 collective-permute-done.6.refs_3_
  26.6 0.7 %finish.1 = (f32[64,32]{1,0:T(8,128)}, f32[64,32]{1,0:T(8,128)}) custom-call(f32[32,128]{1,0:T(8,128)S(1)} %get-tuple-element.22.refs_0_, f32[32,128]{1,0:T(8,128)S(1)} %collective-permute-done.4.refs_1_, f32[32,128]{1,0:T(8,128)S(1)} %collective-permute-done.5.refs_2_, f32[32,128]{1,0:T(8,128)S(1)} %collective-permute-done.6.refs_3_), custom_call_target="tpu_custom_call" | custom-call | tf_op jit(solution)/shard_map/finish/pallas_call | solution.py:509
  (1 shorter events, 0.0 us)
Async XLA Ops:
  0.6 13.7 %copy-start = (bf16[2,4,3,8,8,128]{5,4,3,2,1,0:T(8,128)(2,1)S(1)}, bf16[2,4,3,8,8,128]{5,4,3,2,1,0:T(8,128)(2,1)}, u32[]{:S(2)}) copy-start(bf16[2,4,3,8,8,128]{5,4,3,2,1,0:T(8,128)(2,1)} %param.8) | copy-start | bytes 1179652
  0.6 13.7 %copy-start.2 = (f32[4,8,8,128]{3,2,1,0:T(8,128)S(1)}, f32[4,8,8,128]{3,2,1,0:T(8,128)}, u32[]{:S(2)}) copy-start(f32[4,8,8,128]{3,2,1,0:T(8,128)} %param.9) | copy-start | bytes 393220
  3.5 10.9 %copy-start.1 = (f32[2,3,8,8,128]{4,3,2,1,0:T(8,128)S(1)}, f32[2,3,8,8,128]{4,3,2,1,0:T(8,128)}, u32[]{:S(2)}) copy-start(f32[2,3,8,8,128]{4,3,2,1,0:T(8,128)} %param.6) | copy-start | bytes 589828
  3.5 5.9 %collective-permute-start.1 = (bf16[28,16,128]{2,1,0:T(8,128)(2,1)}, bf16[28,16,128]{2,1,0:T(8,128)(2,1)S(1)}, u32[]{:S(2)}, u32[]{:S(2)}) collective-permute-start(bf16[28,16,128]{2,1,0:T(8,128)(2,1)} %get-tuple-element.18), channel_id=1, source_target_pairs={{0,1},{1,0},{2,3},{3,2},{4,5},{5,4},{6,7},{7,6},{8,9},{9,8},{10,11... | collective-permute-start | bytes 344072 | tf_op jit(solution)/shard_map/ppermute | solution.py:29
  3.6 7.2 %collective-permute-start.2 = (bf16[28,16,128]{2,1,0:T(8,128)(2,1)}, bf16[28,16,128]{2,1,0:T(8,128)(2,1)S(1)}, u32[]{:S(2)}, u32[]{:S(2)}) collective-permute-start(bf16[28,16,128]{2,1,0:T(8,128)(2,1)} %get-tuple-element.19), channel_id=1, source_target_pairs={{1,2},{2,1},{5,6},{6,5},{9,10},{10,9},{13,14},{14,13},{17,18},{18,... | collective-permute-start | bytes 344072 | tf_op jit(solution)/shard_map/ppermute | solution.py:29
  8.1 4.1 %collective-permute-start = (bf16[28,16,128]{2,1,0:T(8,128)(2,1)}, bf16[28,16,128]{2,1,0:T(8,128)(2,1)S(1)}, u32[]{:S(2)}, u32[]{:S(2)}) collective-permute-start(bf16[28,16,128]{2,1,0:T(8,128)(2,1)} %get-tuple-element.17), channel_id=1, source_target_pairs={{0,4},{4,0},{1,5},{5,1},{2,6},{6,2},{3,7},{7,3},{8,12},{12,8},{9,1... | collective-permute-start | bytes 344072 | tf_op jit(solution)/shard_map/ppermute | solution.py:29
  10.8 3.6 %copy-start.4 = (f32[2,2,3,1,1,128]{5,4,3,2,1,0:T(1,128)S(1)}, f32[2,2,3,1,1,128]{5,4,3,2,1,0:T(1,128)}, u32[]{:S(2)}) copy-start(f32[2,2,3,1,1,128]{5,4,3,2,1,0:T(1,128)} %refs_5_.1) | copy-start | bytes 18436
  10.9 3.5 %copy-start.5 = (s32[1,1,128]{2,1,0:T(1,128)S(1)}, s32[1,1,128]{2,1,0:T(1,128)}, u32[]{:S(2)}) copy-start(s32[1,1,128]{2,1,0:T(1,128)} %param.10) | copy-start | bytes 1540
  10.9 3.5 %collective-permute-start.3 = (f32[2,2,32,128]{3,2,1,0:T(8,128)S(1)}, f32[2,2,32,128]{3,2,1,0:T(8,128)S(1)}, u32[]{:S(2)}, u32[]{:S(2)}) collective-permute-start(f32[2,2,32,128]{3,2,1,0:T(8,128)S(1)} %corners.1), channel_id=1, source_target_pairs={{0,4},{4,0},{1,5},{5,1},{2,6},{6,2},{3,7},{7,3},{8,12},{12,8},{9,1... | collective-permute-start | bytes 196616 | tf_op jit(solution)/shard_map/ppermute | solution.py:29
  14.4 0.9 %copy-start.3 = (f32[6,64,128]{2,1,0:T(8,128)S(1)}, f32[6,64,128]{2,1,0:T(8,128)}, u32[]{:S(2)}) copy-start(f32[6,64,128]{2,1,0:T(8,128)} %get-tuple-element.16.refs_1_) | copy-start | bytes 589828
  20.5 5.3 %collective-permute-start.4 = (f32[32,128]{1,0:T(8,128)S(1)}, f32[32,128]{1,0:T(8,128)S(1)}, u32[]{:S(2)}, u32[]{:S(2)}) collective-permute-start(f32[32,128]{1,0:T(8,128)S(1)} %get-tuple-element.23), channel_id=1, source_target_pairs={{0,24},{8,16},{16,8},{24,0},{1,25},{9,17},{17,9},{25,1},{2,26},{10... | collective-permute-start | bytes 49160 | tf_op jit(solution)/shard_map/ppermute | solution.py:508
  24.0 2.6 %collective-permute-start.5 = (f32[32,128]{1,0:T(8,128)S(1)}, f32[32,128]{1,0:T(8,128)S(1)}, u32[]{:S(2)}, u32[]{:S(2)}) collective-permute-start(f32[32,128]{1,0:T(8,128)S(1)} %get-tuple-element.24), channel_id=1, source_target_pairs={{0,16},{8,24},{16,0},{24,8},{1,17},{9,25},{17,1},{25,9},{2,18},{10... | collective-permute-start | bytes 49160 | tf_op jit(solution)/shard_map/ppermute | solution.py:508
  24.2 2.3 %collective-permute-start.6 = (f32[32,128]{1,0:T(8,128)S(1)}, f32[32,128]{1,0:T(8,128)S(1)}, u32[]{:S(2)}, u32[]{:S(2)}) collective-permute-start(f32[32,128]{1,0:T(8,128)S(1)} %get-tuple-element.25), channel_id=1, source_target_pairs={{0,8},{8,0},{16,24},{24,16},{1,9},{9,1},{17,25},{25,17},{2,10},{10... | collective-permute-start | bytes 49160 | tf_op jit(solution)/shard_map/ppermute | solution.py:508

commit v2 on v1

v2 whole, which is shorter than its diff:
```python
import functools

import jax
import jax.numpy as jnp
from jax import lax
from jax.experimental import pallas as pl
from jax.experimental.pallas import tpu as pltpu
from jax.sharding import PartitionSpec as P

STEP_FACTOR = 0.01
F32, BF16 = jnp.float32, jnp.bfloat16
SHEAR, LAME, BUOY, INV = range(4)
ROWS = 16
FULL = pl.BlockSpec(memory_space=pltpu.VMEM)
VMEM_LIMIT = 40 * 1024 * 1024
PACK_LIMIT = 60 * 1024 * 1024


def rounds_of(count):
    return "AB"[: max(0, min(2, count - 1))]


def swap(values, axis, name):
    count = lax.axis_size(axis)
    first = "AB".index(name)
    pairs = []
    for low in range(first, count - 1, 2):
        pairs += [(low, low + 1), (low + 1, low)]
    return lax.ppermute(values, axis, pairs)


def upward(axis, name):
    even = lax.rem(lax.axis_index(axis), 2) == 0
    return even if name == "A" else jnp.logical_not(even)


def split(values):
    high = values.astype(BF16)
    low = (values - high.astype(F32)).astype(BF16)
    return jnp.concatenate([high, low], axis=0)


def join(tile):
    tile = tile.astype(F32)
    return tile[:8] + tile[8:]


def force_field(cells, force_rows, width):
    depth = 128
    count = cells.shape[1]
    place = lax.broadcasted_iota(jnp.int32, (width, count), 0)
    mask = place == cells // depth
    level = lax.broadcasted_iota(jnp.int32, (depth, count), 0)
    hot = jnp.where(level == lax.rem(cells, depth), 1.0, 0.0).astype(BF16)
    left = jnp.concatenate([jnp.where(mask, row, 0.0) for row in force_rows], axis=0)
    total = None
    for _ in range(3):
        part = left.astype(BF16)
        left = left - part.astype(F32)
        term = lax.dot_general(part, hot, (((1,), (1,)), ((), ())), preferred_element_type=F32)
        total = term if total is None else total + term
    return total


def pack_kernel(events, x_rounds, y_rounds, *refs):
    fields = 3 * events
    count = 6
    sources = refs[:count]
    messages = refs[count : count + len(x_rounds) + len(y_rounds)]
    now, prev, fwd, med, cells, force, base, stored, arrived = refs[count + len(messages) :]
    now_in, prev_in, fwd_in, med_in, cells_in, force_in = sources
    pairs = [(cells_in, cells), (force_in, force), (now_in, now), (prev_in, prev), (med_in, med)]
    for e in range(events):
        pairs.append((fwd_in.at[pl.ds(e * 12 + 3, 6)], fwd.at[pl.ds(e * 6, 6)]))
    copies = [
        pltpu.make_async_copy(source, target, arrived.at[k])
        for k, (source, target) in enumerate(pairs)
    ]
    for copy in copies:
        copy.start()
    for copy in copies[:2]:
        copy.wait()
    rows = [force[e, 0, c, 0] for e in range(events) for c in range(3)]
    pushed = force_field(cells[0], rows, 64)
    for copy in copies[2:]:
        copy.wait()
    for f in range(fields):
        base[f] = (
            2.0 * now[f] - prev[f] + STEP_FACTOR * med[BUOY] * pushed[f * 64 : (f + 1) * 64]
        )
        e, c = f // 3, f % 3
        for t in range(2):
            stored[f * 2 + t] = fwd[(e * 2 + t) * 3 + c].astype(F32).reshape(64, 128)

    def fill(message, pick):
        for f in range(fields):
            message[2 * f] = split(pick(now, f, 1))
            message[2 * f + 1] = split(pick(now, f, 2))
            message[2 * fields + f] = split(pick(base, f, 1))
            message[3 * fields + f] = jnp.concatenate(
                [pick(stored, 2 * f, 1), pick(stored, 2 * f + 1, 1)], axis=0
            ).astype(BF16)
        for k, m in enumerate((SHEAR, LAME, INV)):
            message[4 * fields + k] = jnp.concatenate(
                [pick(med, m, 1), pick(med, m, 2)], axis=0
            ).astype(BF16)
        edge = pick(med, BUOY, 1)
        message[4 * fields + 3] = jnp.concatenate([edge, edge], axis=0).astype(BF16)

    for k, name in enumerate(x_rounds):
        up = upward("gx", name)

        def pick_x(ref, index, ring, up=up):
            row = jnp.where(up, 8 - ring, ring - 1)
            return ref[index, pl.ds(pl.multiple_of(row * 8, 8), 8), :]

        fill(messages[k], pick_x)
    for k, name in enumerate(y_rounds):
        up = upward("gy", name)

        def pick_y(ref, index, ring, up=up):
            row = jnp.where(up, 8 - ring, ring - 1)
            return ref[index, pl.ds(row, 8, stride=8), :]

        fill(messages[len(x_rounds) + k], pick_y)


def corner_kernel(fields, x_rounds, y_rounds, *refs):
    sides = refs[: len(y_rounds)]
    outs = refs[len(y_rounds) : len(y_rounds) + len(x_rounds)]
    rows = refs[-1]
    for s, side in enumerate(sides):
        for k in range(3 * fields):
            rows[s, pl.ds(k * 8, 8), :] = join(side[k])
        for k in range(3):
            tile = side[4 * fields + k].astype(F32)
            rows[s, pl.ds((3 * fields + 2 * k) * 8, 16), :] = tile
        tile = side[4 * fields + 3].astype(F32)
        rows[s, pl.ds((3 * fields + 6) * 8, 16), :] = tile
        for k in range(3 * fields + 8, 32):
            rows[s, pl.ds(k * 8, 8), :] = jnp.zeros((8, 128), F32)
    for k, name in enumerate(x_rounds):
        up = upward("gx", name)
        for s in range(len(sides)):
            for ring in (1, 2):
                row = jnp.where(up, 8 - ring, ring - 1)
                outs[k][s, ring - 1] = rows[s, pl.ds(row, 32, stride=8), :]


def shift_z(values, step):
    depth = values.shape[-1]
    lane = lax.broadcasted_iota(jnp.int32, values.shape, values.ndim - 1)
    moved = pltpu.roll(values, (-step) % depth, axis=values.ndim - 1)
    return jnp.where(lane == (depth - 1 if step > 0 else 0), 0.0, moved)


def shift_y(values, step):
    return pltpu.roll(values, (-step) % ROWS, axis=0)


def row_of(ref, index, row):
    return ref[index, pl.ds(row * ROWS, ROWS), :]


COEFFICIENTS = (
    ("own_x", "other_x", "own_y", "other_y", "own_z", "other_z", "cross", "cross_z")
    + ("own_y_down", "other_y_down", "own_z_down", "other_z_down")
)


def coefficients(medium, row, ahead=True):
    def both_of(row):
        return medium(LAME, row) + 2.0 * medium(SHEAR, row)

    shear, lame, inverse = (medium(m, row) for m in (SHEAR, LAME, INV))
    both = both_of(row)
    values = {}
    if ahead:
        values["own_x"] = 0.5 * (both + both_of(row + 1))
        values["other_x"] = 0.5 * (shear + medium(SHEAR, row + 1))
    for tail, step in (("", 1), ("_down", -1)):
        values["own_y" + tail] = 0.5 * (both + shift_y(both, step))
        values["other_y" + tail] = 0.5 * (shear + shift_y(shear, step))
        spacing = 0.25 * (inverse + shift_z(inverse, step))
        values["own_z" + tail] = spacing * (both + shift_z(both, step))
        values["other_z" + tail] = spacing * (shear + shift_z(shear, step))
    values["cross"] = 0.25 * (lame + shear)
    values["cross_z"] = values["cross"] * inverse
    return values


class Event:
    def __init__(self, value):
        self.value = functools.cache(value)
        self.y = functools.cache(lambda c, row, step: shift_y(self.value(c, row), step))
        self.z = functools.cache(lambda c, row, step: shift_z(self.value(c, row), step))

    def slopes(self, c, row):
        return (
            (self.value(c, row + 1) - self.value(c, row - 1))[:8],
            (self.y(c, row, 1) - self.y(c, row, -1))[:8],
            (self.z(c, row, 1) - self.z(c, row, -1))[:8],
        )

    def operator(self, faces):
        value = self.value

        @functools.cache
        def slope(d, row):
            if d == 0:
                return faces("cross", row) * (value(0, row + 1) - value(0, row - 1))
            if d == 1:
                return faces("cross", row) * (self.y(1, row, 1) - self.y(1, row, -1))
            return faces("cross_z", row) * (self.z(2, row, 1) - self.z(2, row, -1))

        @functools.cache
        def flux_x(c, row):
            kind = "own_x" if c == 0 else "other_x"
            return faces(kind, row) * (value(c, row + 1) - value(c, row))

        def apply(row):
            results = []
            for c in range(3):
                here = value(c, row)
                total = flux_x(c, row) - flux_x(c, row - 1)
                kind = "own_y" if c == 1 else "other_y"
                total = total + (
                    faces(kind, row) * (self.y(c, row, 1) - here)
                    - faces(kind + "_down", row) * (here - self.y(c, row, -1))
                )
                kind = "own_z" if c == 2 else "other_z"
                upright = faces(kind, row) * (self.z(c, row, 1) - here) - faces(
                    kind + "_down", row
                ) * (here - self.z(c, row, -1))
                if c == 0:
                    total = total + (
                        (slope(1, row + 1) + slope(2, row + 1))
                        - (slope(1, row - 1) + slope(2, row - 1))
                    )
                elif c == 1:
                    mixed = slope(0, row) + slope(2, row)
                    total = total + (shift_y(mixed, 1) - shift_y(mixed, -1))
                else:
                    mixed = slope(0, row) + slope(1, row)
                    upright = upright + (shift_z(mixed, 1) - shift_z(mixed, -1))
                results.append(total + faces("inverse", row) * upright)
            return results

        return apply


def x_row(up, ring):
    return jnp.where(up, 9 + ring, 2 - ring)


def y_place(up, ring):
    return jnp.where(up, 7 + ring, ROWS - ring)


def tile_row(ref, index, row):
    return ref[index, pl.ds((row - 2) * 8, 8), :]


def own_kernel(events, now, prev, med, cells, force, base, extra):
    fields = 3 * events
    rows = [force[e, s, c, 0] for s in range(2) for e in range(events) for c in range(3)]
    pushed = force_field(cells[0], rows, 64)
    scale = STEP_FACTOR * med[BUOY]
    for f in range(fields):
        base[f] = 2.0 * now[f] - prev[f] + scale * pushed[f * 64 : (f + 1) * 64]
        extra[f] = scale * pushed[(fields + f) * 64 : (fields + f + 1) * 64]


def add_to(sums, key, value):
    sums[key] = sums[key] + value if key in sums else value


def inner_kernel(events, x_rounds, y_rounds, now, base, fwd, med, *refs):
    fields = 3 * events
    x_messages, refs = refs[: len(x_rounds)], refs[len(x_rounds) :]
    y_messages, refs = refs[: len(y_rounds)], refs[len(y_rounds) :]
    here, start, stored, medium, coef, then, part = refs

    for f in range(fields):
        e, c = f // 3, f % 3
        for x in range(8):
            spot = pl.ds((x + 2) * ROWS, 8)
            here[f, spot, :] = now[f, pl.ds(x * 8, 8), :]
            start[f, spot, :] = base[f, pl.ds(x * 8, 8), :]
            for t in range(2):
                stored[2 * f + t, spot, :] = fwd[(e * 4 + t + 1) * 3 + c, x].astype(F32)
    for m in range(4):
        for x in range(8):
            medium[m, pl.ds((x + 2) * ROWS, 8), :] = med[m, pl.ds(x * 8, 8), :]

    def place(tile, put):
        for f in range(fields):
            put(here, f, 1, join(tile(2 * f)))
            put(here, f, 2, join(tile(2 * f + 1)))
            put(start, f, 1, join(tile(2 * fields + f)))
            both = tile(3 * fields + f).astype(F32)
            put(stored, 2 * f, 1, both[:8])
            put(stored, 2 * f + 1, 1, both[8:])
        for k, m in enumerate((SHEAR, LAME, INV)):
            both = tile(4 * fields + k).astype(F32)
            put(medium, m, 1, both[:8])
            put(medium, m, 2, both[8:])
        put(medium, BUOY, 1, tile(4 * fields + 3).astype(F32)[:8])

    def nothing(_):
        return jnp.zeros((16, 128), BF16)

    for k, name in enumerate("AB"):
        up = upward("gx", name)

        def put_x(ref, index, ring, values, up=up):
            row = pl.multiple_of(x_row(up, ring) * ROWS, ROWS)
            ref[index, pl.ds(row, 8), :] = values

        place((lambda i, k=k: x_messages[k][i]) if k < len(x_rounds) else nothing, put_x)
    for k, name in enumerate("AB"):
        up = upward("gy", name)

        def put_y(ref, index, ring, values, up=up):
            ref[index, pl.ds(2 * ROWS + y_place(up, ring), 8, stride=ROWS), :] = values

        place((lambda i, k=k: y_messages[k][i]) if k < len(y_rounds) else nothing, put_y)

    for row in range(1, 11):
        values = coefficients(lambda m, r: row_of(medium, m, r), row, row < 10)
        for name, value in values.items():
            coef[COEFFICIENTS.index(name), pl.ds(row * ROWS, ROWS), :] = value

    def faces(name, row):
        if name == "inverse":
            return row_of(medium, INV, row)
        return row_of(coef, COEFFICIENTS.index(name), row)

    sums = {}
    for e in range(events):
        first = Event(lambda c, row, e=e: row_of(here, 3 * e + c, row))
        apply = first.operator(faces)
        waves = [
            Event(lambda c, row, e=e, t=t: row_of(stored, 2 * (3 * e + c) + t, row))
            for t in range(2)
        ]
        for row in range(2, 10):
            if 3 <= row <= 8:
                scale = STEP_FACTOR * row_of(medium, BUOY, row)
                for c, result in enumerate(apply(row)):
                    f = 3 * e + c
                    then[f, pl.ds(row * ROWS, ROWS), :] = row_of(start, f, row) + scale * result
            gather(sums, first, waves[0], fwd, e, 0, row)
        second = Event(lambda c, row, e=e: row_of(then, 3 * e + c, row))
        for row in range(4, 8):
            gather(sums, second, waves[1], fwd, e, 1, row)
    for row in range(2, 10):
        inverse = tile_row(med, INV, row)
        shear = sums["lateral", row] + inverse * inverse * sums["upright", row]
        part[0, pl.ds((row - 2) * 8, 8), :] = -0.25 * shear
        part[1, pl.ds((row - 2) * 8, 8), :] = -sums["density", row]


def gather(sums, field, wave, fwd, e, t, row):
    for c in range(3):
        ax, ay, az = field.slopes(c, row)
        ux, uy, uz = wave.slopes(c, row)
        newer = fwd[(e * 4 + t) * 3 + c, row - 2].astype(F32)
        older = fwd[(e * 4 + t + 2) * 3 + c, row - 2].astype(F32)
        bend = newer - 2.0 * wave.value(c, row)[:8] + older
        add_to(sums, ("lateral", row), ax * ux + ay * uy)
        add_to(sums, ("upright", row), az * uz)
        add_to(sums, ("density", row), field.value(c, row)[:8] * bend)


OUTER = (0, 1, 10, 11)
EDGES = (1, 2, 9, 10)


def edge_kernel(events, x_rounds, y_rounds, shares, *refs):
    fields = 3 * events
    corners, refs = refs[: len(x_rounds)], refs[len(x_rounds) :]
    (here, start, stored, medium, coef, then, part, fwd, med), refs = refs[:9], refs[9:]
    edge, own_share, *sent = refs[: 1 + shares]
    outer, outer_start, outer_medium, outer_coef, slabs = refs[1 + shares :]

    for k, row in enumerate(OUTER):
        spot = pl.ds(k * ROWS, ROWS)
        for f in range(fields):
            outer[f, spot, :] = row_of(here, f, row)
            if row in EDGES:
                outer_start[f, spot, :] = row_of(start, f, row)
        for m in range(4):
            outer_medium[m, spot, :] = row_of(medium, m, row)
    for kx, name_x in enumerate("AB"):
        for ky, name_y in enumerate("AB"):
            up_x, up_y = upward("gx", name_x), upward("gy", name_y)
            for ring_x in (1, 2):
                for ring_y in (1, 2):
                    place = jnp.where(up_x, 1 + ring_x, 2 - ring_x)
                    spot = place * ROWS + y_place(up_y, ring_y)

                    def move(ref, index, k):
                        if kx < len(x_rounds) and ky < len(y_rounds):
                            values = corners[kx][ky, ring_x - 1, pl.ds(k, 1), :]
                        else:
                            values = jnp.zeros((1, 128), F32)
                        ref[index, pl.ds(spot, 1), :] = values

                    for f in range(fields):
                        move(outer, f, 2 * f + ring_y - 1)
                        if ring_x == 1 and ring_y == 1:
                            move(outer_start, f, 2 * fields + f)
                    for k, m in enumerate((SHEAR, LAME, INV)):
                        move(outer_medium, m, 3 * fields + 2 * k + ring_y - 1)
                    if ring_x == 1 and ring_y == 1:
                        move(outer_medium, BUOY, 3 * fields + 6)

    def outer_or(ref, full):
        def pick(index, row):
            if row in OUTER:
                return row_of(ref, index, OUTER.index(row))
            return row_of(full, index, row)

        return pick

    field_row, start_row = outer_or(outer, here), outer_or(outer_start, start)
    medium_row = outer_or(outer_medium, medium)
    fresh = (0, 1, 9, 10, 11)
    for k, row in enumerate(fresh):
        for name, value in coefficients(medium_row, row, row < 11).items():
            outer_coef[COEFFICIENTS.index(name), pl.ds(k * ROWS, ROWS), :] = value

    def faces(name, row):
        if name == "inverse":
            return medium_row(INV, row)
        index = COEFFICIENTS.index(name)
        if row in fresh:
            return row_of(outer_coef, index, fresh.index(row))
        return row_of(coef, index, row)

    def then_row(f, row):
        if row in EDGES:
            return row_of(edge, f, EDGES.index(row))
        return row_of(then, f, row)

    sums = {}
    for e in range(events):
        apply = Event(lambda c, row, e=e: field_row(3 * e + c, row)).operator(faces)
        for k, row in enumerate(EDGES):
            scale = STEP_FACTOR * medium_row(BUOY, row)
            for c, result in enumerate(apply(row)):
                f = 3 * e + c
                edge[f, pl.ds(k * ROWS, ROWS), :] = start_row(f, row) + scale * result
        second = Event(lambda c, row, e=e: then_row(3 * e + c, row))
        wave = Event(lambda c, row, e=e: row_of(stored, 2 * (3 * e + c) + 1, row))
        for row in (2, 3, 8, 9):
            gather(sums, second, wave, fwd, e, 1, row)
    grads = [[], []]
    for row in range(2, 10):
        shear, density = tile_row(part, 0, row), tile_row(part, 1, row)
        if row in (2, 3, 8, 9):
            inverse = tile_row(med, INV, row)
            more = sums["lateral", row] + inverse * inverse * sums["upright", row]
            shear = shear - 0.25 * more
            density = density - sums["density", row]
        grads[0].append(shear)
        grads[1].append(density)
    grads = grads[0] + grads[1]
    piece = 128 // shares
    quarter = lax.broadcasted_iota(jnp.int32, (8, 128), 1) // piece
    per = len(grads) // shares
    for j in range(shares):
        for r in range(per):
            tile = None
            for g in range(shares):
                source = grads[r * shares + g]
                moved = pltpu.roll(source, ((g - j) * piece) % 128, axis=1) if g != j else source
                tile = moved if tile is None else jnp.where(quarter == g, moved, tile)
            slabs[j, pl.ds(r * 8, 8), :] = tile
    me = lax.axis_index("ev")
    own_share[...] = slabs[me]
    for m in range(1, shares):
        sent[m - 1][...] = slabs[me ^ m]


def second_kernel(events, now, extra, med, medium, coef, then, edge, mid, after):
    def faces(name, row):
        if name == "inverse":
            return row_of(medium, INV, row)
        return row_of(coef, COEFFICIENTS.index(name), row)

    def then_row(f, row):
        if row in EDGES:
            return row_of(edge, f, EDGES.index(row))
        return row_of(then, f, row)

    for e in range(events):
        apply = Event(lambda c, row, e=e: then_row(3 * e + c, row)).operator(faces)
        for row in range(2, 10):
            spot = pl.ds((row - 2) * 8, 8)
            scale = STEP_FACTOR * tile_row(med, BUOY, row)
            for c, result in enumerate(apply(row)):
                f = 3 * e + c
                current = then_row(f, row)[:8]
                mid[f, spot, :] = current
                after[f, spot, :] = (
                    2.0 * current - now[f, spot, :] + extra[f, spot, :] + scale * result[:8]
                )


def finish_kernel(shares, scale, *refs):
    pieces, (shear, density) = refs[:shares], refs[shares:]
    total = pieces[0][...]
    for piece in pieces[1:]:
        total = total + piece[...]
    width = 128 // shares
    for v in range(16):
        g, r = v % shares, v // shares
        tile = total[r * 8 : (r + 1) * 8]
        if g:
            tile = pltpu.roll(tile, (-g * width) % 128, axis=1)
        out = shear if v < 8 else density
        out[pl.ds((v % 8) * 8, 8), :] = tile[:, :width] * scale


def call(kernel, outs, ins, scratch=(), name=None, limit=VMEM_LIMIT, cost=1000):
    return pl.pallas_call(
        kernel,
        out_shape=[jax.ShapeDtypeStruct(s, d) for s, d in outs],
        in_specs=[pl.BlockSpec(memory_space=m) for m in ins],
        scratch_shapes=[s if not isinstance(s, tuple) else pltpu.VMEM(*s) for s in scratch],
        compiler_params=pltpu.CompilerParams(vmem_limit_bytes=limit),
        cost_estimate=pl.CostEstimate(
            flops=cost * 1024, bytes_accessed=cost * 1024, transcendentals=0
        ),
        name=name,
    )


def body(adjoint_now, adjoint_prev, forward, medium, drm_cells, drm_force):
    events, _, width_x, width_y, depth = adjoint_now.shape
    fields = 3 * events
    tile = width_x * width_y
    shares = lax.axis_size("ev")
    x_rounds, y_rounds = rounds_of(lax.axis_size("gx")), rounds_of(lax.axis_size("gy"))
    now = adjoint_now.reshape(fields, tile, depth)
    prev = adjoint_prev.reshape(fields, tile, depth)
    fwd = forward.reshape(events * 12, width_x, width_y, depth)
    med = medium.reshape(4, tile, depth)
    own = ((fields, tile, depth), F32)
    tall = 12 * ROWS

    messages = call(
        functools.partial(pack_kernel, events, x_rounds, y_rounds),
        [((4 * fields + 4, 16, depth), BF16)] * (len(x_rounds) + len(y_rounds)),
        [pltpu.HBM] * 6,
        [
            own,
            own,
            ((2 * fields, width_x, width_y, depth), BF16),
            ((4, tile, depth), F32),
            (drm_cells.shape, drm_cells.dtype),
            (drm_force.shape, F32),
            own,
            ((2 * fields, tile, depth), F32),
            pltpu.SemaphoreType.DMA((5 + events,)),
        ],
        "pack",
        PACK_LIMIT,
    )(now, prev, fwd, med, drm_cells, drm_force)
    y_messages = [swap(m, "gy", r) for m, r in zip(messages[len(x_rounds) :], y_rounds)]
    x_messages = [swap(m, "gx", r) for m, r in zip(messages, x_rounds)]
    base, extra = call(
        functools.partial(own_kernel, events),
        [own, own],
        [pltpu.VMEM] * 5,
        name="own",
    )(now, prev, med, drm_cells, drm_force)
    corners = []
    if x_rounds and y_rounds:
        corners = call(
            functools.partial(corner_kernel, fields, x_rounds, y_rounds),
            [((len(y_rounds), 2, 32, depth), F32)] * len(x_rounds),
            [pltpu.VMEM] * len(y_rounds),
            [((len(y_rounds), 32 * 8, depth), F32)],
            "corners",
        )(*y_messages)
        corners = [swap(m, "gx", r) for m, r in zip(corners, x_rounds)]

    wide = ((fields, tall, depth), F32)
    here, start, stored, tall_medium, coef, then, part = call(
        functools.partial(inner_kernel, events, x_rounds, y_rounds),
        [
            wide,
            wide,
            ((2 * fields, tall, depth), F32),
            ((4, tall, depth), F32),
            ((len(COEFFICIENTS), tall, depth), F32),
            wide,
            ((2, tile, depth), F32),
        ],
        [pltpu.VMEM] * (4 + len(x_messages) + len(y_messages)),
        name="inner",
        cost=3000,
    )(now, base, fwd, med, *x_messages, *y_messages)
    slab = ((16 // shares * 8, depth), F32)
    outer = ((fields, len(OUTER) * ROWS, depth), F32)
    if not corners:
        corners = [jnp.zeros((2, 2, 32, depth), F32)] * len(x_rounds)
    edge, own_share, *sent = call(
        functools.partial(edge_kernel, events, x_rounds, y_rounds, shares),
        [outer] + [slab] * shares,
        [pltpu.VMEM] * (9 + len(corners)),
        [
            outer,
            outer,
            ((4, len(OUTER) * ROWS, depth), F32),
            ((len(COEFFICIENTS), 5 * ROWS, depth), F32),
            ((shares,) + slab[0], F32),
        ],
        "edges",
    )(*corners, here, start, stored, tall_medium, coef, then, part, fwd, med)
    pieces = [own_share]
    for m in reversed(range(1, shares)):
        pairs = [(i, i ^ m) for i in range(shares)]
        pieces.append(lax.ppermute(sent[m - 1], "ev", pairs))
    mid, after = call(
        functools.partial(second_kernel, events),
        [own, own],
        [pltpu.VMEM] * 7,
        name="second",
    )(now, extra, med, tall_medium, coef, then, edge)
    shear, density = call(
        functools.partial(finish_kernel, shares, 1.0 / (events * shares)),
        [((tile, depth // shares), F32)] * 2,
        [pltpu.VMEM] * shares,
        name="finish",
    )(*pieces)
    shape = adjoint_now.shape
    grad = (width_x, width_y, depth // shares)
    return mid.reshape(shape), after.reshape(shape), shear.reshape(grad), density.reshape(grad)


def solution(mesh):
    in_specs = (
        P("ev", None, "gx", "gy", None),
        P("ev", None, "gx", "gy", None),
        P("ev", None, None, "gx", "gy", None),
        P(None, "gx", "gy", None),
        P("gx", "gy", None),
        P("ev", None, None, "gx", "gy", None),
    )
    out_specs = (
        P("ev", None, "gx", "gy", None),
        P("ev", None, "gx", "gy", None),
        P("gx", "gy", "ev"),
        P("gx", "gy", "ev"),
    )
    return jax.shard_map(body, mesh=mesh, in_specs=in_specs, out_specs=out_specs, check_vma=False)
```

time: 27.8 us -> 21.7 us (0.78)
  the two profiles are of different devices: /device:TPU:9 before, /device:TPU:21 now
where the time goes in v2:
time: 21.7 us; the launch traced here: 21.5 us
  starting transfers between devices  8.74 us (40%)
  waiting for transfers between devices  6.18 us (28%)
  Pallas kernels  5.83 us (27%)
  between operations  0.75 us (3%)
    ppermute x4, waiting for transfers between devices, swap(): return lax.ppermute(values, axis, pairs)  5.02 us
    ppermute x3, starting transfers between devices, body(): pieces.append(lax.ppermute(sent[m - 1], 'ev', pairs))  4.89 us
    ppermute x4, starting transfers between devices, swap(): return lax.ppermute(values, axis, pairs)  3.85 us
    pallas_call x1, Pallas kernels, body(): call(functools.partial(pack_kernel, events, x_rounds, y_rounds), [((4 * f...  2.17 us
    ppermute x3, waiting for transfers between devices, body(): pieces.append(lax.ppermute(sent[m - 1], 'ev', pairs))  1.16 us
    pallas_call x1, Pallas kernels, body(): call(functools.partial(inner_kernel, events, x_rounds, y_rounds), [wide,...  1 us
    pallas_call x1, Pallas kernels, body(): call(functools.partial(second_kernel, events), [own, own], [pltpu.VMEM] *...  0.96 us
    pallas_call x1, Pallas kernels, body(): call(functools.partial(finish_kernel, shares, 1.0 / (events * shares)), [...  0.7 us
  transfers between devices with their start and end apart: 7, of which 5 were waited for; matrix products, arithmetic and copies ran while one was open for 0% of the time, Pallas kernels for 11%

profile of v2, /device:TPU:21, one launch (start us, length us, event | category | flops | bytes accessed | tf_op | source)
XLA Modules:
  0.0 21.5 jit_solution(5876481944759317181)
XLA Ops:
  0.6 0.0 copy-start.2
  0.6 0.0 copy-start.3
  0.7 0.0 copy-start.1
  0.7 0.0 copy-start.5
  0.7 0.0 copy-start.4
  0.7 0.0 copy-start
  0.7 2.2 %pack.1 = (bf16[28,16,128]{2,1,0:T(8,128)(2,1)}, bf16[28,16,128]{2,1,0:T(8,128)(2,1)}, bf16[28,16,128]{2,1,0:T(8,128)(2,1)}) custom-call(f32[6,64,128]{2,1,0:T(8,128)} %bitcast.16, f32[6,64,128]{2,1,0:T(8,128)} %bitcast.20, bf16[24,8,8,128]{3,2,1,0:T(8,128)(2,1)} %bitcast.8, f32[4,64,128]{2,1,0:T(8,128)} %bitcast.11, s32[1,1,128]{2,1,0:T(1,128)} %refs_4_.1, ...), custom_call_target="tpu_custom_call" | custom-call | flops 1024000 | bytes 1024000 | tf_op jit(solution)/shard_map/pack/pallas_call | solution.py:554
  2.9 1.4 %collective-permute-start.1 = (bf16[28,16,128]{2,1,0:T(8,128)(2,1)}, bf16[28,16,128]{2,1,0:T(8,128)(2,1)S(1)}, u32[]{:S(2)}, u32[]{:S(2)}) collective-permute-start(bf16[28,16,128]{2,1,0:T(8,128)(2,1)} %get-tuple-element.28), channel_id=1, source_target_pairs={{0,1},{1,0},{2,3},{3,2},{4,5},{5,4},{6,7},{7,6},{8,9},{9,8},{10,11... | collective-permute-start | bytes 344072 | tf_op jit(solution)/shard_map/ppermute | solution.py:29
  4.2 1.9 %collective-permute-start.2 = (bf16[28,16,128]{2,1,0:T(8,128)(2,1)}, bf16[28,16,128]{2,1,0:T(8,128)(2,1)S(1)}, u32[]{:S(2)}, u32[]{:S(2)}) collective-permute-start(bf16[28,16,128]{2,1,0:T(8,128)(2,1)} %get-tuple-element.29), channel_id=1, source_target_pairs={{1,2},{2,1},{5,6},{6,5},{9,10},{10,9},{13,14},{14,13},{17,18},{18,... | collective-permute-start | bytes 344072 | tf_op jit(solution)/shard_map/ppermute | solution.py:29
  6.1 0.3 %collective-permute-start = (bf16[28,16,128]{2,1,0:T(8,128)(2,1)}, bf16[28,16,128]{2,1,0:T(8,128)(2,1)S(1)}, u32[]{:S(2)}, u32[]{:S(2)}) collective-permute-start(bf16[28,16,128]{2,1,0:T(8,128)(2,1)} %get-tuple-element.27), channel_id=1, source_target_pairs={{0,4},{4,0},{1,5},{5,1},{2,6},{6,2},{3,7},{7,3},{8,12},{12,8},{9,1... | collective-permute-start | bytes 344072 | tf_op jit(solution)/shard_map/ppermute | solution.py:29
  6.4 0.7 %collective-permute-done.1.refs_1_.refs_0_ = bf16[28,16,128]{2,1,0:T(8,128)(2,1)S(1)} collective-permute-done((bf16[28,16,128]{2,1,0:T(8,128)(2,1)}, bf16[28,16,128]{2,1,0:T(8,128)(2,1)S(1)}, u32[]{:S(2)}, u32[]{:S(2)}) %collective-permute-start.1) | collective-permute-done | bytes 114720 | tf_op jit(solution)/shard_map/ppermute | solution.py:29
  7.2 2.8 %collective-permute-done.2.refs_2_.refs_1_ = bf16[28,16,128]{2,1,0:T(8,128)(2,1)S(1)} collective-permute-done((bf16[28,16,128]{2,1,0:T(8,128)(2,1)}, bf16[28,16,128]{2,1,0:T(8,128)(2,1)S(1)}, u32[]{:S(2)}, u32[]{:S(2)}) %collective-permute-start.2) | collective-permute-done | bytes 114720 | tf_op jit(solution)/shard_map/ppermute | solution.py:29
  10.0 0.3 %collective-permute-start.3 = (f32[2,2,32,128]{3,2,1,0:T(8,128)S(1)}, f32[2,2,32,128]{3,2,1,0:T(8,128)S(1)}, u32[]{:S(2)}, u32[]{:S(2)}) collective-permute-start(f32[2,2,32,128]{3,2,1,0:T(8,128)S(1)} %corners.1), channel_id=1, source_target_pairs={{0,4},{4,0},{1,5},{5,1},{2,6},{6,2},{3,7},{7,3},{8,12},{12,8},{9,1... | collective-permute-start | bytes 196616 | tf_op jit(solution)/shard_map/ppermute | solution.py:29
  10.3 0.0 copy-done.2
  10.3 0.0 copy-done.3
  10.3 0.0 copy-done.1
  10.3 0.0 copy-done.5
  10.3 0.0 copy-done.4
  10.3 0.3 %own.1 = (f32[6,64,128]{2,1,0:T(8,128)S(1)}, f32[6,64,128]{2,1,0:T(8,128)S(1)}) custom-call(f32[6,64,128]{2,1,0:T(8,128)S(1)} %bitcast.17, f32[6,64,128]{2,1,0:T(8,128)S(1)} %bitcast.21, f32[4,64,128]{2,1,0:T(8,128)S(1)} %bitcast.12, s32[1,1,128]{2,1,0:T(1,128)S(1)} %copy-done.5, f32[2,2,3,1,1,128]{5,4,3,2,1,0:T(1,128)S(1)} %copy-done.4), custom_call_target="tpu_custom_call" | custom-call | flops 1024000 | bytes 1024000 | tf_op jit(solution)/shard_map/own/pallas_call | solution.py:574
  10.7 0.0 collective-permute-done.refs_0_
  10.7 0.0 copy-done
  10.7 1.0 %inner.1 = (f32[6,192,128]{2,1,0:T(8,128)S(1)}, f32[6,192,128]{2,1,0:T(8,128)S(1)}, f32[12,192,128]{2,1,0:T(8,128)S(1)}, f32[4,192,128]{2,1,0:T(8,128)S(1)}, f32...) custom-call(f32[6,64,128]{2,1,0:T(8,128)S(1)} %bitcast.18, ...), custom_call_target="tpu_custom_call" | custom-call | flops 3072000 | bytes 3072000 | tf_op jit(solution)/shard_map/inner/pallas_call | solution.py:592
  11.7 1.5 %collective-permute-done.3.refs_0_ = f32[2,2,32,128]{3,2,1,0:T(8,128)S(1)} collective-permute-done((f32[2,2,32,128]{3,2,1,0:T(8,128)S(1)}, f32[2,2,32,128]{3,2,1,0:T(8,128)S(1)}, u32[]{:S(2)}, u32[]{:S(2)}) %collective-permute-start.3) | collective-permute-done | bytes 65568 | tf_op jit(solution)/shard_map/ppermute | solution.py:29
  13.2 0.6 %edges.1 = (f32[6,64,128]{2,1,0:T(8,128)S(1)}, f32[32,128]{1,0:T(8,128)S(1)}, f32[32,128]{1,0:T(8,128)S(1)}, f32[32,128]{1,0:T(8,128)S(1)}, f32[32,128]{1,0:T(8,128)S(1)}) custom-call(f32[2,2,32,128]{3,2,1,0:T(8,128)S(1)} %collective-permute-done.3.refs_0_, f32[6,192,128]{2,1,0:T(8,128)S(1)} %get-tuple-element.33.refs_1_, ...), custom_call_target="tpu_custom_call" | custom-call | flops 1024000 | bytes 1024000 | tf_op jit(solution)/shard_map/edges/pallas_call | solution.py:611
  13.8 4.4 %collective-permute-start.4 = (f32[32,128]{1,0:T(8,128)S(1)}, f32[32,128]{1,0:T(8,128)S(1)}, u32[]{:S(2)}, u32[]{:S(2)}) collective-permute-start(f32[32,128]{1,0:T(8,128)S(1)} %get-tuple-element.41), channel_id=1, source_target_pairs={{0,24},{8,16},{16,8},{24,0},{1,25},{9,17},{17,9},{25,1},{2,26},{10... | collective-permute-start | bytes 49160 | tf_op jit(solution)/shard_map/ppermute | solution.py:627
  18.2 0.3 %collective-permute-start.5 = (f32[32,128]{1,0:T(8,128)S(1)}, f32[32,128]{1,0:T(8,128)S(1)}, u32[]{:S(2)}, u32[]{:S(2)}) collective-permute-start(f32[32,128]{1,0:T(8,128)S(1)} %get-tuple-element.42), channel_id=1, source_target_pairs={{0,16},{8,24},{16,0},{24,8},{1,17},{9,25},{17,1},{25,9},{2,18},{10... | collective-permute-start | bytes 49160 | tf_op jit(solution)/shard_map/ppermute | solution.py:627
  18.5 0.2 %collective-permute-start.6 = (f32[32,128]{1,0:T(8,128)S(1)}, f32[32,128]{1,0:T(8,128)S(1)}, u32[]{:S(2)}, u32[]{:S(2)}) collective-permute-start(f32[32,128]{1,0:T(8,128)S(1)} %get-tuple-element.43), channel_id=1, source_target_pairs={{0,8},{8,0},{16,24},{24,16},{1,9},{9,1},{17,25},{25,17},{2,10},{10... | collective-permute-start | bytes 49160 | tf_op jit(solution)/shard_map/ppermute | solution.py:627
  18.7 1.0 %second.1 = (f32[6,64,128]{2,1,0:T(8,128)}, f32[6,64,128]{2,1,0:T(8,128)}) custom-call(f32[6,64,128]{2,1,0:T(8,128)S(1)} %bitcast.19, f32[6,64,128]{2,1,0:T(8,128)S(1)} %get-tuple-element.25.extra, f32[4,64,128]{2,1,0:T(8,128)S(1)} %bitcast.15, f32[4,192,128]{2,1,0:T(8,128)S(1)} %get-tuple-element.30.refs_4_.medium, ...), custom_call_target="tpu_custom_call" | custom-call | flops 1024000 | bytes 1024000 | tf_op jit(solution)/shard_map/second/pallas_call | solution.py:628
  19.7 0.4 %collective-permute-done.4.refs_1_ = f32[32,128]{1,0:T(8,128)S(1)} collective-permute-done((f32[32,128]{1,0:T(8,128)S(1)}, f32[32,128]{1,0:T(8,128)S(1)}, u32[]{:S(2)}, u32[]{:S(2)}) %collective-permute-start.4) | collective-permute-done | bytes 16416 | tf_op jit(solution)/shard_map/ppermute | solution.py:627
  20.0 0.8 %collective-permute-done.5.refs_2_ = f32[32,128]{1,0:T(8,128)S(1)} collective-permute-done((f32[32,128]{1,0:T(8,128)S(1)}, f32[32,128]{1,0:T(8,128)S(1)}, u32[]{:S(2)}, u32[]{:S(2)}) %collective-permute-start.5) | collective-permute-done | bytes 16416 | tf_op jit(solution)/shard_map/ppermute | solution.py:627
  20.8 0.0 collective-permute-done.6.refs_3_
  20.8 0.7 %finish.1 = (f32[64,32]{1,0:T(8,128)}, f32[64,32]{1,0:T(8,128)}) custom-call(f32[32,128]{1,0:T(8,128)S(1)} %get-tuple-element.40.refs_0_, f32[32,128]{1,0:T(8,128)S(1)} %collective-permute-done.4.refs_1_, f32[32,128]{1,0:T(8,128)S(1)} %collective-permute-done.5.refs_2_, f32[32,128]{1,0:T(8,128)S(1)} %collective-permute-done.6.refs_3_), custom_call_target="tpu_custom_call" | custom-call | flops 1024000 | bytes 1024000 | tf_op jit(solution)/shard_map/finish/pallas_call | solution.py:634
  (1 shorter events, 0.0 us)
Async XLA Ops:
  0.6 9.7 %copy-start.2 = (f32[2,3,8,8,128]{4,3,2,1,0:T(8,128)S(1)}, f32[2,3,8,8,128]{4,3,2,1,0:T(8,128)}, u32[]{:S(2)}) copy-start(f32[2,3,8,8,128]{4,3,2,1,0:T(8,128)} %param.6) | copy-start | bytes 589828
  0.6 9.7 %copy-start.3 = (f32[2,3,8,8,128]{4,3,2,1,0:T(8,128)S(1)}, f32[2,3,8,8,128]{4,3,2,1,0:T(8,128)}, u32[]{:S(2)}) copy-start(f32[2,3,8,8,128]{4,3,2,1,0:T(8,128)} %param.7) | copy-start | bytes 589828
  0.7 9.7 %copy-start.1 = (f32[4,8,8,128]{3,2,1,0:T(8,128)S(1)}, f32[4,8,8,128]{3,2,1,0:T(8,128)}, u32[]{:S(2)}) copy-start(f32[4,8,8,128]{3,2,1,0:T(8,128)} %param.9) | copy-start | bytes 393220
  0.7 9.6 %copy-start.5 = (s32[1,1,128]{2,1,0:T(1,128)S(1)}, s32[1,1,128]{2,1,0:T(1,128)}, u32[]{:S(2)}) copy-start(s32[1,1,128]{2,1,0:T(1,128)} %refs_4_.1) | copy-start | bytes 1540
  0.7 9.6 %copy-start.4 = (f32[2,2,3,1,1,128]{5,4,3,2,1,0:T(1,128)S(1)}, f32[2,2,3,1,1,128]{5,4,3,2,1,0:T(1,128)}, u32[]{:S(2)}) copy-start(f32[2,2,3,1,1,128]{5,4,3,2,1,0:T(1,128)} %refs_5_.1) | copy-start | bytes 18436
  0.7 10.0 %copy-start = (bf16[2,4,3,8,8,128]{5,4,3,2,1,0:T(8,128)(2,1)S(1)}, bf16[2,4,3,8,8,128]{5,4,3,2,1,0:T(8,128)(2,1)}, u32[]{:S(2)}) copy-start(bf16[2,4,3,8,8,128]{5,4,3,2,1,0:T(8,128)(2,1)} %param.8) | copy-start | bytes 1179652
  2.9 4.3 %collective-permute-start.1 = (bf16[28,16,128]{2,1,0:T(8,128)(2,1)}, bf16[28,16,128]{2,1,0:T(8,128)(2,1)S(1)}, u32[]{:S(2)}, u32[]{:S(2)}) collective-permute-start(bf16[28,16,128]{2,1,0:T(8,128)(2,1)} %get-tuple-element.28), channel_id=1, source_target_pairs={{0,1},{1,0},{2,3},{3,2},{4,5},{5,4},{6,7},{7,6},{8,9},{9,8},{10,11... | collective-permute-start | bytes 344072 | tf_op jit(solution)/shard_map/ppermute | solution.py:29
  4.2 5.7 %collective-permute-start.2 = (bf16[28,16,128]{2,1,0:T(8,128)(2,1)}, bf16[28,16,128]{2,1,0:T(8,128)(2,1)S(1)}, u32[]{:S(2)}, u32[]{:S(2)}) collective-permute-start(bf16[28,16,128]{2,1,0:T(8,128)(2,1)} %get-tuple-element.29), channel_id=1, source_target_pairs={{1,2},{2,1},{5,6},{6,5},{9,10},{10,9},{13,14},{14,13},{17,18},{18,... | collective-permute-start | bytes 344072 | tf_op jit(solution)/shard_map/ppermute | solution.py:29
  6.1 4.5 %collective-permute-start = (bf16[28,16,128]{2,1,0:T(8,128)(2,1)}, bf16[28,16,128]{2,1,0:T(8,128)(2,1)S(1)}, u32[]{:S(2)}, u32[]{:S(2)}) collective-permute-start(bf16[28,16,128]{2,1,0:T(8,128)(2,1)} %get-tuple-element.27), channel_id=1, source_target_pairs={{0,4},{4,0},{1,5},{5,1},{2,6},{6,2},{3,7},{7,3},{8,12},{12,8},{9,1... | collective-permute-start | bytes 344072 | tf_op jit(solution)/shard_map/ppermute | solution.py:29
  10.0 3.2 %collective-permute-start.3 = (f32[2,2,32,128]{3,2,1,0:T(8,128)S(1)}, f32[2,2,32,128]{3,2,1,0:T(8,128)S(1)}, u32[]{:S(2)}, u32[]{:S(2)}) collective-permute-start(f32[2,2,32,128]{3,2,1,0:T(8,128)S(1)} %corners.1), channel_id=1, source_target_pairs={{0,4},{4,0},{1,5},{5,1},{2,6},{6,2},{3,7},{7,3},{8,12},{12,8},{9,1... | collective-permute-start | bytes 196616 | tf_op jit(solution)/shard_map/ppermute | solution.py:29
  13.8 6.2 %collective-permute-start.4 = (f32[32,128]{1,0:T(8,128)S(1)}, f32[32,128]{1,0:T(8,128)S(1)}, u32[]{:S(2)}, u32[]{:S(2)}) collective-permute-start(f32[32,128]{1,0:T(8,128)S(1)} %get-tuple-element.41), channel_id=1, source_target_pairs={{0,24},{8,16},{16,8},{24,0},{1,25},{9,17},{17,9},{25,1},{2,26},{10... | collective-permute-start | bytes 49160 | tf_op jit(solution)/shard_map/ppermute | solution.py:627
  18.2 2.6 %collective-permute-start.5 = (f32[32,128]{1,0:T(8,128)S(1)}, f32[32,128]{1,0:T(8,128)S(1)}, u32[]{:S(2)}, u32[]{:S(2)}) collective-permute-start(f32[32,128]{1,0:T(8,128)S(1)} %get-tuple-element.42), channel_id=1, source_target_pairs={{0,16},{8,24},{16,0},{24,8},{1,17},{9,25},{17,1},{25,9},{2,18},{10... | collective-permute-start | bytes 49160 | tf_op jit(solution)/shard_map/ppermute | solution.py:627
  18.5 2.3 %collective-permute-start.6 = (f32[32,128]{1,0:T(8,128)S(1)}, f32[32,128]{1,0:T(8,128)S(1)}, u32[]{:S(2)}, u32[]{:S(2)}) collective-permute-start(f32[32,128]{1,0:T(8,128)S(1)} %get-tuple-element.43), channel_id=1, source_target_pairs={{0,8},{8,0},{16,24},{24,16},{1,9},{9,1},{17,25},{25,17},{2,10},{10... | collective-permute-start | bytes 49160 | tf_op jit(solution)/shard_map/ppermute | solution.py:627

commit v3 on v2

--- a/solution.py
+++ b/solution.py
@@ -1,4 +1,5 @@
 import functools
+import itertools
 
 import jax
 import jax.numpy as jnp
@@ -21,12 +22,24 @@
 
 
 def swap(values, axis, name):
-    count = lax.axis_size(axis)
-    first = "AB".index(name)
+    names = ("ev", "gx", "gy")
+    sizes = [lax.axis_size(a) for a in names]
+    along = names.index(axis)
     pairs = []
-    for low in range(first, count - 1, 2):
-        pairs += [(low, low + 1), (low + 1, low)]
-    return lax.ppermute(values, axis, pairs)
+    for source in itertools.product(*map(range, sizes)):
+        target = list(source)
+        up = (source[along] % 2 == 0) == (name == "A")
+        target[along] += 1 if up else -1
+        if not 0 <= target[along] < sizes[along]:
+            target = [source[0] ^ 1, *source[1:]]
+        flat = [(s[0] * sizes[1] + s[1]) * sizes[2] + s[2] for s in (source, target)]
+        pairs.append(tuple(flat))
+    return lax.ppermute(values, names, pairs)
+
+
+def linked(axis, name):
+    other = lax.axis_index(axis) + jnp.where(upward(axis, name), 1, -1)
+    return jnp.logical_and(other >= 0, other < lax.axis_size(axis))
 
 
 def upward(axis, name):
@@ -125,23 +138,31 @@
         fill(messages[len(x_rounds) + k], pick_y)
 
 
+def masked(message, axis, name):
+    if name == "A" and lax.axis_size(axis) % 2 == 0:
+        return lambda index: message[index]
+    real = linked(axis, name)
+    return lambda index: jnp.where(real, message[index].astype(F32), 0.0).astype(BF16)
+
+
 def corner_kernel(fields, x_rounds, y_rounds, *refs):
     sides = refs[: len(y_rounds)]
     outs = refs[len(y_rounds) : len(y_rounds) + len(x_rounds)]
     rows = refs[-1]
-    for s, side in enumerate(sides):
+    for s, name in enumerate(y_rounds):
+        side = masked(sides[s], "gy", name)
         for k in range(3 * fields):
-            rows[s, pl.ds(k * 8, 8), :] = join(side[k])
+            rows[s, pl.ds(k * 8, 8), :] = join(side(k))
         for k in range(3):
-            tile = side[4 * fields + k].astype(F32)
+            tile = side(4 * fields + k).astype(F32)
             rows[s, pl.ds((3 * fields + 2 * k) * 8, 16), :] = tile
-        tile = side[4 * fields + 3].astype(F32)
+        tile = side(4 * fields + 3).astype(F32)
         rows[s, pl.ds((3 * fields + 6) * 8, 16), :] = tile
         for k in range(3 * fields + 8, 32):
             rows[s, pl.ds(k * 8, 8), :] = jnp.zeros((8, 128), F32)
     for k, name in enumerate(x_rounds):
         up = upward("gx", name)
-        for s in range(len(sides)):
+        for s in range(len(y_rounds)):
             for ring in (1, 2):
                 row = jnp.where(up, 8 - ring, ring - 1)
                 outs[k][s, ring - 1] = rows[s, pl.ds(row, 32, stride=8), :]
@@ -317,14 +338,14 @@
             row = pl.multiple_of(x_row(up, ring) * ROWS, ROWS)
             ref[index, pl.ds(row, 8), :] = values
 
-        place((lambda i, k=k: x_messages[k][i]) if k < len(x_rounds) else nothing, put_x)
+        place(masked(x_messages[k], "gx", name) if k < len(x_rounds) else nothing, put_x)
     for k, name in enumerate("AB"):
         up = upward("gy", name)
 
         def put_y(ref, index, ring, values, up=up):
             ref[index, pl.ds(2 * ROWS + y_place(up, ring), 8, stride=ROWS), :] = values
 
-        place((lambda i, k=k: y_messages[k][i]) if k < len(y_rounds) else nothing, put_y)
+        place(masked(y_messages[k], "gy", name) if k < len(y_rounds) else nothing, put_y)
 
     for row in range(1, 11):
         values = coefficients(lambda m, r: row_of(medium, m, r), row, row < 10)
@@ -403,6 +424,8 @@
                     def move(ref, index, k):
                         if kx < len(x_rounds) and ky < len(y_rounds):
                             values = corners[kx][ky, ring_x - 1, pl.ds(k, 1), :]
+                            if name_x == "B" or lax.axis_size("gx") % 2:
+                                values = jnp.where(linked("gx", name_x), values, 0.0)
                         else:
                             values = jnp.zeros((1, 128), F32)
                         ref[index, pl.ds(spot, 1), :] = values

time: 21.7 us -> 19.8 us (0.912)
  starting transfers between devices: 8.74 us -> 6.54 us
  waiting for transfers between devices: 6.18 us -> 6.49 us
    ppermute x4, starting transfers between devices: 3.85 us -> 1.88 us  [swap(): return lax.ppermute(values, names, pairs)]
    ppermute x4, waiting for transfers between devices: 5.02 us -> 5.33 us  [swap(): return lax.ppermute(values, names, pairs)]
    ppermute x3, starting transfers between devices: 4.89 us -> 4.66 us  [body(): pieces.append(lax.ppermute(sent[m - 1], 'ev', pairs))]
  transfers between devices with their start and end apart: 7 -> 7, of which waited for: 5 -> 5; matrix products, arithmetic and copies ran while one was open for 0% -> 0% of each run, Pallas kernels for 11% -> 12%
where the time goes in v3:
time: 19.8 us; the launch traced here: 19.7 us
  starting transfers between devices  6.54 us (33%)
  waiting for transfers between devices  6.49 us (33%)
  Pallas kernels  5.85 us (30%)
  between operations  0.75 us (4%)
    ppermute x4, waiting for transfers between devices, swap(): return lax.ppermute(values, names, pairs)  5.33 us
    ppermute x3, starting transfers between devices, body(): pieces.append(lax.ppermute(sent[m - 1], 'ev', pairs))  4.66 us
    pallas_call x1, Pallas kernels, body(): call(functools.partial(pack_kernel, events, x_rounds, y_rounds), [((4 * f...  2.17 us
    ppermute x4, starting transfers between devices, swap(): return lax.ppermute(values, names, pairs)  1.88 us
    ppermute x3, waiting for transfers between devices, body(): pieces.append(lax.ppermute(sent[m - 1], 'ev', pairs))  1.16 us
    pallas_call x1, Pallas kernels, body(): call(functools.partial(inner_kernel, events, x_rounds, y_rounds), [wide,...  1.01 us
    pallas_call x1, Pallas kernels, body(): call(functools.partial(second_kernel, events), [own, own], [pltpu.VMEM] *...  0.96 us
    pallas_call x1, Pallas kernels, body(): call(functools.partial(finish_kernel, shares, 1.0 / (events * shares)), [...  0.7 us
  transfers between devices with their start and end apart: 7, of which 5 were waited for; matrix products, arithmetic and copies ran while one was open for 0% of the time, Pallas kernels for 12%

profile of v3, /device:TPU:21, one launch (start us, length us, event | category | flops | bytes accessed | tf_op | source)
XLA Modules:
  0.0 19.7 jit_solution(9355823158903637401)
XLA Ops:
  0.6 0.0 copy-start.2
  0.6 0.0 copy-start.3
  0.7 0.0 copy-start.1
  0.7 0.0 copy-start.5
  0.7 0.0 copy-start.4
  0.7 0.0 copy-start
  0.7 2.2 %pack.1 = (bf16[28,16,128]{2,1,0:T(8,128)(2,1)}, bf16[28,16,128]{2,1,0:T(8,128)(2,1)}, bf16[28,16,128]{2,1,0:T(8,128)(2,1)}) custom-call(f32[6,64,128]{2,1,0:T(8,128)} %bitcast.16, f32[6,64,128]{2,1,0:T(8,128)} %bitcast.20, bf16[24,8,8,128]{3,2,1,0:T(8,128)(2,1)} %bitcast.8, f32[4,64,128]{2,1,0:T(8,128)} %bitcast.11, s32[1,1,128]{2,1,0:T(1,128)} %refs_4_.1, ...), custom_call_target="tpu_custom_call" | custom-call | flops 1024000 | bytes 1024000 | tf_op jit(solution)/shard_map/pack/pallas_call | solution.py:577
  2.9 1.4 %collective-permute-start.1 = (bf16[28,16,128]{2,1,0:T(8,128)(2,1)}, bf16[28,16,128]{2,1,0:T(8,128)(2,1)S(1)}, u32[]{:S(2)}, u32[]{:S(2)}) collective-permute-start(bf16[28,16,128]{2,1,0:T(8,128)(2,1)} %get-tuple-element.28), channel_id=1, source_target_pairs={{0,1},{1,0},{2,3},{3,2},{4,5},{5,4},{6,7},{7,6},{8,9},{9,8},{10,11... | collective-permute-start | bytes 344072 | tf_op jit(solution)/shard_map/ppermute | solution.py:37
  4.2 0.0 collective-permute-start.2
  4.2 0.2 %collective-permute-start = (bf16[28,16,128]{2,1,0:T(8,128)(2,1)}, bf16[28,16,128]{2,1,0:T(8,128)(2,1)S(1)}, u32[]{:S(2)}, u32[]{:S(2)}) collective-permute-start(bf16[28,16,128]{2,1,0:T(8,128)(2,1)} %get-tuple-element.27), channel_id=1, source_target_pairs={{0,4},{1,5},{2,6},{3,7},{4,0},{5,1},{6,2},{7,3},{8,12},{9,13},{10,... | collective-permute-start | bytes 344072 | tf_op jit(solution)/shard_map/ppermute | solution.py:37
  4.5 2.7 %collective-permute-done.1.refs_1_.refs_0_ = bf16[28,16,128]{2,1,0:T(8,128)(2,1)S(1)} collective-permute-done((bf16[28,16,128]{2,1,0:T(8,128)(2,1)}, bf16[28,16,128]{2,1,0:T(8,128)(2,1)S(1)}, u32[]{:S(2)}, u32[]{:S(2)}) %collective-permute-start.1) | collective-permute-done | bytes 114720 | tf_op jit(solution)/shard_map/ppermute | solution.py:37
  7.2 1.2 %collective-permute-done.2.refs_2_.refs_1_ = bf16[28,16,128]{2,1,0:T(8,128)(2,1)S(1)} collective-permute-done((bf16[28,16,128]{2,1,0:T(8,128)(2,1)}, bf16[28,16,128]{2,1,0:T(8,128)(2,1)S(1)}, u32[]{:S(2)}, u32[]{:S(2)}) %collective-permute-start.2) | collective-permute-done | bytes 114720 | tf_op jit(solution)/shard_map/ppermute | solution.py:37
  8.3 0.1 corners.1
  8.4 0.3 %collective-permute-start.3 = (f32[2,2,32,128]{3,2,1,0:T(8,128)S(1)}, f32[2,2,32,128]{3,2,1,0:T(8,128)S(1)}, u32[]{:S(2)}, u32[]{:S(2)}) collective-permute-start(f32[2,2,32,128]{3,2,1,0:T(8,128)S(1)} %corners.1), channel_id=1, source_target_pairs={{0,4},{1,5},{2,6},{3,7},{4,0},{5,1},{6,2},{7,3},{8,12},{9,13},{10,... | collective-permute-start | bytes 196616 | tf_op jit(solution)/shard_map/ppermute | solution.py:37
  8.7 0.0 copy-done.2
  8.7 0.0 copy-done.3
  8.7 0.0 copy-done.1
  8.7 0.0 copy-done.5
  8.7 0.0 copy-done.4
  8.7 0.3 %own.1 = (f32[6,64,128]{2,1,0:T(8,128)S(1)}, f32[6,64,128]{2,1,0:T(8,128)S(1)}) custom-call(f32[6,64,128]{2,1,0:T(8,128)S(1)} %bitcast.17, f32[6,64,128]{2,1,0:T(8,128)S(1)} %bitcast.21, f32[4,64,128]{2,1,0:T(8,128)S(1)} %bitcast.12, s32[1,1,128]{2,1,0:T(1,128)S(1)} %copy-done.5, f32[2,2,3,1,1,128]{5,4,3,2,1,0:T(1,128)S(1)} %copy-done.4), custom_call_target="tpu_custom_call" | custom-call | flops 1024000 | bytes 1024000 | tf_op jit(solution)/shard_map/own/pallas_call | solution.py:597
  9.0 0.0 collective-permute-done.refs_0_
  9.0 1.0 %inner.1 = (f32[6,192,128]{2,1,0:T(8,128)S(1)}, f32[6,192,128]{2,1,0:T(8,128)S(1)}, f32[12,192,128]{2,1,0:T(8,128)S(1)}, f32[4,192,128]{2,1,0:T(8,128)S(1)}, f32...) custom-call(f32[6,64,128]{2,1,0:T(8,128)S(1)} %bitcast.18, ...), custom_call_target="tpu_custom_call" | custom-call | flops 3072000 | bytes 3072000 | tf_op jit(solution)/shard_map/inner/pallas_call | solution.py:615
  10.1 1.5 %collective-permute-done.3.refs_0_ = f32[2,2,32,128]{3,2,1,0:T(8,128)S(1)} collective-permute-done((f32[2,2,32,128]{3,2,1,0:T(8,128)S(1)}, f32[2,2,32,128]{3,2,1,0:T(8,128)S(1)}, u32[]{:S(2)}, u32[]{:S(2)}) %collective-permute-start.3) | collective-permute-done | bytes 65568 | tf_op jit(solution)/shard_map/ppermute | solution.py:37
  11.5 0.6 %edges.1 = (f32[6,64,128]{2,1,0:T(8,128)S(1)}, f32[32,128]{1,0:T(8,128)S(1)}, f32[32,128]{1,0:T(8,128)S(1)}, f32[32,128]{1,0:T(8,128)S(1)}, f32[32,128]{1,0:T(8,128)S(1)}) custom-call(f32[2,2,32,128]{3,2,1,0:T(8,128)S(1)} %collective-permute-done.3.refs_0_, f32[6,192,128]{2,1,0:T(8,128)S(1)} %get-tuple-element.33.refs_1_, ...), custom_call_target="tpu_custom_call" | custom-call | flops 1024000 | bytes 1024000 | tf_op jit(solution)/shard_map/edges/pallas_call | solution.py:634
  12.2 4.2 %collective-permute-start.4 = (f32[32,128]{1,0:T(8,128)S(1)}, f32[32,128]{1,0:T(8,128)S(1)}, u32[]{:S(2)}, u32[]{:S(2)}) collective-permute-start(f32[32,128]{1,0:T(8,128)S(1)} %get-tuple-element.41), channel_id=1, source_target_pairs={{0,24},{8,16},{16,8},{24,0},{1,25},{9,17},{17,9},{25,1},{2,26},{10... | collective-permute-start | bytes 49160 | tf_op jit(solution)/shard_map/ppermute | solution.py:650
  16.4 0.3 %collective-permute-start.5 = (f32[32,128]{1,0:T(8,128)S(1)}, f32[32,128]{1,0:T(8,128)S(1)}, u32[]{:S(2)}, u32[]{:S(2)}) collective-permute-start(f32[32,128]{1,0:T(8,128)S(1)} %get-tuple-element.42), channel_id=1, source_target_pairs={{0,16},{8,24},{16,0},{24,8},{1,17},{9,25},{17,1},{25,9},{2,18},{10... | collective-permute-start | bytes 49160 | tf_op jit(solution)/shard_map/ppermute | solution.py:650
  16.6 0.2 %collective-permute-start.6 = (f32[32,128]{1,0:T(8,128)S(1)}, f32[32,128]{1,0:T(8,128)S(1)}, u32[]{:S(2)}, u32[]{:S(2)}) collective-permute-start(f32[32,128]{1,0:T(8,128)S(1)} %get-tuple-element.43), channel_id=1, source_target_pairs={{0,8},{8,0},{16,24},{24,16},{1,9},{9,1},{17,25},{25,17},{2,10},{10... | collective-permute-start | bytes 49160 | tf_op jit(solution)/shard_map/ppermute | solution.py:650
  16.8 1.0 %second.1 = (f32[6,64,128]{2,1,0:T(8,128)}, f32[6,64,128]{2,1,0:T(8,128)}) custom-call(f32[6,64,128]{2,1,0:T(8,128)S(1)} %bitcast.19, f32[6,64,128]{2,1,0:T(8,128)S(1)} %get-tuple-element.25.extra, f32[4,64,128]{2,1,0:T(8,128)S(1)} %bitcast.15, f32[4,192,128]{2,1,0:T(8,128)S(1)} %get-tuple-element.30.refs_4_.medium, ...), custom_call_target="tpu_custom_call" | custom-call | flops 1024000 | bytes 1024000 | tf_op jit(solution)/shard_map/second/pallas_call | solution.py:651
  17.8 0.4 %collective-permute-done.4.refs_1_ = f32[32,128]{1,0:T(8,128)S(1)} collective-permute-done((f32[32,128]{1,0:T(8,128)S(1)}, f32[32,128]{1,0:T(8,128)S(1)}, u32[]{:S(2)}, u32[]{:S(2)}) %collective-permute-start.4) | collective-permute-done | bytes 16416 | tf_op jit(solution)/shard_map/ppermute | solution.py:650
  18.2 0.8 %collective-permute-done.5.refs_2_ = f32[32,128]{1,0:T(8,128)S(1)} collective-permute-done((f32[32,128]{1,0:T(8,128)S(1)}, f32[32,128]{1,0:T(8,128)S(1)}, u32[]{:S(2)}, u32[]{:S(2)}) %collective-permute-start.5) | collective-permute-done | bytes 16416 | tf_op jit(solution)/shard_map/ppermute | solution.py:650
  18.9 0.0 collective-permute-done.6.refs_3_
  19.0 0.7 %finish.1 = (f32[64,32]{1,0:T(8,128)}, f32[64,32]{1,0:T(8,128)}) custom-call(f32[32,128]{1,0:T(8,128)S(1)} %get-tuple-element.40.refs_0_, f32[32,128]{1,0:T(8,128)S(1)} %collective-permute-done.4.refs_1_, f32[32,128]{1,0:T(8,128)S(1)} %collective-permute-done.5.refs_2_, f32[32,128]{1,0:T(8,128)S(1)} %collective-permute-done.6.refs_3_), custom_call_target="tpu_custom_call" | custom-call | flops 1024000 | bytes 1024000 | tf_op jit(solution)/shard_map/finish/pallas_call | solution.py:657
  (1 shorter events, 0.0 us)
Async XLA Ops:
  0.6 8.0 %copy-start.2 = (f32[2,3,8,8,128]{4,3,2,1,0:T(8,128)S(1)}, f32[2,3,8,8,128]{4,3,2,1,0:T(8,128)}, u32[]{:S(2)}) copy-start(f32[2,3,8,8,128]{4,3,2,1,0:T(8,128)} %param.6) | copy-start | bytes 589828
  0.6 8.0 %copy-start.3 = (f32[2,3,8,8,128]{4,3,2,1,0:T(8,128)S(1)}, f32[2,3,8,8,128]{4,3,2,1,0:T(8,128)}, u32[]{:S(2)}) copy-start(f32[2,3,8,8,128]{4,3,2,1,0:T(8,128)} %param.7) | copy-start | bytes 589828
  0.7 8.0 %copy-start.1 = (f32[4,8,8,128]{3,2,1,0:T(8,128)S(1)}, f32[4,8,8,128]{3,2,1,0:T(8,128)}, u32[]{:S(2)}) copy-start(f32[4,8,8,128]{3,2,1,0:T(8,128)} %param.9) | copy-start | bytes 393220
  0.7 8.0 %copy-start.5 = (s32[1,1,128]{2,1,0:T(1,128)S(1)}, s32[1,1,128]{2,1,0:T(1,128)}, u32[]{:S(2)}) copy-start(s32[1,1,128]{2,1,0:T(1,128)} %refs_4_.1) | copy-start | bytes 1540
  0.7 8.0 %copy-start.4 = (f32[2,2,3,1,1,128]{5,4,3,2,1,0:T(1,128)S(1)}, f32[2,2,3,1,1,128]{5,4,3,2,1,0:T(1,128)}, u32[]{:S(2)}) copy-start(f32[2,2,3,1,1,128]{5,4,3,2,1,0:T(1,128)} %refs_5_.1) | copy-start | bytes 18436
  0.7 8.4 %copy-start = (bf16[2,4,3,8,8,128]{5,4,3,2,1,0:T(8,128)(2,1)S(1)}, bf16[2,4,3,8,8,128]{5,4,3,2,1,0:T(8,128)(2,1)}, u32[]{:S(2)}) copy-start(bf16[2,4,3,8,8,128]{5,4,3,2,1,0:T(8,128)(2,1)} %param.8) | copy-start | bytes 1179652
  2.9 4.3 %collective-permute-start.1 = (bf16[28,16,128]{2,1,0:T(8,128)(2,1)}, bf16[28,16,128]{2,1,0:T(8,128)(2,1)S(1)}, u32[]{:S(2)}, u32[]{:S(2)}) collective-permute-start(bf16[28,16,128]{2,1,0:T(8,128)(2,1)} %get-tuple-element.28), channel_id=1, source_target_pairs={{0,1},{1,0},{2,3},{3,2},{4,5},{5,4},{6,7},{7,6},{8,9},{9,8},{10,11... | collective-permute-start | bytes 344072 | tf_op jit(solution)/shard_map/ppermute | solution.py:37
  4.2 4.1 %collective-permute-start.2 = (bf16[28,16,128]{2,1,0:T(8,128)(2,1)}, bf16[28,16,128]{2,1,0:T(8,128)(2,1)S(1)}, u32[]{:S(2)}, u32[]{:S(2)}) collective-permute-start(bf16[28,16,128]{2,1,0:T(8,128)(2,1)} %get-tuple-element.29), channel_id=1, source_target_pairs={{0,8},{1,2},{2,1},{3,11},{4,12},{5,6},{6,5},{7,15},{8,0},{9,10},{1... | collective-permute-start | bytes 344072 | tf_op jit(solution)/shard_map/ppermute | solution.py:37
  4.2 4.8 %collective-permute-start = (bf16[28,16,128]{2,1,0:T(8,128)(2,1)}, bf16[28,16,128]{2,1,0:T(8,128)(2,1)S(1)}, u32[]{:S(2)}, u32[]{:S(2)}) collective-permute-start(bf16[28,16,128]{2,1,0:T(8,128)(2,1)} %get-tuple-element.27), channel_id=1, source_target_pairs={{0,4},{1,5},{2,6},{3,7},{4,0},{5,1},{6,2},{7,3},{8,12},{9,13},{10,... | collective-permute-start | bytes 344072 | tf_op jit(solution)/shard_map/ppermute | solution.py:37
  8.4 3.2 %collective-permute-start.3 = (f32[2,2,32,128]{3,2,1,0:T(8,128)S(1)}, f32[2,2,32,128]{3,2,1,0:T(8,128)S(1)}, u32[]{:S(2)}, u32[]{:S(2)}) collective-permute-start(f32[2,2,32,128]{3,2,1,0:T(8,128)S(1)} %corners.1), channel_id=1, source_target_pairs={{0,4},{1,5},{2,6},{3,7},{4,0},{5,1},{6,2},{7,3},{8,12},{9,13},{10,... | collective-permute-start | bytes 196616 | tf_op jit(solution)/shard_map/ppermute | solution.py:37
  12.2 6.0 %collective-permute-start.4 = (f32[32,128]{1,0:T(8,128)S(1)}, f32[32,128]{1,0:T(8,128)S(1)}, u32[]{:S(2)}, u32[]{:S(2)}) collective-permute-start(f32[32,128]{1,0:T(8,128)S(1)} %get-tuple-element.41), channel_id=1, source_target_pairs={{0,24},{8,16},{16,8},{24,0},{1,25},{9,17},{17,9},{25,1},{2,26},{10... | collective-permute-start | bytes 49160 | tf_op jit(solution)/shard_map/ppermute | solution.py:650
  16.4 2.6 %collective-permute-start.5 = (f32[32,128]{1,0:T(8,128)S(1)}, f32[32,128]{1,0:T(8,128)S(1)}, u32[]{:S(2)}, u32[]{:S(2)}) collective-permute-start(f32[32,128]{1,0:T(8,128)S(1)} %get-tuple-element.42), channel_id=1, source_target_pairs={{0,16},{8,24},{16,0},{24,8},{1,17},{9,25},{17,1},{25,9},{2,18},{10... | collective-permute-start | bytes 49160 | tf_op jit(solution)/shard_map/ppermute | solution.py:650
  16.6 2.3 %collective-permute-start.6 = (f32[32,128]{1,0:T(8,128)S(1)}, f32[32,128]{1,0:T(8,128)S(1)}, u32[]{:S(2)}, u32[]{:S(2)}) collective-permute-start(f32[32,128]{1,0:T(8,128)S(1)} %get-tuple-element.43), channel_id=1, source_target_pairs={{0,8},{8,0},{16,24},{24,16},{1,9},{9,1},{17,25},{25,17},{2,10},{10... | collective-permute-start | bytes 49160 | tf_op jit(solution)/shard_map/ppermute | solution.py:650

commit v4 on v3

--- a/solution.py
+++ b/solution.py
@@ -12,7 +12,6 @@
 F32, BF16 = jnp.float32, jnp.bfloat16
 SHEAR, LAME, BUOY, INV = range(4)
 ROWS = 16
-FULL = pl.BlockSpec(memory_space=pltpu.VMEM)
 VMEM_LIMIT = 40 * 1024 * 1024
 PACK_LIMIT = 60 * 1024 * 1024
 
@@ -21,16 +20,16 @@
     return "AB"[: max(0, min(2, count - 1))]
 
 
-def swap(values, axis, name):
+def swap(values, rounds):
     names = ("ev", "gx", "gy")
     sizes = [lax.axis_size(a) for a in names]
-    along = names.index(axis)
     pairs = []
     for source in itertools.product(*map(range, sizes)):
         target = list(source)
-        up = (source[along] % 2 == 0) == (name == "A")
-        target[along] += 1 if up else -1
-        if not 0 <= target[along] < sizes[along]:
+        for axis, name in rounds.items():
+            along = names.index(axis)
+            target[along] += 1 if (source[along] % 2 == 0) == (name == "A") else -1
+        if not all(0 <= t < size for t, size in zip(target, sizes)):
             target = [source[0] ^ 1, *source[1:]]
         flat = [(s[0] * sizes[1] + s[1]) * sizes[2] + s[2] for s in (source, target)]
         pairs.append(tuple(flat))
@@ -77,10 +76,10 @@
 
 def pack_kernel(events, x_rounds, y_rounds, *refs):
     fields = 3 * events
-    count = 6
-    sources = refs[:count]
-    messages = refs[count : count + len(x_rounds) + len(y_rounds)]
-    now, prev, fwd, med, cells, force, base, stored, arrived = refs[count + len(messages) :]
+    total = len(x_rounds) + len(y_rounds) + len(x_rounds) * len(y_rounds)
+    sources, targets, refs = refs[:6], refs[6 : 6 + total], refs[6 + total :]
+    now, prev, fwd, med, cells, force, base, stored, arrived, left = refs[:10]
+    messages = refs[10:]
     now_in, prev_in, fwd_in, med_in, cells_in, force_in = sources
     pairs = [(cells_in, cells), (force_in, force), (now_in, now), (prev_in, prev), (med_in, med)]
     for e in range(events):
@@ -97,13 +96,14 @@
     pushed = force_field(cells[0], rows, 64)
     for copy in copies[2:]:
         copy.wait()
+    scale = STEP_FACTOR * med[pl.ds(BUOY * 64, 64), :]
     for f in range(fields):
-        base[f] = (
-            2.0 * now[f] - prev[f] + STEP_FACTOR * med[BUOY] * pushed[f * 64 : (f + 1) * 64]
-        )
+        spot = pl.ds(f * 64, 64)
+        base[spot, :] = 2.0 * now[spot, :] - prev[spot, :] + scale * pushed[f * 64 : (f + 1) * 64]
         e, c = f // 3, f % 3
         for t in range(2):
-            stored[f * 2 + t] = fwd[(e * 2 + t) * 3 + c].astype(F32).reshape(64, 128)
+            part = fwd[(e * 2 + t) * 3 + c].astype(F32).reshape(64, 128)
+            stored[pl.ds((f * 2 + t) * 64, 64), :] = part
 
     def fill(message, pick):
         for f in range(fields):
@@ -120,22 +120,45 @@
         edge = pick(med, BUOY, 1)
         message[4 * fields + 3] = jnp.concatenate([edge, edge], axis=0).astype(BF16)
 
-    for k, name in enumerate(x_rounds):
-        up = upward("gx", name)
-
-        def pick_x(ref, index, ring, up=up):
-            row = jnp.where(up, 8 - ring, ring - 1)
-            return ref[index, pl.ds(pl.multiple_of(row * 8, 8), 8), :]
-
-        fill(messages[k], pick_x)
-    for k, name in enumerate(y_rounds):
-        up = upward("gy", name)
-
-        def pick_y(ref, index, ring, up=up):
-            row = jnp.where(up, 8 - ring, ring - 1)
-            return ref[index, pl.ds(row, 8, stride=8), :]
-
-        fill(messages[len(x_rounds) + k], pick_y)
+    def face(axis, name, ring):
+        return jnp.where(upward(axis, name), 8 - ring, ring - 1)
+
+    out = []
+
+    def send():
+        k = len(out)
+        out.append(pltpu.make_async_copy(messages[k], targets[k], left.at[k]))
+        out[k].start()
+
+    for name in y_rounds:
+
+        def pick_y(ref, index, ring, name=name):
+            return ref[pl.ds(index * 64 + face("gy", name, ring), 8, stride=8), :]
+
+        fill(messages[len(out)], pick_y)
+        send()
+    for name in x_rounds:
+
+        def pick_x(ref, index, ring, name=name):
+            row = pl.multiple_of(face("gx", name, ring) * 8, 8)
+            return ref[pl.ds(index * 64 + row, 8), :]
+
+        fill(messages[len(out)], pick_x)
+        send()
+    for name_x in x_rounds:
+        for name_y in y_rounds:
+            message = messages[len(out)]
+            for ring_x in (1, 2):
+                for ring_y in (1, 2):
+                    cell = face("gx", name_x, ring_x) * 8 + face("gy", name_y, ring_y)
+                    target = message.at[ring_x - 1, ring_y - 1]
+                    target[pl.ds(0, fields), :] = now[pl.ds(cell, fields, stride=64), :]
+                    target[pl.ds(fields, 4), :] = med[pl.ds(cell, 4, stride=64), :]
+                    picked = base[pl.ds(cell, fields, stride=64), :]
+                    target[pl.ds(fields + 4, fields), :] = picked
+            send()
+    for copy in out:
+        copy.wait()
 
 
 def masked(message, axis, name):
@@ -143,29 +166,6 @@
         return lambda index: message[index]
     real = linked(axis, name)
     return lambda index: jnp.where(real, message[index].astype(F32), 0.0).astype(BF16)
-
-
-def corner_kernel(fields, x_rounds, y_rounds, *refs):
-    sides = refs[: len(y_rounds)]
-    outs = refs[len(y_rounds) : len(y_rounds) + len(x_rounds)]
-    rows = refs[-1]
-    for s, name in enumerate(y_rounds):
-        side = masked(sides[s], "gy", name)
-        for k in range(3 * fields):
-            rows[s, pl.ds(k * 8, 8), :] = join(side(k))
-        for k in range(3):
-            tile = side(4 * fields + k).astype(F32)
-            rows[s, pl.ds((3 * fields + 2 * k) * 8, 16), :] = tile
-        tile = side(4 * fields + 3).astype(F32)
-        rows[s, pl.ds((3 * fields + 6) * 8, 16), :] = tile
-        for k in range(3 * fields + 8, 32):
-            rows[s, pl.ds(k * 8, 8), :] = jnp.zeros((8, 128), F32)
-    for k, name in enumerate(x_rounds):
-        up = upward("gx", name)
-        for s in range(len(y_rounds)):
-            for ring in (1, 2):
-                row = jnp.where(up, 8 - ring, ring - 1)
-                outs[k][s, ring - 1] = rows[s, pl.ds(row, 32, stride=8), :]
 
 
 def shift_z(values, step):
@@ -282,7 +282,8 @@
     return ref[index, pl.ds((row - 2) * 8, 8), :]
 
 
-def own_kernel(events, now, prev, med, cells, force, base, extra):
+def own_kernel(events, now, prev, med, cells, force, *refs):
+    base, extra = refs[-2:]
     fields = 3 * events
     rows = [force[e, s, c, 0] for s in range(2) for e in range(events) for c in range(3)]
     pushed = force_field(cells[0], rows, 64)
@@ -400,49 +401,49 @@
 
 def edge_kernel(events, x_rounds, y_rounds, shares, *refs):
     fields = 3 * events
-    corners, refs = refs[: len(x_rounds)], refs[len(x_rounds) :]
+    count = len(x_rounds) * len(y_rounds)
+    corners, refs = refs[:count], refs[count:]
     (here, start, stored, medium, coef, then, part, fwd, med), refs = refs[:9], refs[9:]
     edge, own_share, *sent = refs[: 1 + shares]
     outer, outer_start, outer_medium, outer_coef, slabs = refs[1 + shares :]
 
+    height = len(OUTER) * ROWS
     for k, row in enumerate(OUTER):
-        spot = pl.ds(k * ROWS, ROWS)
         for f in range(fields):
-            outer[f, spot, :] = row_of(here, f, row)
+            spot = pl.ds(f * height + k * ROWS, ROWS)
+            outer[spot, :] = row_of(here, f, row)
             if row in EDGES:
-                outer_start[f, spot, :] = row_of(start, f, row)
+                outer_start[spot, :] = row_of(start, f, row)
         for m in range(4):
-            outer_medium[m, spot, :] = row_of(medium, m, row)
+            outer_medium[pl.ds(m * height + k * ROWS, ROWS), :] = row_of(medium, m, row)
     for kx, name_x in enumerate("AB"):
         for ky, name_y in enumerate("AB"):
+            corner = None
+            if kx < len(x_rounds) and ky < len(y_rounds):
+                corner = corners[kx * len(y_rounds) + ky]
             up_x, up_y = upward("gx", name_x), upward("gy", name_y)
+            real = jnp.logical_and(linked("gx", name_x), linked("gy", name_y))
             for ring_x in (1, 2):
                 for ring_y in (1, 2):
                     place = jnp.where(up_x, 1 + ring_x, 2 - ring_x)
                     spot = place * ROWS + y_place(up_y, ring_y)
 
-                    def move(ref, index, k):
-                        if kx < len(x_rounds) and ky < len(y_rounds):
-                            values = corners[kx][ky, ring_x - 1, pl.ds(k, 1), :]
-                            if name_x == "B" or lax.axis_size("gx") % 2:
-                                values = jnp.where(linked("gx", name_x), values, 0.0)
-                        else:
-                            values = jnp.zeros((1, 128), F32)
-                        ref[index, pl.ds(spot, 1), :] = values
-
-                    for f in range(fields):
-                        move(outer, f, 2 * f + ring_y - 1)
-                        if ring_x == 1 and ring_y == 1:
-                            move(outer_start, f, 2 * fields + f)
-                    for k, m in enumerate((SHEAR, LAME, INV)):
-                        move(outer_medium, m, 3 * fields + 2 * k + ring_y - 1)
+                    def put(ref, first, count):
+                        values = jnp.zeros((count, 128), F32)
+                        if corner is not None:
+                            values = corner[ring_x - 1, ring_y - 1, pl.ds(first, count), :]
+                            values = jnp.where(real, values, 0.0)
+                        ref[pl.ds(spot, count, stride=height), :] = values
+
+                    put(outer, 0, fields)
+                    put(outer_medium, fields, 4)
                     if ring_x == 1 and ring_y == 1:
-                        move(outer_medium, BUOY, 3 * fields + 6)
+                        put(outer_start, fields + 4, fields)
 
     def outer_or(ref, full):
         def pick(index, row):
             if row in OUTER:
-                return row_of(ref, index, OUTER.index(row))
+                return ref[pl.ds(index * height + OUTER.index(row) * ROWS, ROWS), :]
             return row_of(full, index, row)
 
         return pick
@@ -547,11 +548,14 @@
         out[pl.ds((v % 8) * 8, 8), :] = tile[:, :width] * scale
 
 
-def call(kernel, outs, ins, scratch=(), name=None, limit=VMEM_LIMIT, cost=1000):
+def call(
+    kernel, outs, ins, scratch=(), name=None, limit=VMEM_LIMIT, cost=1000, out_memory=pltpu.VMEM
+):
     return pl.pallas_call(
         kernel,
         out_shape=[jax.ShapeDtypeStruct(s, d) for s, d in outs],
         in_specs=[pl.BlockSpec(memory_space=m) for m in ins],
+        out_specs=[pl.BlockSpec(memory_space=out_memory)] * len(outs),
         scratch_shapes=[s if not isinstance(s, tuple) else pltpu.VMEM(*s) for s in scratch],
         compiler_params=pltpu.CompilerParams(vmem_limit_bytes=limit),
         cost_estimate=pl.CostEstimate(
@@ -574,42 +578,53 @@
     own = ((fields, tile, depth), F32)
     tall = 12 * ROWS
 
+    face = ((4 * fields + 4, 16, depth), BF16)
+    corner = ((2, 2, 2 * fields + 4, depth), F32)
+    shapes = [face] * (len(y_rounds) + len(x_rounds)) + [corner] * (len(x_rounds) * len(y_rounds))
+    flat = ((fields * tile, depth), F32)
     messages = call(
         functools.partial(pack_kernel, events, x_rounds, y_rounds),
-        [((4 * fields + 4, 16, depth), BF16)] * (len(x_rounds) + len(y_rounds)),
+        shapes,
         [pltpu.HBM] * 6,
         [
-            own,
-            own,
+            flat,
+            flat,
             ((2 * fields, width_x, width_y, depth), BF16),
-            ((4, tile, depth), F32),
+            ((4 * tile, depth), F32),
             (drm_cells.shape, drm_cells.dtype),
             (drm_force.shape, F32),
-            own,
-            ((2 * fields, tile, depth), F32),
+            flat,
+            ((2 * fields * tile, depth), F32),
             pltpu.SemaphoreType.DMA((5 + events,)),
+            pltpu.SemaphoreType.DMA((len(shapes),)),
+            *shapes,
         ],
         "pack",
         PACK_LIMIT,
-    )(now, prev, fwd, med, drm_cells, drm_force)
-    y_messages = [swap(m, "gy", r) for m, r in zip(messages[len(x_rounds) :], y_rounds)]
-    x_messages = [swap(m, "gx", r) for m, r in zip(messages, x_rounds)]
+        cost=8000,
+        out_memory=pltpu.HBM,
+    )(now.reshape(-1, depth), prev.reshape(-1, depth), fwd, med.reshape(-1, depth), drm_cells, drm_force)
+    kinds = [{"gy": r} for r in y_rounds] + [{"gx": r} for r in x_rounds]
+    kinds += [{"gx": x, "gy": y} for x in x_rounds for y in y_rounds]
+    received = [swap(message, kind) for message, kind in zip(messages, kinds)]
+    y_messages, rest = received[: len(y_rounds)], received[len(y_rounds) :]
+    x_messages, corners = rest[: len(x_rounds)], rest[len(x_rounds) :]
+    arrival = ()
+    if y_messages:
+        arrival = call(
+            lambda *refs: None,
+            [((8, depth), F32)],
+            [pl.ANY] * len(y_messages),
+            name="arrival",
+            out_memory=pl.ANY,
+            cost=8000,
+        )(*y_messages)
     base, extra = call(
         functools.partial(own_kernel, events),
         [own, own],
-        [pltpu.VMEM] * 5,
+        [pltpu.VMEM] * 5 + [pl.ANY] * len(arrival),
         name="own",
-    )(now, prev, med, drm_cells, drm_force)
-    corners = []
-    if x_rounds and y_rounds:
-        corners = call(
-            functools.partial(corner_kernel, fields, x_rounds, y_rounds),
-            [((len(y_rounds), 2, 32, depth), F32)] * len(x_rounds),
-            [pltpu.VMEM] * len(y_rounds),
-            [((len(y_rounds), 32 * 8, depth), F32)],
-            "corners",
-        )(*y_messages)
-        corners = [swap(m, "gx", r) for m, r in zip(corners, x_rounds)]
+    )(now, prev, med, drm_cells, drm_force, *arrival)
 
     wide = ((fields, tall, depth), F32)
     here, start, stored, tall_medium, coef, then, part = call(
@@ -629,16 +644,14 @@
     )(now, base, fwd, med, *x_messages, *y_messages)
     slab = ((16 // shares * 8, depth), F32)
     outer = ((fields, len(OUTER) * ROWS, depth), F32)
-    if not corners:
-        corners = [jnp.zeros((2, 2, 32, depth), F32)] * len(x_rounds)
     edge, own_share, *sent = call(
         functools.partial(edge_kernel, events, x_rounds, y_rounds, shares),
         [outer] + [slab] * shares,
         [pltpu.VMEM] * (9 + len(corners)),
         [
-            outer,
-            outer,
-            ((4, len(OUTER) * ROWS, depth), F32),
+            ((fields * len(OUTER) * ROWS, depth), F32),
+            ((fields * len(OUTER) * ROWS, depth), F32),
+            ((4 * len(OUTER) * ROWS, depth), F32),
             ((len(COEFFICIENTS), 5 * ROWS, depth), F32),
             ((shares,) + slab[0], F32),
         ],

time: 19.8 us -> 19.2 us (0.970)
  the two profiles are of different devices: /device:TPU:21 before, /device:TPU:9 now
where the time goes in v4:
time: 19.2 us; the launch traced here: 18.8 us
  starting transfers between devices  10.1 us (53%)
  Pallas kernels  5.86 us (31%)
  waiting for transfers between devices  2.05 us (11%)
  between operations  0.76 us (4%)
    ppermute x5, starting transfers between devices, swap(): return lax.ppermute(values, names, pairs)  5.91 us
    ppermute x3, starting transfers between devices, body(): pieces.append(lax.ppermute(sent[m - 1], 'ev', pairs))  4.2 us
    pallas_call x1, Pallas kernels, body(): call(functools.partial(pack_kernel, events, x_rounds, y_rounds), shapes,...  2.22 us
    ppermute x3, waiting for transfers between devices, body(): pieces.append(lax.ppermute(sent[m - 1], 'ev', pairs))  1.16 us
    pallas_call x1, Pallas kernels, body(): call(functools.partial(inner_kernel, events, x_rounds, y_rounds), [wide,...  1.01 us
    pallas_call x1, Pallas kernels, body(): call(functools.partial(second_kernel, events), [own, own], [pltpu.VMEM] *...  0.96 us
    ppermute x5, waiting for transfers between devices, swap(): return lax.ppermute(values, names, pairs)  0.89 us
    pallas_call x1, Pallas kernels, body(): call(functools.partial(finish_kernel, shares, 1.0 / (events * shares)), [...  0.7 us
  transfers between devices with their start and end apart: 8, of which 4 were waited for; matrix products, arithmetic and copies ran while one was open for 0% of the time, Pallas kernels for 12%

profile of v4, /device:TPU:9, one launch (start us, length us, event | category | flops | bytes accessed | tf_op | source)
XLA Modules:
  0.0 18.8 jit_solution(4680985409873555294)
XLA Ops:
  0.6 0.0 copy-start.4
  0.6 0.0 copy-start.5
  0.7 0.0 copy-start.2
  0.7 0.0 copy-start.3
  0.7 0.0 copy-start.1
  0.7 0.0 copy-start
  0.7 2.2 %pack.1 = (bf16[28,16,128]{2,1,0:T(8,128)(2,1)}, bf16[28,16,128]{2,1,0:T(8,128)(2,1)}, bf16[28,16,128]{2,1,0:T(8,128)(2,1)}, f32[2,2,16,128]{3,2,1,0:T(8,128)}, f32[2,2,16,128]{3,2,1,0:T(8,128)}) custom-call(f32[384,128]{1,0:T(8,128)} %bitcast.19, f32[384,128]{1,0:T(8,128)} %bitcast.23, bf16[24,8,8,128]{3,2,1,0:T(8,128)(2,1)} %bitcast.11, ...), custom_call_target="tpu_custom_call" | custom-call | flops 8192000 | bytes 8192000 | tf_op jit(solution)/shard_map/pack/pallas_call | solution.py:585
  2.9 0.1 collective-permute-start
  3.0 2.6 %collective-permute-start.1 = (bf16[28,16,128]{2,1,0:T(8,128)(2,1)}, bf16[28,16,128]{2,1,0:T(8,128)(2,1)S(1)}, u32[]{:S(2)}, u32[]{:S(2)}) collective-permute-start(bf16[28,16,128]{2,1,0:T(8,128)(2,1)} %get-tuple-element.28), channel_id=1, source_target_pairs={{0,8},{1,2},{2,1},{3,11},{4,12},{5,6},{6,5},{7,15},{8,0},{9,10},{1... | collective-permute-start | bytes 344072 | tf_op jit(solution)/shard_map/ppermute | solution.py:36
  5.6 1.2 %collective-permute-start.2 = (bf16[28,16,128]{2,1,0:T(8,128)(2,1)}, bf16[28,16,128]{2,1,0:T(8,128)(2,1)S(1)}, u32[]{:S(2)}, u32[]{:S(2)}) collective-permute-start(bf16[28,16,128]{2,1,0:T(8,128)(2,1)} %get-tuple-element.31), channel_id=1, source_target_pairs={{0,4},{1,5},{2,6},{3,7},{4,0},{5,1},{6,2},{7,3},{8,12},{9,13},{10,... | collective-permute-start | bytes 344072 | tf_op jit(solution)/shard_map/ppermute | solution.py:36
  6.8 0.0 collective-permute-start.3
  6.8 2.0 %collective-permute-start.4 = (f32[2,2,16,128]{3,2,1,0:T(8,128)}, f32[2,2,16,128]{3,2,1,0:T(8,128)S(1)}, u32[]{:S(2)}, u32[]{:S(2)}) collective-permute-start(f32[2,2,16,128]{3,2,1,0:T(8,128)} %get-tuple-element.36), channel_id=1, source_target_pairs={{0,8},{1,6},{2,5},{3,11},{4,12},{5,2},{6,1},{7,15},{8,0},{9,14},{1... | collective-permute-start | bytes 98312 | tf_op jit(solution)/shard_map/ppermute | solution.py:36
  8.8 0.0 collective-permute-done.refs_0_.refs_1_
  8.8 0.0 collective-permute-done.1.refs_1_.refs_2_
  8.8 0.0 copy-done.4
  8.9 0.0 copy-done.5
  8.9 0.0 copy-done.2
  8.9 0.0 copy-done.3
  8.9 0.3 %own.1 = (f32[6,64,128]{2,1,0:T(8,128)S(1)}, f32[6,64,128]{2,1,0:T(8,128)S(1)}) custom-call(f32[6,64,128]{2,1,0:T(8,128)S(1)} %bitcast.20, f32[6,64,128]{2,1,0:T(8,128)S(1)} %bitcast.24, f32[4,64,128]{2,1,0:T(8,128)S(1)} %bitcast.15, s32[1,1,128]{2,1,0:T(1,128)S(1)} %copy-done.5, f32[2,2,3,1,1,128]{5,4,3,2,1,0:T(1,128)S(1)} %copy-done.4, ...), custom_call_target="tpu_custom_call" | custom-call | flops 1024000 | bytes 1024000 | tf_op jit(solution)/shard_map/own/pallas_call | solution.py:622
  9.2 0.2 %collective-permute-done.2.refs_0_ = bf16[28,16,128]{2,1,0:T(8,128)(2,1)S(1)} collective-permute-done((bf16[28,16,128]{2,1,0:T(8,128)(2,1)}, bf16[28,16,128]{2,1,0:T(8,128)(2,1)S(1)}, u32[]{:S(2)}, u32[]{:S(2)}) %collective-permute-start.2) | collective-permute-done | bytes 114720 | tf_op jit(solution)/shard_map/ppermute | solution.py:36
  9.5 1.0 %inner.1 = (f32[6,192,128]{2,1,0:T(8,128)S(1)}, f32[6,192,128]{2,1,0:T(8,128)S(1)}, f32[12,192,128]{2,1,0:T(8,128)S(1)}, f32[4,192,128]{2,1,0:T(8,128)S(1)}, f32...) custom-call(f32[6,64,128]{2,1,0:T(8,128)S(1)} %bitcast.21, ...), custom_call_target="tpu_custom_call" | custom-call | flops 3072000 | bytes 3072000 | tf_op jit(solution)/shard_map/inner/pallas_call | solution.py:630
  10.5 0.6 %collective-permute-done.3.refs_0_ = f32[2,2,16,128]{3,2,1,0:T(8,128)S(1)} collective-permute-done((f32[2,2,16,128]{3,2,1,0:T(8,128)}, f32[2,2,16,128]{3,2,1,0:T(8,128)S(1)}, u32[]{:S(2)}, u32[]{:S(2)}) %collective-permute-start.3) | collective-permute-done | bytes 32800 | tf_op jit(solution)/shard_map/ppermute | solution.py:36
  11.1 0.0 collective-permute-done.4.refs_1_
  11.1 0.6 %edges.1 = (f32[6,64,128]{2,1,0:T(8,128)S(1)}, f32[32,128]{1,0:T(8,128)S(1)}, f32[32,128]{1,0:T(8,128)S(1)}, f32[32,128]{1,0:T(8,128)S(1)}, f32[32,128]{1,0:T(8,128)S(1)}) custom-call(f32[2,2,16,128]{3,2,1,0:T(8,128)S(1)} %collective-permute-done.3.refs_0_, f32[2,2,16,128]{3,2,1,0:T(8,128)S(1)} %collective-permute-done.4.refs_1_, ...), custom_call_target="tpu_custom_call" | custom-call | flops 1024000 | bytes 1024000 | tf_op jit(solution)/shard_map/edges/pallas_call | solution.py:647
  11.8 3.7 %collective-permute-start.5 = (f32[32,128]{1,0:T(8,128)S(1)}, f32[32,128]{1,0:T(8,128)S(1)}, u32[]{:S(2)}, u32[]{:S(2)}) collective-permute-start(f32[32,128]{1,0:T(8,128)S(1)} %get-tuple-element.45), channel_id=1, source_target_pairs={{0,24},{8,16},{16,8},{24,0},{1,25},{9,17},{17,9},{25,1},{2,26},{10... | collective-permute-start | bytes 49160 | tf_op jit(solution)/shard_map/ppermute | solution.py:663
  15.5 0.3 %collective-permute-start.6 = (f32[32,128]{1,0:T(8,128)S(1)}, f32[32,128]{1,0:T(8,128)S(1)}, u32[]{:S(2)}, u32[]{:S(2)}) collective-permute-start(f32[32,128]{1,0:T(8,128)S(1)} %get-tuple-element.46), channel_id=1, source_target_pairs={{0,16},{8,24},{16,0},{24,8},{1,17},{9,25},{17,1},{25,9},{2,18},{10... | collective-permute-start | bytes 49160 | tf_op jit(solution)/shard_map/ppermute | solution.py:663
  15.8 0.2 %collective-permute-start.7 = (f32[32,128]{1,0:T(8,128)S(1)}, f32[32,128]{1,0:T(8,128)S(1)}, u32[]{:S(2)}, u32[]{:S(2)}) collective-permute-start(f32[32,128]{1,0:T(8,128)S(1)} %get-tuple-element.47), channel_id=1, source_target_pairs={{0,8},{8,0},{16,24},{24,16},{1,9},{9,1},{17,25},{25,17},{2,10},{10... | collective-permute-start | bytes 49160 | tf_op jit(solution)/shard_map/ppermute | solution.py:663
  16.0 1.0 %second.1 = (f32[6,64,128]{2,1,0:T(8,128)}, f32[6,64,128]{2,1,0:T(8,128)}) custom-call(f32[6,64,128]{2,1,0:T(8,128)S(1)} %bitcast.22, f32[6,64,128]{2,1,0:T(8,128)S(1)} %get-tuple-element.29.extra, f32[4,64,128]{2,1,0:T(8,128)S(1)} %bitcast.18, f32[4,192,128]{2,1,0:T(8,128)S(1)} %get-tuple-element.32.refs_5_.medium, ...), custom_call_target="tpu_custom_call" | custom-call | flops 1024000 | bytes 1024000 | tf_op jit(solution)/shard_map/second/pallas_call | solution.py:664
  16.9 0.4 %collective-permute-done.5.refs_1_ = f32[32,128]{1,0:T(8,128)S(1)} collective-permute-done((f32[32,128]{1,0:T(8,128)S(1)}, f32[32,128]{1,0:T(8,128)S(1)}, u32[]{:S(2)}, u32[]{:S(2)}) %collective-permute-start.5) | collective-permute-done | bytes 16416 | tf_op jit(solution)/shard_map/ppermute | solution.py:663
  17.3 0.8 %collective-permute-done.6.refs_2_ = f32[32,128]{1,0:T(8,128)S(1)} collective-permute-done((f32[32,128]{1,0:T(8,128)S(1)}, f32[32,128]{1,0:T(8,128)S(1)}, u32[]{:S(2)}, u32[]{:S(2)}) %collective-permute-start.6) | collective-permute-done | bytes 16416 | tf_op jit(solution)/shard_map/ppermute | solution.py:663
  18.1 0.0 collective-permute-done.7.refs_3_
  18.1 0.7 %finish.1 = (f32[64,32]{1,0:T(8,128)}, f32[64,32]{1,0:T(8,128)}) custom-call(f32[32,128]{1,0:T(8,128)S(1)} %get-tuple-element.44.refs_0_, f32[32,128]{1,0:T(8,128)S(1)} %collective-permute-done.5.refs_1_, f32[32,128]{1,0:T(8,128)S(1)} %collective-permute-done.6.refs_2_, f32[32,128]{1,0:T(8,128)S(1)} %collective-permute-done.7.refs_3_), custom_call_target="tpu_custom_call" | custom-call | flops 1024000 | bytes 1024000 | tf_op jit(solution)/shard_map/finish/pallas_call | solution.py:670
  (3 shorter events, 0.0 us)
Async XLA Ops:
  0.6 8.2 %copy-start.4 = (f32[2,2,3,1,1,128]{5,4,3,2,1,0:T(1,128)S(1)}, f32[2,2,3,1,1,128]{5,4,3,2,1,0:T(1,128)}, u32[]{:S(2)}) copy-start(f32[2,2,3,1,1,128]{5,4,3,2,1,0:T(1,128)} %force.1) | copy-start | bytes 18436
  0.6 8.2 %copy-start.5 = (s32[1,1,128]{2,1,0:T(1,128)S(1)}, s32[1,1,128]{2,1,0:T(1,128)}, u32[]{:S(2)}) copy-start(s32[1,1,128]{2,1,0:T(1,128)} %cells.1) | copy-start | bytes 1540
  0.7 8.2 %copy-start.2 = (f32[2,3,8,8,128]{4,3,2,1,0:T(8,128)S(1)}, f32[2,3,8,8,128]{4,3,2,1,0:T(8,128)}, u32[]{:S(2)}) copy-start(f32[2,3,8,8,128]{4,3,2,1,0:T(8,128)} %param.6) | copy-start | bytes 589828
  0.7 8.2 %copy-start.3 = (f32[2,3,8,8,128]{4,3,2,1,0:T(8,128)S(1)}, f32[2,3,8,8,128]{4,3,2,1,0:T(8,128)}, u32[]{:S(2)}) copy-start(f32[2,3,8,8,128]{4,3,2,1,0:T(8,128)} %param.7) | copy-start | bytes 589828
  0.7 8.2 %copy-start.1 = (f32[4,8,8,128]{3,2,1,0:T(8,128)S(1)}, f32[4,8,8,128]{3,2,1,0:T(8,128)}, u32[]{:S(2)}) copy-start(f32[4,8,8,128]{3,2,1,0:T(8,128)} %param.9) | copy-start | bytes 393220
  0.7 8.8 %copy-start = (bf16[2,4,3,8,8,128]{5,4,3,2,1,0:T(8,128)(2,1)S(1)}, bf16[2,4,3,8,8,128]{5,4,3,2,1,0:T(8,128)(2,1)}, u32[]{:S(2)}) copy-start(bf16[2,4,3,8,8,128]{5,4,3,2,1,0:T(8,128)(2,1)} %param.8) | copy-start | bytes 1179652
  2.9 5.9 %collective-permute-start = (bf16[28,16,128]{2,1,0:T(8,128)(2,1)}, bf16[28,16,128]{2,1,0:T(8,128)(2,1)S(1)}, u32[]{:S(2)}, u32[]{:S(2)}) collective-permute-start(bf16[28,16,128]{2,1,0:T(8,128)(2,1)} %get-tuple-element.27), channel_id=1, source_target_pairs={{0,1},{1,0},{2,3},{3,2},{4,5},{5,4},{6,7},{7,6},{8,9},{9,8},{10,11... | collective-permute-start | bytes 344072 | tf_op jit(solution)/shard_map/ppermute | solution.py:36
  3.0 5.9 %collective-permute-start.1 = (bf16[28,16,128]{2,1,0:T(8,128)(2,1)}, bf16[28,16,128]{2,1,0:T(8,128)(2,1)S(1)}, u32[]{:S(2)}, u32[]{:S(2)}) collective-permute-start(bf16[28,16,128]{2,1,0:T(8,128)(2,1)} %get-tuple-element.28), channel_id=1, source_target_pairs={{0,8},{1,2},{2,1},{3,11},{4,12},{5,6},{6,5},{7,15},{8,0},{9,10},{1... | collective-permute-start | bytes 344072 | tf_op jit(solution)/shard_map/ppermute | solution.py:36
  5.6 3.9 %collective-permute-start.2 = (bf16[28,16,128]{2,1,0:T(8,128)(2,1)}, bf16[28,16,128]{2,1,0:T(8,128)(2,1)S(1)}, u32[]{:S(2)}, u32[]{:S(2)}) collective-permute-start(bf16[28,16,128]{2,1,0:T(8,128)(2,1)} %get-tuple-element.31), channel_id=1, source_target_pairs={{0,4},{1,5},{2,6},{3,7},{4,0},{5,1},{6,2},{7,3},{8,12},{9,13},{10,... | collective-permute-start | bytes 344072 | tf_op jit(solution)/shard_map/ppermute | solution.py:36
  6.8 4.3 %collective-permute-start.3 = (f32[2,2,16,128]{3,2,1,0:T(8,128)}, f32[2,2,16,128]{3,2,1,0:T(8,128)S(1)}, u32[]{:S(2)}, u32[]{:S(2)}) collective-permute-start(f32[2,2,16,128]{3,2,1,0:T(8,128)} %get-tuple-element.35), channel_id=1, source_target_pairs={{0,5},{1,4},{2,7},{3,6},{4,1},{5,0},{6,3},{7,2},{8,13},{9,12},{10,... | collective-permute-start | bytes 98312 | tf_op jit(solution)/shard_map/ppermute | solution.py:36
  6.8 4.3 %collective-permute-start.4 = (f32[2,2,16,128]{3,2,1,0:T(8,128)}, f32[2,2,16,128]{3,2,1,0:T(8,128)S(1)}, u32[]{:S(2)}, u32[]{:S(2)}) collective-permute-start(f32[2,2,16,128]{3,2,1,0:T(8,128)} %get-tuple-element.36), channel_id=1, source_target_pairs={{0,8},{1,6},{2,5},{3,11},{4,12},{5,2},{6,1},{7,15},{8,0},{9,14},{1... | collective-permute-start | bytes 98312 | tf_op jit(solution)/shard_map/ppermute | solution.py:36
  11.8 5.5 %collective-permute-start.5 = (f32[32,128]{1,0:T(8,128)S(1)}, f32[32,128]{1,0:T(8,128)S(1)}, u32[]{:S(2)}, u32[]{:S(2)}) collective-permute-start(f32[32,128]{1,0:T(8,128)S(1)} %get-tuple-element.45), channel_id=1, source_target_pairs={{0,24},{8,16},{16,8},{24,0},{1,25},{9,17},{17,9},{25,1},{2,26},{10... | collective-permute-start | bytes 49160 | tf_op jit(solution)/shard_map/ppermute | solution.py:663
  15.5 2.6 %collective-permute-start.6 = (f32[32,128]{1,0:T(8,128)S(1)}, f32[32,128]{1,0:T(8,128)S(1)}, u32[]{:S(2)}, u32[]{:S(2)}) collective-permute-start(f32[32,128]{1,0:T(8,128)S(1)} %get-tuple-element.46), channel_id=1, source_target_pairs={{0,16},{8,24},{16,0},{24,8},{1,17},{9,25},{17,1},{25,9},{2,18},{10... | collective-permute-start | bytes 49160 | tf_op jit(solution)/shard_map/ppermute | solution.py:663
  15.8 2.3 %collective-permute-start.7 = (f32[32,128]{1,0:T(8,128)S(1)}, f32[32,128]{1,0:T(8,128)S(1)}, u32[]{:S(2)}, u32[]{:S(2)}) collective-permute-start(f32[32,128]{1,0:T(8,128)S(1)} %get-tuple-element.47), channel_id=1, source_target_pairs={{0,8},{8,0},{16,24},{24,16},{1,9},{9,1},{17,25},{25,17},{2,10},{10... | collective-permute-start | bytes 49160 | tf_op jit(solution)/shard_map/ppermute | solution.py:663

commit v5 on v4

--- a/solution.py
+++ b/solution.py
@@ -20,20 +20,30 @@
     return "AB"[: max(0, min(2, count - 1))]
 
 
-def swap(values, rounds):
+def swap(values, rounds, first_along_x=False, first_idle=False):
     names = ("ev", "gx", "gy")
     sizes = [lax.axis_size(a) for a in names]
     pairs = []
     for source in itertools.product(*map(range, sizes)):
         target = list(source)
-        for axis, name in rounds.items():
+        steps = {"gx": "A"}.items() if first_along_x and source[2] == 0 else rounds.items()
+        for axis, name in steps:
             along = names.index(axis)
             target[along] += 1 if (source[along] % 2 == 0) == (name == "A") else -1
-        if not all(0 <= t < size for t, size in zip(target, sizes)):
+        idle = first_idle and source[2] == 0
+        if idle or not all(0 <= t < size for t, size in zip(target, sizes)):
             target = [source[0] ^ 1, *source[1:]]
         flat = [(s[0] * sizes[1] + s[1]) * sizes[2] + s[2] for s in (source, target)]
         pairs.append(tuple(flat))
     return lax.ppermute(values, names, pairs)
+
+
+def their_turn(x_rounds, y_rounds):
+    return bool(x_rounds) and "B" in y_rounds
+
+
+def is_first():
+    return lax.axis_index("gy") == 0
 
 
 def linked(axis, name):
@@ -123,6 +133,13 @@
     def face(axis, name, ring):
         return jnp.where(upward(axis, name), 8 - ring, ring - 1)
 
+    def pick_x(name):
+        def pick(ref, index, ring):
+            row = pl.multiple_of(face("gx", name, ring) * 8, 8)
+            return ref[pl.ds(index * 64 + row, 8), :]
+
+        return pick
+
     out = []
 
     def send():
@@ -135,15 +152,14 @@
         def pick_y(ref, index, ring, name=name):
             return ref[pl.ds(index * 64 + face("gy", name, ring), 8, stride=8), :]
 
-        fill(messages[len(out)], pick_y)
+        if name == "B" and their_turn(x_rounds, y_rounds):
+            pl.when(is_first())(functools.partial(fill, messages[len(out)], pick_x("A")))
+            pl.when(jnp.logical_not(is_first()))(functools.partial(fill, messages[len(out)], pick_y))
+        else:
+            fill(messages[len(out)], pick_y)
         send()
     for name in x_rounds:
-
-        def pick_x(ref, index, ring, name=name):
-            row = pl.multiple_of(face("gx", name, ring) * 8, 8)
-            return ref[pl.ds(index * 64 + row, 8), :]
-
-        fill(messages[len(out)], pick_x)
+        fill(messages[len(out)], pick_x(name))
         send()
     for name_x in x_rounds:
         for name_y in y_rounds:
@@ -301,7 +317,7 @@
     fields = 3 * events
     x_messages, refs = refs[: len(x_rounds)], refs[len(x_rounds) :]
     y_messages, refs = refs[: len(y_rounds)], refs[len(y_rounds) :]
-    here, start, stored, medium, coef, then, part = refs
+    here, start, stored, medium, coef, then, part = refs[-7:]
 
     for f in range(fields):
         e, c = f // 3, f % 3
@@ -339,7 +355,14 @@
             row = pl.multiple_of(x_row(up, ring) * ROWS, ROWS)
             ref[index, pl.ds(row, 8), :] = values
 
-        place(masked(x_messages[k], "gx", name) if k < len(x_rounds) else nothing, put_x)
+        if name == "A" and their_turn(x_rounds, y_rounds):
+            for message, when in (
+                (y_messages[1], is_first()),
+                (x_messages[0], jnp.logical_not(is_first())),
+            ):
+                pl.when(when)(functools.partial(place, masked(message, "gx", name), put_x))
+        else:
+            place(masked(x_messages[k], "gx", name) if k < len(x_rounds) else nothing, put_x)
     for k, name in enumerate("AB"):
         up = upward("gy", name)
 
@@ -565,6 +588,18 @@
     )
 
 
+def wait_for(before, messages):
+    arrays = [*before, *messages]
+    return call(
+        lambda *refs: None,
+        [((8, 128), F32)],
+        [pl.ANY] * len(arrays),
+        name="arrival",
+        out_memory=pl.ANY,
+        cost=8000,
+    )(*arrays)
+
+
 def body(adjoint_now, adjoint_prev, forward, medium, drm_cells, drm_force):
     events, _, width_x, width_y, depth = adjoint_now.shape
     fields = 3 * events
@@ -606,26 +641,22 @@
     )(now.reshape(-1, depth), prev.reshape(-1, depth), fwd, med.reshape(-1, depth), drm_cells, drm_force)
     kinds = [{"gy": r} for r in y_rounds] + [{"gx": r} for r in x_rounds]
     kinds += [{"gx": x, "gy": y} for x in x_rounds for y in y_rounds]
-    received = [swap(message, kind) for message, kind in zip(messages, kinds)]
+    turn = their_turn(x_rounds, y_rounds)
+    received = [
+        swap(message, kind, turn and kind == {"gy": "B"}, turn and kind == {"gx": "A"})
+        for message, kind in zip(messages, kinds)
+    ]
     y_messages, rest = received[: len(y_rounds)], received[len(y_rounds) :]
     x_messages, corners = rest[: len(x_rounds)], rest[len(x_rounds) :]
-    arrival = ()
-    if y_messages:
-        arrival = call(
-            lambda *refs: None,
-            [((8, depth), F32)],
-            [pl.ANY] * len(y_messages),
-            name="arrival",
-            out_memory=pl.ANY,
-            cost=8000,
-        )(*y_messages)
+    order = [y_messages[1], y_messages[0]] if turn else [*x_messages[:1], *y_messages[:1]]
+    arrival = wait_for([], order[:1])
+    arrival = wait_for(arrival, order[1:2])
     base, extra = call(
         functools.partial(own_kernel, events),
         [own, own],
         [pltpu.VMEM] * 5 + [pl.ANY] * len(arrival),
         name="own",
     )(now, prev, med, drm_cells, drm_force, *arrival)
-
     wide = ((fields, tall, depth), F32)
     here, start, stored, tall_medium, coef, then, part = call(
         functools.partial(inner_kernel, events, x_rounds, y_rounds),

time: 19.2 us -> 18.5 us (0.964); the launches traced: 18.8 us -> 18.4 us
  starting transfers between devices: 10.1 us -> 8.54 us
  waiting for transfers between devices: 2.05 us -> 3.09 us
    ppermute x3, starting transfers between devices: 4.2 us -> 3.07 us  [body(): pieces.append(lax.ppermute(sent[m - 1], 'ev', pairs))]
    ppermute x5, waiting for transfers between devices: 0.89 us -> 1.93 us  [swap(): return lax.ppermute(values, names, pairs)]
    ppermute x5, starting transfers between devices: 5.91 us -> 5.47 us  [swap(): return lax.ppermute(values, names, pairs)]
  transfers between devices with their start and end apart: 8 -> 8, of which waited for: 4 -> 3; matrix products, arithmetic and copies ran while one was open for 0% -> 0% of each run, Pallas kernels for 12% -> 13%
where the time goes in v5:
time: 18.5 us; the launch traced here: 18.4 us
  starting transfers between devices  8.54 us (46%)
  Pallas kernels  5.92 us (32%)
  waiting for transfers between devices  3.09 us (17%)
  between operations  0.78 us (4%)
    ppermute x5, starting transfers between devices, swap(): return lax.ppermute(values, names, pairs)  5.47 us
    ppermute x3, starting transfers between devices, body(): pieces.append(lax.ppermute(sent[m - 1], 'ev', pairs))  3.07 us
    pallas_call x1, Pallas kernels, body(): call(functools.partial(pack_kernel, events, x_rounds, y_rounds), shapes,...  2.23 us
    ppermute x5, waiting for transfers between devices, swap(): return lax.ppermute(values, names, pairs)  1.93 us
    ppermute x3, waiting for transfers between devices, body(): pieces.append(lax.ppermute(sent[m - 1], 'ev', pairs))  1.16 us
    pallas_call x1, Pallas kernels, body(): call(functools.partial(inner_kernel, events, x_rounds, y_rounds), [wide,...  1.06 us
    pallas_call x1, Pallas kernels, body(): call(functools.partial(second_kernel, events), [own, own], [pltpu.VMEM] *...  0.96 us
    pallas_call x1, Pallas kernels, body(): call(functools.partial(finish_kernel, shares, 1.0 / (events * shares)), [...  0.7 us
  transfers between devices with their start and end apart: 8, of which 3 were waited for; matrix products, arithmetic and copies ran while one was open for 0% of the time, Pallas kernels for 13%

profile of v5, /device:TPU:9, one launch (start us, length us, event | category | flops | bytes accessed | tf_op | source)
XLA Modules:
  0.0 18.4 jit_solution(17549175686350976354)
XLA Ops:
  0.6 0.0 copy-start.4
  0.6 0.0 copy-start.5
  0.7 0.0 copy-start.2
  0.7 0.0 copy-start.3
  0.7 0.0 copy-start.1
  0.7 0.0 copy-start
  0.7 2.2 %pack.1 = (bf16[28,16,128]{2,1,0:T(8,128)(2,1)}, bf16[28,16,128]{2,1,0:T(8,128)(2,1)}, bf16[28,16,128]{2,1,0:T(8,128)(2,1)}, f32[2,2,16,128]{3,2,1,0:T(8,128)}, f32[2,2,16,128]{3,2,1,0:T(8,128)}) custom-call(f32[384,128]{1,0:T(8,128)} %bitcast.19, f32[384,128]{1,0:T(8,128)} %bitcast.23, bf16[24,8,8,128]{3,2,1,0:T(8,128)(2,1)} %bitcast.11, ...), custom_call_target="tpu_custom_call" | custom-call | flops 8192000 | bytes 8192000 | tf_op jit(solution)/shard_map/pack/pallas_call | solution.py:620
  2.9 1.4 %collective-permute-start = (bf16[28,16,128]{2,1,0:T(8,128)(2,1)}, bf16[28,16,128]{2,1,0:T(8,128)(2,1)S(1)}, u32[]{:S(2)}, u32[]{:S(2)}) collective-permute-start(bf16[28,16,128]{2,1,0:T(8,128)(2,1)} %get-tuple-element.27), channel_id=1, source_target_pairs={{0,4},{1,2},{2,1},{3,11},{4,0},{5,6},{6,5},{7,15},{8,12},{9,10},{1... | collective-permute-start | bytes 344072 | tf_op jit(solution)/shard_map/ppermute | solution.py:38
  4.3 0.1 collective-permute-start.1
  4.4 1.1 %collective-permute-start.2 = (bf16[28,16,128]{2,1,0:T(8,128)(2,1)}, bf16[28,16,128]{2,1,0:T(8,128)(2,1)S(1)}, u32[]{:S(2)}, u32[]{:S(2)}) collective-permute-start(bf16[28,16,128]{2,1,0:T(8,128)(2,1)} %get-tuple-element.31), channel_id=1, source_target_pairs={{0,8},{1,5},{2,6},{3,7},{4,12},{5,1},{6,2},{7,3},{8,0},{9,13},{10,... | collective-permute-start | bytes 344072 | tf_op jit(solution)/shard_map/ppermute | solution.py:38
  5.5 2.4 %collective-permute-start.3 = (f32[2,2,16,128]{3,2,1,0:T(8,128)}, f32[2,2,16,128]{3,2,1,0:T(8,128)S(1)}, u32[]{:S(2)}, u32[]{:S(2)}) collective-permute-start(f32[2,2,16,128]{3,2,1,0:T(8,128)} %get-tuple-element.35), channel_id=1, source_target_pairs={{0,5},{1,4},{2,7},{3,6},{4,1},{5,0},{6,3},{7,2},{8,13},{9,12},{10,... | collective-permute-start | bytes 98312 | tf_op jit(solution)/shard_map/ppermute | solution.py:38
  8.0 0.5 %collective-permute-start.4 = (f32[2,2,16,128]{3,2,1,0:T(8,128)}, f32[2,2,16,128]{3,2,1,0:T(8,128)S(1)}, u32[]{:S(2)}, u32[]{:S(2)}) collective-permute-start(f32[2,2,16,128]{3,2,1,0:T(8,128)} %get-tuple-element.36), channel_id=1, source_target_pairs={{0,8},{1,6},{2,5},{3,11},{4,12},{5,2},{6,1},{7,15},{8,0},{9,14},{1... | collective-permute-start | bytes 98312 | tf_op jit(solution)/shard_map/ppermute | solution.py:38
  8.4 0.0 collective-permute-done.refs_0_.refs_2_
  8.4 0.0 collective-permute-done.1.refs_1_
  8.4 0.0 copy-done.4
  8.4 0.0 copy-done.5
  8.4 0.0 copy-done.2
  8.5 0.3 %own.1 = (f32[6,64,128]{2,1,0:T(8,128)S(1)}, f32[6,64,128]{2,1,0:T(8,128)S(1)}) custom-call(f32[6,64,128]{2,1,0:T(8,128)S(1)} %bitcast.20, f32[6,64,128]{2,1,0:T(8,128)S(1)} %bitcast.24, f32[4,64,128]{2,1,0:T(8,128)S(1)} %bitcast.15, s32[1,1,128]{2,1,0:T(1,128)S(1)} %copy-done.5, f32[2,2,3,1,1,128]{5,4,3,2,1,0:T(1,128)S(1)} %copy-done.4, ...), custom_call_target="tpu_custom_call" | custom-call | flops 1024000 | bytes 1024000 | tf_op jit(solution)/shard_map/own/pallas_call | solution.py:654
  8.8 0.0 collective-permute-done.2.refs_0_
  8.8 0.0 copy-done
  8.8 1.1 %inner.1 = (f32[6,192,128]{2,1,0:T(8,128)S(1)}, f32[6,192,128]{2,1,0:T(8,128)S(1)}, f32[12,192,128]{2,1,0:T(8,128)S(1)}, f32[4,192,128]{2,1,0:T(8,128)S(1)}, f32...) custom-call(f32[6,64,128]{2,1,0:T(8,128)S(1)} %bitcast.21, ...), custom_call_target="tpu_custom_call" | custom-call | flops 3072000 | bytes 3072000 | tf_op jit(solution)/shard_map/inner/pallas_call | solution.py:661
  9.9 0.0 collective-permute-done.3.refs_0_
  9.9 1.9 %collective-permute-done.4.refs_1_ = f32[2,2,16,128]{3,2,1,0:T(8,128)S(1)} collective-permute-done((f32[2,2,16,128]{3,2,1,0:T(8,128)}, f32[2,2,16,128]{3,2,1,0:T(8,128)S(1)}, u32[]{:S(2)}, u32[]{:S(2)}) %collective-permute-start.4) | collective-permute-done | bytes 32800 | tf_op jit(solution)/shard_map/ppermute | solution.py:38
  11.8 0.6 %edges.1 = (f32[6,64,128]{2,1,0:T(8,128)S(1)}, f32[32,128]{1,0:T(8,128)S(1)}, f32[32,128]{1,0:T(8,128)S(1)}, f32[32,128]{1,0:T(8,128)S(1)}, f32[32,128]{1,0:T(8,128)S(1)}) custom-call(f32[2,2,16,128]{3,2,1,0:T(8,128)S(1)} %collective-permute-done.3.refs_0_, f32[2,2,16,128]{3,2,1,0:T(8,128)S(1)} %collective-permute-done.4.refs_1_, ...), custom_call_target="tpu_custom_call" | custom-call | flops 1024000 | bytes 1024000 | tf_op jit(solution)/shard_map/edges/pallas_call | solution.py:678
  12.5 2.6 %collective-permute-start.5 = (f32[32,128]{1,0:T(8,128)S(1)}, f32[32,128]{1,0:T(8,128)S(1)}, u32[]{:S(2)}, u32[]{:S(2)}) collective-permute-start(f32[32,128]{1,0:T(8,128)S(1)} %get-tuple-element.45), channel_id=1, source_target_pairs={{0,24},{8,16},{16,8},{24,0},{1,25},{9,17},{17,9},{25,1},{2,26},{10... | collective-permute-start | bytes 49160 | tf_op jit(solution)/shard_map/ppermute | solution.py:694
  15.1 0.3 %collective-permute-start.6 = (f32[32,128]{1,0:T(8,128)S(1)}, f32[32,128]{1,0:T(8,128)S(1)}, u32[]{:S(2)}, u32[]{:S(2)}) collective-permute-start(f32[32,128]{1,0:T(8,128)S(1)} %get-tuple-element.46), channel_id=1, source_target_pairs={{0,16},{8,24},{16,0},{24,8},{1,17},{9,25},{17,1},{25,9},{2,18},{10... | collective-permute-start | bytes 49160 | tf_op jit(solution)/shard_map/ppermute | solution.py:694
  15.3 0.2 %collective-permute-start.7 = (f32[32,128]{1,0:T(8,128)S(1)}, f32[32,128]{1,0:T(8,128)S(1)}, u32[]{:S(2)}, u32[]{:S(2)}) collective-permute-start(f32[32,128]{1,0:T(8,128)S(1)} %get-tuple-element.47), channel_id=1, source_target_pairs={{0,8},{8,0},{16,24},{24,16},{1,9},{9,1},{17,25},{25,17},{2,10},{10... | collective-permute-start | bytes 49160 | tf_op jit(solution)/shard_map/ppermute | solution.py:694
  15.5 1.0 %second.1 = (f32[6,64,128]{2,1,0:T(8,128)}, f32[6,64,128]{2,1,0:T(8,128)}) custom-call(f32[6,64,128]{2,1,0:T(8,128)S(1)} %bitcast.22, f32[6,64,128]{2,1,0:T(8,128)S(1)} %get-tuple-element.29.extra, f32[4,64,128]{2,1,0:T(8,128)S(1)} %bitcast.18, f32[4,192,128]{2,1,0:T(8,128)S(1)} %get-tuple-element.32.refs_5_.medium, ...), custom_call_target="tpu_custom_call" | custom-call | flops 1024000 | bytes 1024000 | tf_op jit(solution)/shard_map/second/pallas_call | solution.py:695
  16.5 0.4 %collective-permute-done.5.refs_1_ = f32[32,128]{1,0:T(8,128)S(1)} collective-permute-done((f32[32,128]{1,0:T(8,128)S(1)}, f32[32,128]{1,0:T(8,128)S(1)}, u32[]{:S(2)}, u32[]{:S(2)}) %collective-permute-start.5) | collective-permute-done | bytes 16416 | tf_op jit(solution)/shard_map/ppermute | solution.py:694
  16.9 0.8 %collective-permute-done.6.refs_2_ = f32[32,128]{1,0:T(8,128)S(1)} collective-permute-done((f32[32,128]{1,0:T(8,128)S(1)}, f32[32,128]{1,0:T(8,128)S(1)}, u32[]{:S(2)}, u32[]{:S(2)}) %collective-permute-start.6) | collective-permute-done | bytes 16416 | tf_op jit(solution)/shard_map/ppermute | solution.py:694
  17.6 0.0 collective-permute-done.7.refs_3_
  17.7 0.7 %finish.1 = (f32[64,32]{1,0:T(8,128)}, f32[64,32]{1,0:T(8,128)}) custom-call(f32[32,128]{1,0:T(8,128)S(1)} %get-tuple-element.44.refs_0_, f32[32,128]{1,0:T(8,128)S(1)} %collective-permute-done.5.refs_1_, f32[32,128]{1,0:T(8,128)S(1)} %collective-permute-done.6.refs_2_, f32[32,128]{1,0:T(8,128)S(1)} %collective-permute-done.7.refs_3_), custom_call_target="tpu_custom_call" | custom-call | flops 1024000 | bytes 1024000 | tf_op jit(solution)/shard_map/finish/pallas_call | solution.py:701
  (4 shorter events, 0.0 us)
Async XLA Ops:
  0.6 7.8 %copy-start.4 = (f32[2,2,3,1,1,128]{5,4,3,2,1,0:T(1,128)S(1)}, f32[2,2,3,1,1,128]{5,4,3,2,1,0:T(1,128)}, u32[]{:S(2)}) copy-start(f32[2,2,3,1,1,128]{5,4,3,2,1,0:T(1,128)} %force.1) | copy-start | bytes 18436
  0.6 7.8 %copy-start.5 = (s32[1,1,128]{2,1,0:T(1,128)S(1)}, s32[1,1,128]{2,1,0:T(1,128)}, u32[]{:S(2)}) copy-start(s32[1,1,128]{2,1,0:T(1,128)} %cells.1) | copy-start | bytes 1540
  0.7 7.8 %copy-start.2 = (f32[2,3,8,8,128]{4,3,2,1,0:T(8,128)S(1)}, f32[2,3,8,8,128]{4,3,2,1,0:T(8,128)}, u32[]{:S(2)}) copy-start(f32[2,3,8,8,128]{4,3,2,1,0:T(8,128)} %param.6) | copy-start | bytes 589828
  0.7 7.8 %copy-start.3 = (f32[2,3,8,8,128]{4,3,2,1,0:T(8,128)S(1)}, f32[2,3,8,8,128]{4,3,2,1,0:T(8,128)}, u32[]{:S(2)}) copy-start(f32[2,3,8,8,128]{4,3,2,1,0:T(8,128)} %param.7) | copy-start | bytes 589828
  0.7 7.8 %copy-start.1 = (f32[4,8,8,128]{3,2,1,0:T(8,128)S(1)}, f32[4,8,8,128]{3,2,1,0:T(8,128)}, u32[]{:S(2)}) copy-start(f32[4,8,8,128]{3,2,1,0:T(8,128)} %param.9) | copy-start | bytes 393220
  0.7 8.1 %copy-start = (bf16[2,4,3,8,8,128]{5,4,3,2,1,0:T(8,128)(2,1)S(1)}, bf16[2,4,3,8,8,128]{5,4,3,2,1,0:T(8,128)(2,1)}, u32[]{:S(2)}) copy-start(bf16[2,4,3,8,8,128]{5,4,3,2,1,0:T(8,128)(2,1)} %param.8) | copy-start | bytes 1179652
  2.9 5.5 %collective-permute-start = (bf16[28,16,128]{2,1,0:T(8,128)(2,1)}, bf16[28,16,128]{2,1,0:T(8,128)(2,1)S(1)}, u32[]{:S(2)}, u32[]{:S(2)}) collective-permute-start(bf16[28,16,128]{2,1,0:T(8,128)(2,1)} %get-tuple-element.27), channel_id=1, source_target_pairs={{0,4},{1,2},{2,1},{3,11},{4,0},{5,6},{6,5},{7,15},{8,12},{9,10},{1... | collective-permute-start | bytes 344072 | tf_op jit(solution)/shard_map/ppermute | solution.py:38
  4.3 4.1 %collective-permute-start.1 = (bf16[28,16,128]{2,1,0:T(8,128)(2,1)}, bf16[28,16,128]{2,1,0:T(8,128)(2,1)S(1)}, u32[]{:S(2)}, u32[]{:S(2)}) collective-permute-start(bf16[28,16,128]{2,1,0:T(8,128)(2,1)} %get-tuple-element.28), channel_id=1, source_target_pairs={{0,1},{1,0},{2,3},{3,2},{4,5},{5,4},{6,7},{7,6},{8,9},{9,8},{10,11... | collective-permute-start | bytes 344072 | tf_op jit(solution)/shard_map/ppermute | solution.py:38
  4.4 4.4 %collective-permute-start.2 = (bf16[28,16,128]{2,1,0:T(8,128)(2,1)}, bf16[28,16,128]{2,1,0:T(8,128)(2,1)S(1)}, u32[]{:S(2)}, u32[]{:S(2)}) collective-permute-start(bf16[28,16,128]{2,1,0:T(8,128)(2,1)} %get-tuple-element.31), channel_id=1, source_target_pairs={{0,8},{1,5},{2,6},{3,7},{4,12},{5,1},{6,2},{7,3},{8,0},{9,13},{10,... | collective-permute-start | bytes 344072 | tf_op jit(solution)/shard_map/ppermute | solution.py:38
  5.5 4.4 %collective-permute-start.3 = (f32[2,2,16,128]{3,2,1,0:T(8,128)}, f32[2,2,16,128]{3,2,1,0:T(8,128)S(1)}, u32[]{:S(2)}, u32[]{:S(2)}) collective-permute-start(f32[2,2,16,128]{3,2,1,0:T(8,128)} %get-tuple-element.35), channel_id=1, source_target_pairs={{0,5},{1,4},{2,7},{3,6},{4,1},{5,0},{6,3},{7,2},{8,13},{9,12},{10,... | collective-permute-start | bytes 98312 | tf_op jit(solution)/shard_map/ppermute | solution.py:38
  8.0 3.9 %collective-permute-start.4 = (f32[2,2,16,128]{3,2,1,0:T(8,128)}, f32[2,2,16,128]{3,2,1,0:T(8,128)S(1)}, u32[]{:S(2)}, u32[]{:S(2)}) collective-permute-start(f32[2,2,16,128]{3,2,1,0:T(8,128)} %get-tuple-element.36), channel_id=1, source_target_pairs={{0,8},{1,6},{2,5},{3,11},{4,12},{5,2},{6,1},{7,15},{8,0},{9,14},{1... | collective-permute-start | bytes 98312 | tf_op jit(solution)/shard_map/ppermute | solution.py:38
  12.5 4.4 %collective-permute-start.5 = (f32[32,128]{1,0:T(8,128)S(1)}, f32[32,128]{1,0:T(8,128)S(1)}, u32[]{:S(2)}, u32[]{:S(2)}) collective-permute-start(f32[32,128]{1,0:T(8,128)S(1)} %get-tuple-element.45), channel_id=1, source_target_pairs={{0,24},{8,16},{16,8},{24,0},{1,25},{9,17},{17,9},{25,1},{2,26},{10... | collective-permute-start | bytes 49160 | tf_op jit(solution)/shard_map/ppermute | solution.py:694
  15.1 2.6 %collective-permute-start.6 = (f32[32,128]{1,0:T(8,128)S(1)}, f32[32,128]{1,0:T(8,128)S(1)}, u32[]{:S(2)}, u32[]{:S(2)}) collective-permute-start(f32[32,128]{1,0:T(8,128)S(1)} %get-tuple-element.46), channel_id=1, source_target_pairs={{0,16},{8,24},{16,0},{24,8},{1,17},{9,25},{17,1},{25,9},{2,18},{10... | collective-permute-start | bytes 49160 | tf_op jit(solution)/shard_map/ppermute | solution.py:694
  15.3 2.3 %collective-permute-start.7 = (f32[32,128]{1,0:T(8,128)S(1)}, f32[32,128]{1,0:T(8,128)S(1)}, u32[]{:S(2)}, u32[]{:S(2)}) collective-permute-start(f32[32,128]{1,0:T(8,128)S(1)} %get-tuple-element.47), channel_id=1, source_target_pairs={{0,8},{8,0},{16,24},{24,16},{1,9},{9,1},{17,25},{25,17},{2,10},{10... | collective-permute-start | bytes 49160 | tf_op jit(solution)/shard_map/ppermute | solution.py:694

commit v6 on v5

--- a/solution.py
+++ b/solution.py
@@ -13,7 +13,6 @@
 SHEAR, LAME, BUOY, INV = range(4)
 ROWS = 16
 VMEM_LIMIT = 40 * 1024 * 1024
-PACK_LIMIT = 60 * 1024 * 1024
 
 
 def rounds_of(count):
@@ -86,14 +85,14 @@
 
 def pack_kernel(events, x_rounds, y_rounds, *refs):
     fields = 3 * events
-    total = len(x_rounds) + len(y_rounds) + len(x_rounds) * len(y_rounds)
-    sources, targets, refs = refs[:6], refs[6 : 6 + total], refs[6 + total :]
-    now, prev, fwd, med, cells, force, base, stored, arrived, left = refs[:10]
-    messages = refs[10:]
-    now_in, prev_in, fwd_in, med_in, cells_in, force_in = sources
+    now_in, prev_in, fwd_in, med_in, cells_in, force_in = refs[:6]
+    now, fwd, med, cells, force, base = refs[6:12]
+    messages, (prev, stored, arrived) = refs[12:-3], refs[-3:]
     pairs = [(cells_in, cells), (force_in, force), (now_in, now), (prev_in, prev), (med_in, med)]
-    for e in range(events):
-        pairs.append((fwd_in.at[pl.ds(e * 12 + 3, 6)], fwd.at[pl.ds(e * 6, 6)]))
+    for first, count in ((3, 6), (0, 3), (9, 3)):
+        for e in range(events):
+            part = pl.ds(e * 12 + first, count)
+            pairs.append((fwd_in.at[part], fwd.at[part]))
     copies = [
         pltpu.make_async_copy(source, target, arrived.at[k])
         for k, (source, target) in enumerate(pairs)
@@ -104,7 +103,7 @@
         copy.wait()
     rows = [force[e, 0, c, 0] for e in range(events) for c in range(3)]
     pushed = force_field(cells[0], rows, 64)
-    for copy in copies[2:]:
+    for copy in copies[2 : 5 + events]:
         copy.wait()
     scale = STEP_FACTOR * med[pl.ds(BUOY * 64, 64), :]
     for f in range(fields):
@@ -112,7 +111,7 @@
         base[spot, :] = 2.0 * now[spot, :] - prev[spot, :] + scale * pushed[f * 64 : (f + 1) * 64]
         e, c = f // 3, f % 3
         for t in range(2):
-            part = fwd[(e * 2 + t) * 3 + c].astype(F32).reshape(64, 128)
+            part = fwd[(e * 4 + t + 1) * 3 + c].astype(F32).reshape(64, 128)
             stored[pl.ds((f * 2 + t) * 64, 64), :] = part
 
     def fill(message, pick):
@@ -140,30 +139,23 @@
 
         return pick
 
-    out = []
-
-    def send():
-        k = len(out)
-        out.append(pltpu.make_async_copy(messages[k], targets[k], left.at[k]))
-        out[k].start()
-
+    targets = iter(messages)
     for name in y_rounds:
 
         def pick_y(ref, index, ring, name=name):
             return ref[pl.ds(index * 64 + face("gy", name, ring), 8, stride=8), :]
 
         if name == "B" and their_turn(x_rounds, y_rounds):
-            pl.when(is_first())(functools.partial(fill, messages[len(out)], pick_x("A")))
-            pl.when(jnp.logical_not(is_first()))(functools.partial(fill, messages[len(out)], pick_y))
+            message = next(targets)
+            pl.when(is_first())(functools.partial(fill, message, pick_x("A")))
+            pl.when(jnp.logical_not(is_first()))(functools.partial(fill, message, pick_y))
         else:
-            fill(messages[len(out)], pick_y)
-        send()
+            fill(next(targets), pick_y)
     for name in x_rounds:
-        fill(messages[len(out)], pick_x(name))
-        send()
+        fill(next(targets), pick_x(name))
     for name_x in x_rounds:
         for name_y in y_rounds:
-            message = messages[len(out)]
+            message = next(targets)
             for ring_x in (1, 2):
                 for ring_y in (1, 2):
                     cell = face("gx", name_x, ring_x) * 8 + face("gy", name_y, ring_y)
@@ -172,8 +164,7 @@
                     target[pl.ds(fields, 4), :] = med[pl.ds(cell, 4, stride=64), :]
                     picked = base[pl.ds(cell, fields, stride=64), :]
                     target[pl.ds(fields + 4, fields), :] = picked
-            send()
-    for copy in out:
+    for copy in copies[5 + events :]:
         copy.wait()
 
 
@@ -295,18 +286,7 @@
 
 
 def tile_row(ref, index, row):
-    return ref[index, pl.ds((row - 2) * 8, 8), :]
-
-
-def own_kernel(events, now, prev, med, cells, force, *refs):
-    base, extra = refs[-2:]
-    fields = 3 * events
-    rows = [force[e, s, c, 0] for s in range(2) for e in range(events) for c in range(3)]
-    pushed = force_field(cells[0], rows, 64)
-    scale = STEP_FACTOR * med[BUOY]
-    for f in range(fields):
-        base[f] = 2.0 * now[f] - prev[f] + scale * pushed[f * 64 : (f + 1) * 64]
-        extra[f] = scale * pushed[(fields + f) * 64 : (fields + f + 1) * 64]
+    return ref[pl.ds(index * 64 + (row - 2) * 8, 8), :]
 
 
 def add_to(sums, key, value):
@@ -323,13 +303,13 @@
         e, c = f // 3, f % 3
         for x in range(8):
             spot = pl.ds((x + 2) * ROWS, 8)
-            here[f, spot, :] = now[f, pl.ds(x * 8, 8), :]
-            start[f, spot, :] = base[f, pl.ds(x * 8, 8), :]
+            here[f, spot, :] = now[pl.ds(f * 64 + x * 8, 8), :]
+            start[f, spot, :] = base[pl.ds(f * 64 + x * 8, 8), :]
             for t in range(2):
                 stored[2 * f + t, spot, :] = fwd[(e * 4 + t + 1) * 3 + c, x].astype(F32)
     for m in range(4):
         for x in range(8):
-            medium[m, pl.ds((x + 2) * ROWS, 8), :] = med[m, pl.ds(x * 8, 8), :]
+            medium[m, pl.ds((x + 2) * ROWS, 8), :] = med[pl.ds(m * 64 + x * 8, 8), :]
 
     def place(tile, put):
         for f in range(fields):
@@ -402,8 +382,8 @@
     for row in range(2, 10):
         inverse = tile_row(med, INV, row)
         shear = sums["lateral", row] + inverse * inverse * sums["upright", row]
-        part[0, pl.ds((row - 2) * 8, 8), :] = -0.25 * shear
-        part[1, pl.ds((row - 2) * 8, 8), :] = -sums["density", row]
+        part[pl.ds((row - 2) * 8, 8), :] = -0.25 * shear
+        part[pl.ds(64 + (row - 2) * 8, 8), :] = -sums["density", row]
 
 
 def gather(sums, field, wave, fwd, e, t, row):
@@ -531,7 +511,10 @@
         sent[m - 1][...] = slabs[me ^ m]
 
 
-def second_kernel(events, now, extra, med, medium, coef, then, edge, mid, after):
+def second_kernel(events, now, med, cells, force, medium, coef, then, edge, mid, after):
+    rows = [force[e, 1, c, 0] for e in range(events) for c in range(3)]
+    pushed = force_field(cells[0], rows, 64)
+
     def faces(name, row):
         if name == "inverse":
             return row_of(medium, INV, row)
@@ -545,14 +528,15 @@
     for e in range(events):
         apply = Event(lambda c, row, e=e: then_row(3 * e + c, row)).operator(faces)
         for row in range(2, 10):
-            spot = pl.ds((row - 2) * 8, 8)
             scale = STEP_FACTOR * tile_row(med, BUOY, row)
             for c, result in enumerate(apply(row)):
                 f = 3 * e + c
+                first = f * 64 + (row - 2) * 8
+                spot = pl.ds(first, 8)
                 current = then_row(f, row)[:8]
-                mid[f, spot, :] = current
-                after[f, spot, :] = (
-                    2.0 * current - now[f, spot, :] + extra[f, spot, :] + scale * result[:8]
+                mid[spot, :] = current
+                after[spot, :] = (
+                    2.0 * current - now[spot, :] + scale * (result[:8] + pushed[first : first + 8])
                 )
 
 
@@ -571,16 +555,14 @@
         out[pl.ds((v % 8) * 8, 8), :] = tile[:, :width] * scale
 
 
-def call(
-    kernel, outs, ins, scratch=(), name=None, limit=VMEM_LIMIT, cost=1000, out_memory=pltpu.VMEM
-):
+def call(kernel, outs, ins, scratch=(), name=None, cost=1000, out_memory=pltpu.VMEM, pinned=False):
     return pl.pallas_call(
         kernel,
-        out_shape=[jax.ShapeDtypeStruct(s, d) for s, d in outs],
+        out_shape=[pltpu.VMEM(s, d) if pinned else jax.ShapeDtypeStruct(s, d) for s, d in outs],
         in_specs=[pl.BlockSpec(memory_space=m) for m in ins],
         out_specs=[pl.BlockSpec(memory_space=out_memory)] * len(outs),
         scratch_shapes=[s if not isinstance(s, tuple) else pltpu.VMEM(*s) for s in scratch],
-        compiler_params=pltpu.CompilerParams(vmem_limit_bytes=limit),
+        compiler_params=pltpu.CompilerParams(vmem_limit_bytes=VMEM_LIMIT),
         cost_estimate=pl.CostEstimate(
             flops=cost * 1024, bytes_accessed=cost * 1024, transcendentals=0
         ),
@@ -606,39 +588,31 @@
     tile = width_x * width_y
     shares = lax.axis_size("ev")
     x_rounds, y_rounds = rounds_of(lax.axis_size("gx")), rounds_of(lax.axis_size("gy"))
-    now = adjoint_now.reshape(fields, tile, depth)
-    prev = adjoint_prev.reshape(fields, tile, depth)
-    fwd = forward.reshape(events * 12, width_x, width_y, depth)
-    med = medium.reshape(4, tile, depth)
-    own = ((fields, tile, depth), F32)
+    flat = ((fields * tile, depth), F32)
     tall = 12 * ROWS
 
     face = ((4 * fields + 4, 16, depth), BF16)
     corner = ((2, 2, 2 * fields + 4, depth), F32)
-    shapes = [face] * (len(y_rounds) + len(x_rounds)) + [corner] * (len(x_rounds) * len(y_rounds))
-    flat = ((fields * tile, depth), F32)
-    messages = call(
+    inputs = [
+        adjoint_now.reshape(flat[0]),
+        adjoint_prev.reshape(flat[0]),
+        forward.reshape(events * 12, width_x, width_y, depth),
+        medium.reshape(4 * tile, depth),
+        drm_cells,
+        drm_force,
+    ]
+    now, fwd, med, cells, force, base, *messages = call(
         functools.partial(pack_kernel, events, x_rounds, y_rounds),
-        shapes,
-        [pltpu.HBM] * 6,
-        [
-            flat,
-            flat,
-            ((2 * fields, width_x, width_y, depth), BF16),
-            ((4 * tile, depth), F32),
-            (drm_cells.shape, drm_cells.dtype),
-            (drm_force.shape, F32),
-            flat,
-            ((2 * fields * tile, depth), F32),
-            pltpu.SemaphoreType.DMA((5 + events,)),
-            pltpu.SemaphoreType.DMA((len(shapes),)),
-            *shapes,
-        ],
+        [(a.shape, a.dtype) for k, a in enumerate(inputs) if k != 1]
+        + [flat]
+        + [face] * (len(y_rounds) + len(x_rounds))
+        + [corner] * (len(x_rounds) * len(y_rounds)),
+        [pltpu.HBM] * len(inputs),
+        [flat, ((2 * fields * tile, depth), F32), pltpu.SemaphoreType.DMA((5 + 3 * events,))],
         "pack",
-        PACK_LIMIT,
         cost=8000,
-        out_memory=pltpu.HBM,
-    )(now.reshape(-1, depth), prev.reshape(-1, depth), fwd, med.reshape(-1, depth), drm_cells, drm_force)
+        pinned=True,
+    )(*(pltpu.with_memory_space_constraint(a, pltpu.HBM) for a in inputs))
     kinds = [{"gy": r} for r in y_rounds] + [{"gx": r} for r in x_rounds]
     kinds += [{"gx": x, "gy": y} for x in x_rounds for y in y_rounds]
     turn = their_turn(x_rounds, y_rounds)
@@ -649,14 +623,10 @@
     y_messages, rest = received[: len(y_rounds)], received[len(y_rounds) :]
     x_messages, corners = rest[: len(x_rounds)], rest[len(x_rounds) :]
     order = [y_messages[1], y_messages[0]] if turn else [*x_messages[:1], *y_messages[:1]]
-    arrival = wait_for([], order[:1])
-    arrival = wait_for(arrival, order[1:2])
-    base, extra = call(
-        functools.partial(own_kernel, events),
-        [own, own],
-        [pltpu.VMEM] * 5 + [pl.ANY] * len(arrival),
-        name="own",
-    )(now, prev, med, drm_cells, drm_force, *arrival)
+    arrival = ()
+    for message in order:
+        arrival = wait_for(arrival, [message])
+
     wide = ((fields, tall, depth), F32)
     here, start, stored, tall_medium, coef, then, part = call(
         functools.partial(inner_kernel, events, x_rounds, y_rounds),
@@ -667,12 +637,12 @@
             ((4, tall, depth), F32),
             ((len(COEFFICIENTS), tall, depth), F32),
             wide,
-            ((2, tile, depth), F32),
+            ((2 * tile, depth), F32),
         ],
-        [pltpu.VMEM] * (4 + len(x_messages) + len(y_messages)),
+        [pltpu.VMEM] * (4 + len(x_messages) + len(y_messages)) + [pl.ANY] * len(arrival),
         name="inner",
         cost=3000,
-    )(now, base, fwd, med, *x_messages, *y_messages)
+    )(now, base, fwd, med, *x_messages, *y_messages, *arrival)
     slab = ((16 // shares * 8, depth), F32)
     outer = ((fields, len(OUTER) * ROWS, depth), F32)
     edge, own_share, *sent = call(
@@ -694,10 +664,10 @@
         pieces.append(lax.ppermute(sent[m - 1], "ev", pairs))
     mid, after = call(
         functools.partial(second_kernel, events),
-        [own, own],
-        [pltpu.VMEM] * 7,
+        [flat, flat],
+        [pltpu.VMEM] * 8,
         name="second",
-    )(now, extra, med, tall_medium, coef, then, edge)
+    )(now, med, cells, force, tall_medium, coef, then, edge)
     shear, density = call(
         functools.partial(finish_kernel, shares, 1.0 / (events * shares)),
         [((tile, depth // shares), F32)] * 2,

time: 18.5 us -> 17.6 us (0.951)
  Pallas kernels: 5.92 us -> 5.12 us
    pallas_call x3 -> x2, Pallas kernels: 3.53 us -> 2.65 us  [the longest x1 1.55 us: body(): call(functools.partial(pack_kernel, events, x_rounds, y_rounds), [(a.shap...]
where the time goes in v6:
time: 17.6 us; the launch traced here: 17.4 us
  starting transfers between devices  8.54 us (49%)
  Pallas kernels  5.12 us (29%)
  waiting for transfers between devices  3.1 us (18%)
  between operations  0.68 us (4%)
    ppermute x5, starting transfers between devices, swap(): return lax.ppermute(values, names, pairs)  5.47 us
    ppermute x3, starting transfers between devices, body(): pieces.append(lax.ppermute(sent[m - 1], 'ev', pairs))  3.07 us
    ppermute x5, waiting for transfers between devices, swap(): return lax.ppermute(values, names, pairs)  2.08 us
    pallas_call x1, Pallas kernels, body(): call(functools.partial(pack_kernel, events, x_rounds, y_rounds), [(a.shap...  1.55 us
    pallas_call x1, Pallas kernels, body(): call(functools.partial(second_kernel, events), [flat, flat], [pltpu.VMEM]...  1.1 us
    pallas_call x1, Pallas kernels, body(): call(functools.partial(inner_kernel, events, x_rounds, y_rounds), [wide,...  1.1 us
    ppermute x3, waiting for transfers between devices, body(): pieces.append(lax.ppermute(sent[m - 1], 'ev', pairs))  1.02 us
    pallas_call x1, Pallas kernels, body(): call(functools.partial(finish_kernel, shares, 1.0 / (events * shares)), [...  0.7 us
  transfers between devices with their start and end apart: 8, of which 3 were waited for; matrix products, arithmetic and copies ran while one was open for 0% of the time, Pallas kernels for 13%

profile of v6, /device:TPU:9, one launch (start us, length us, event | category | flops | bytes accessed | tf_op | source)
XLA Modules:
  0.0 17.4 jit_solution(7585765546700762354)
XLA Ops:
  0.6 1.6 %pack.1 = (f32[384,128]{1,0:T(8,128)S(1)}, bf16[24,8,8,128]{3,2,1,0:T(8,128)(2,1)S(1)}, f32[256,128]{1,0:T(8,128)S(1)}, s32[1,1,128]{2,1,0:T(1,128)S(1)}, f32[2,...) custom-call(f32[384,128]{1,0:T(8,128)} %bitcast.9, ...), custom_call_target="tpu_custom_call" | custom-call | flops 8192000 | bytes 8192000 | tf_op jit(solution)/shard_map/pack/pallas_call | solution.py:604
  2.2 1.4 %collective-permute-start.2 = (bf16[28,16,128]{2,1,0:T(8,128)(2,1)S(1)}, bf16[28,16,128]{2,1,0:T(8,128)(2,1)S(1)}, u32[]{:S(2)}, u32[]{:S(2)}) collective-permute-start(bf16[28,16,128]{2,1,0:T(8,128)(2,1)S(1)} %get-tuple-element.39), channel_id=1, source_target_pairs={{0,4},{1,2},{2,1},{3,11},{4,0},{5,6},{6,5},{7,15},{8,12},{9,10},{1... | collective-permute-start | bytes 344072 | tf_op jit(solution)/shard_map/ppermute | solution.py:37
  3.6 0.1 collective-permute-start.1
  3.7 1.1 %collective-permute-start = (bf16[28,16,128]{2,1,0:T(8,128)(2,1)S(1)}, bf16[28,16,128]{2,1,0:T(8,128)(2,1)S(1)}, u32[]{:S(2)}, u32[]{:S(2)}) collective-permute-start(bf16[28,16,128]{2,1,0:T(8,128)(2,1)S(1)} %get-tuple-element.37), channel_id=1, source_target_pairs={{0,8},{1,5},{2,6},{3,7},{4,12},{5,1},{6,2},{7,3},{8,0},{9,13},{10,... | collective-permute-start | bytes 344072 | tf_op jit(solution)/shard_map/ppermute | solution.py:37
  4.8 2.4 %collective-permute-start.3 = (f32[2,2,16,128]{3,2,1,0:T(8,128)S(1)}, f32[2,2,16,128]{3,2,1,0:T(8,128)S(1)}, u32[]{:S(2)}, u32[]{:S(2)}) collective-permute-start(f32[2,2,16,128]{3,2,1,0:T(8,128)S(1)} %get-tuple-element.43), channel_id=1, source_target_pairs={{0,5},{1,4},{2,7},{3,6},{4,1},{5,0},{6,3},{7,2},{8,13},{9,12},{10,... | collective-permute-start | bytes 98312 | tf_op jit(solution)/shard_map/ppermute | solution.py:37
  7.2 0.5 %collective-permute-start.4 = (f32[2,2,16,128]{3,2,1,0:T(8,128)S(1)}, f32[2,2,16,128]{3,2,1,0:T(8,128)S(1)}, u32[]{:S(2)}, u32[]{:S(2)}) collective-permute-start(f32[2,2,16,128]{3,2,1,0:T(8,128)S(1)} %get-tuple-element.44), channel_id=1, source_target_pairs={{0,8},{1,6},{2,5},{3,11},{4,12},{5,2},{6,1},{7,15},{8,0},{9,14},{1... | collective-permute-start | bytes 98312 | tf_op jit(solution)/shard_map/ppermute | solution.py:37
  7.7 0.0 collective-permute-done.2.refs_0_.refs_2_
  7.7 0.0 collective-permute-done.1.refs_1_
  7.7 0.0 collective-permute-done.refs_0_
  7.7 1.1 %inner.1 = (f32[6,192,128]{2,1,0:T(8,128)S(1)}, f32[6,192,128]{2,1,0:T(8,128)S(1)}, f32[12,192,128]{2,1,0:T(8,128)S(1)}, f32[4,192,128]{2,1,0:T(8,128)S(1)}, f32...) custom-call(f32[384,128]{1,0:T(8,128)S(1)} %get-tuple-element.31.now, ...), custom_call_target="tpu_custom_call" | custom-call | flops 3072000 | bytes 3072000 | tf_op jit(solution)/shard_map/inner/pallas_call | solution.py:631
  8.8 0.0 collective-permute-done.3.refs_0_
  8.8 2.1 %collective-permute-done.4.refs_1_ = f32[2,2,16,128]{3,2,1,0:T(8,128)S(1)} collective-permute-done((f32[2,2,16,128]{3,2,1,0:T(8,128)S(1)}, f32[2,2,16,128]{3,2,1,0:T(8,128)S(1)}, u32[]{:S(2)}, u32[]{:S(2)}) %collective-permute-start.4) | collective-permute-done | bytes 32800 | tf_op jit(solution)/shard_map/ppermute | solution.py:37
  10.9 0.7 %edges.1 = (f32[6,64,128]{2,1,0:T(8,128)S(1)}, f32[32,128]{1,0:T(8,128)S(1)}, f32[32,128]{1,0:T(8,128)S(1)}, f32[32,128]{1,0:T(8,128)S(1)}, f32[32,128]{1,0:T(8,128)S(1)}) custom-call(f32[2,2,16,128]{3,2,1,0:T(8,128)S(1)} %collective-permute-done.3.refs_0_, f32[2,2,16,128]{3,2,1,0:T(8,128)S(1)} %collective-permute-done.4.refs_1_, ...), custom_call_target="tpu_custom_call" | custom-call | flops 1024000 | bytes 1024000 | tf_op jit(solution)/shard_map/edges/pallas_call | solution.py:648
  11.6 2.6 %collective-permute-start.5 = (f32[32,128]{1,0:T(8,128)S(1)}, f32[32,128]{1,0:T(8,128)S(1)}, u32[]{:S(2)}, u32[]{:S(2)}) collective-permute-start(f32[32,128]{1,0:T(8,128)S(1)} %get-tuple-element.53), channel_id=1, source_target_pairs={{0,24},{8,16},{16,8},{24,0},{1,25},{9,17},{17,9},{25,1},{2,26},{10... | collective-permute-start | bytes 49160 | tf_op jit(solution)/shard_map/ppermute | solution.py:664
  14.1 0.3 %collective-permute-start.6 = (f32[32,128]{1,0:T(8,128)S(1)}, f32[32,128]{1,0:T(8,128)S(1)}, u32[]{:S(2)}, u32[]{:S(2)}) collective-permute-start(f32[32,128]{1,0:T(8,128)S(1)} %get-tuple-element.54), channel_id=1, source_target_pairs={{0,16},{8,24},{16,0},{24,8},{1,17},{9,25},{17,1},{25,9},{2,18},{10... | collective-permute-start | bytes 49160 | tf_op jit(solution)/shard_map/ppermute | solution.py:664
  14.4 0.2 %collective-permute-start.7 = (f32[32,128]{1,0:T(8,128)S(1)}, f32[32,128]{1,0:T(8,128)S(1)}, u32[]{:S(2)}, u32[]{:S(2)}) collective-permute-start(f32[32,128]{1,0:T(8,128)S(1)} %get-tuple-element.55), channel_id=1, source_target_pairs={{0,8},{8,0},{16,24},{24,16},{1,9},{9,1},{17,25},{25,17},{2,10},{10... | collective-permute-start | bytes 49160 | tf_op jit(solution)/shard_map/ppermute | solution.py:664
  14.6 1.1 %second.1 = (f32[384,128]{1,0:T(8,128)}, f32[384,128]{1,0:T(8,128)}) custom-call(f32[384,128]{1,0:T(8,128)S(1)} %get-tuple-element.31.now, f32[256,128]{1,0:T(8,128)S(1)} %get-tuple-element.32.med.refs_10_, s32[1,1,128]{2,1,0:T(1,128)S(1)} %get-tuple-element.33.cells, f32[2,2,3,1,1,128]{5,4,3,2,1,0:T(1,128)S(1)} %get-tuple-element.34.force, ...), custom_call_target="tpu_custom_call" | custom-call | flops 1024000 | bytes 1024000 | tf_op jit(solution)/shard_map/second/pallas_call | solution.py:665
  15.7 0.2 %collective-permute-done.5.refs_1_ = f32[32,128]{1,0:T(8,128)S(1)} collective-permute-done((f32[32,128]{1,0:T(8,128)S(1)}, f32[32,128]{1,0:T(8,128)S(1)}, u32[]{:S(2)}, u32[]{:S(2)}) %collective-permute-start.5) | collective-permute-done | bytes 16416 | tf_op jit(solution)/shard_map/ppermute | solution.py:664
  15.9 0.8 %collective-permute-done.6.refs_2_ = f32[32,128]{1,0:T(8,128)S(1)} collective-permute-done((f32[32,128]{1,0:T(8,128)S(1)}, f32[32,128]{1,0:T(8,128)S(1)}, u32[]{:S(2)}, u32[]{:S(2)}) %collective-permute-start.6) | collective-permute-done | bytes 16416 | tf_op jit(solution)/shard_map/ppermute | solution.py:664
  16.7 0.0 collective-permute-done.7.refs_3_
  16.7 0.7 %finish.1 = (f32[64,32]{1,0:T(8,128)}, f32[64,32]{1,0:T(8,128)}) custom-call(f32[32,128]{1,0:T(8,128)S(1)} %get-tuple-element.52.refs_0_, f32[32,128]{1,0:T(8,128)S(1)} %collective-permute-done.5.refs_1_, f32[32,128]{1,0:T(8,128)S(1)} %collective-permute-done.6.refs_2_, f32[32,128]{1,0:T(8,128)S(1)} %collective-permute-done.7.refs_3_), custom_call_target="tpu_custom_call" | custom-call | flops 1024000 | bytes 1024000 | tf_op jit(solution)/shard_map/finish/pallas_call | solution.py:671
  (2 shorter events, 0.0 us)
Async XLA Ops:
  2.2 5.5 %collective-permute-start.2 = (bf16[28,16,128]{2,1,0:T(8,128)(2,1)S(1)}, bf16[28,16,128]{2,1,0:T(8,128)(2,1)S(1)}, u32[]{:S(2)}, u32[]{:S(2)}) collective-permute-start(bf16[28,16,128]{2,1,0:T(8,128)(2,1)S(1)} %get-tuple-element.39), channel_id=1, source_target_pairs={{0,4},{1,2},{2,1},{3,11},{4,0},{5,6},{6,5},{7,15},{8,12},{9,10},{1... | collective-permute-start | bytes 344072 | tf_op jit(solution)/shard_map/ppermute | solution.py:37
  3.6 4.1 %collective-permute-start.1 = (bf16[28,16,128]{2,1,0:T(8,128)(2,1)S(1)}, bf16[28,16,128]{2,1,0:T(8,128)(2,1)S(1)}, u32[]{:S(2)}, u32[]{:S(2)}) collective-permute-start(bf16[28,16,128]{2,1,0:T(8,128)(2,1)S(1)} %get-tuple-element.38), channel_id=1, source_target_pairs={{0,1},{1,0},{2,3},{3,2},{4,5},{5,4},{6,7},{7,6},{8,9},{9,8},{10,11... | collective-permute-start | bytes 344072 | tf_op jit(solution)/shard_map/ppermute | solution.py:37
  3.7 4.0 %collective-permute-start = (bf16[28,16,128]{2,1,0:T(8,128)(2,1)S(1)}, bf16[28,16,128]{2,1,0:T(8,128)(2,1)S(1)}, u32[]{:S(2)}, u32[]{:S(2)}) collective-permute-start(bf16[28,16,128]{2,1,0:T(8,128)(2,1)S(1)} %get-tuple-element.37), channel_id=1, source_target_pairs={{0,8},{1,5},{2,6},{3,7},{4,12},{5,1},{6,2},{7,3},{8,0},{9,13},{10,... | collective-permute-start | bytes 344072 | tf_op jit(solution)/shard_map/ppermute | solution.py:37
  4.8 4.0 %collective-permute-start.3 = (f32[2,2,16,128]{3,2,1,0:T(8,128)S(1)}, f32[2,2,16,128]{3,2,1,0:T(8,128)S(1)}, u32[]{:S(2)}, u32[]{:S(2)}) collective-permute-start(f32[2,2,16,128]{3,2,1,0:T(8,128)S(1)} %get-tuple-element.43), channel_id=1, source_target_pairs={{0,5},{1,4},{2,7},{3,6},{4,1},{5,0},{6,3},{7,2},{8,13},{9,12},{10,... | collective-permute-start | bytes 98312 | tf_op jit(solution)/shard_map/ppermute | solution.py:37
  7.2 3.7 %collective-permute-start.4 = (f32[2,2,16,128]{3,2,1,0:T(8,128)S(1)}, f32[2,2,16,128]{3,2,1,0:T(8,128)S(1)}, u32[]{:S(2)}, u32[]{:S(2)}) collective-permute-start(f32[2,2,16,128]{3,2,1,0:T(8,128)S(1)} %get-tuple-element.44), channel_id=1, source_target_pairs={{0,8},{1,6},{2,5},{3,11},{4,12},{5,2},{6,1},{7,15},{8,0},{9,14},{1... | collective-permute-start | bytes 98312 | tf_op jit(solution)/shard_map/ppermute | solution.py:37
  11.6 4.4 %collective-permute-start.5 = (f32[32,128]{1,0:T(8,128)S(1)}, f32[32,128]{1,0:T(8,128)S(1)}, u32[]{:S(2)}, u32[]{:S(2)}) collective-permute-start(f32[32,128]{1,0:T(8,128)S(1)} %get-tuple-element.53), channel_id=1, source_target_pairs={{0,24},{8,16},{16,8},{24,0},{1,25},{9,17},{17,9},{25,1},{2,26},{10... | collective-permute-start | bytes 49160 | tf_op jit(solution)/shard_map/ppermute | solution.py:664
  14.1 2.6 %collective-permute-start.6 = (f32[32,128]{1,0:T(8,128)S(1)}, f32[32,128]{1,0:T(8,128)S(1)}, u32[]{:S(2)}, u32[]{:S(2)}) collective-permute-start(f32[32,128]{1,0:T(8,128)S(1)} %get-tuple-element.54), channel_id=1, source_target_pairs={{0,16},{8,24},{16,0},{24,8},{1,17},{9,25},{17,1},{25,9},{2,18},{10... | collective-permute-start | bytes 49160 | tf_op jit(solution)/shard_map/ppermute | solution.py:664
  14.4 2.3 %collective-permute-start.7 = (f32[32,128]{1,0:T(8,128)S(1)}, f32[32,128]{1,0:T(8,128)S(1)}, u32[]{:S(2)}, u32[]{:S(2)}) collective-permute-start(f32[32,128]{1,0:T(8,128)S(1)} %get-tuple-element.55), channel_id=1, source_target_pairs={{0,8},{8,0},{16,24},{24,16},{1,9},{9,1},{17,25},{25,17},{2,10},{10... | collective-permute-start | bytes 49160 | tf_op jit(solution)/shard_map/ppermute | solution.py:664

commit v7 on v6

--- a/solution.py
+++ b/solution.py
@@ -230,13 +230,16 @@
             (self.z(c, row, 1) - self.z(c, row, -1))[:8],
         )
 
-    def operator(self, faces):
+    def operator(self, faces, sign=None):
         value = self.value
+
+        def signed(values):
+            return values if sign is None else sign * values
 
         @functools.cache
         def slope(d, row):
             if d == 0:
-                return faces("cross", row) * (value(0, row + 1) - value(0, row - 1))
+                return signed(faces("cross", row) * (value(0, row + 1) - value(0, row - 1)))
             if d == 1:
                 return faces("cross", row) * (self.y(1, row, 1) - self.y(1, row, -1))
             return faces("cross_z", row) * (self.z(2, row, 1) - self.z(2, row, -1))
@@ -261,7 +264,7 @@
                     kind + "_down", row
                 ) * (here - self.z(c, row, -1))
                 if c == 0:
-                    total = total + (
+                    total = total + signed(
                         (slope(1, row + 1) + slope(2, row + 1))
                         - (slope(1, row - 1) + slope(2, row - 1))
                     )
@@ -328,7 +331,20 @@
     def nothing(_):
         return jnp.zeros((16, 128), BF16)
 
-    for k, name in enumerate("AB"):
+    near = one_sided(x_rounds)
+    if near:
+        zeros = jnp.zeros((ROWS, 128), F32)
+        for row in (0, 1, 10, 11):
+            spot = pl.ds(row * ROWS, ROWS)
+            for f in range(fields):
+                here[f, spot, :] = zeros
+                start[f, spot, :] = zeros
+            for m in range(4):
+                medium[m, spot, :] = zeros
+        for row in (1, 10):
+            for k in range(2 * fields):
+                stored[k, pl.ds(row * ROWS, 8), :] = zeros[:8]
+    for k, name in enumerate("A" if near else "AB"):
         up = upward("gx", name)
 
         def put_x(ref, index, ring, values, up=up):
@@ -370,7 +386,7 @@
             for t in range(2)
         ]
         for row in range(2, 10):
-            if 3 <= row <= 8:
+            if near or 3 <= row <= 8:
                 scale = STEP_FACTOR * row_of(medium, BUOY, row)
                 for c, result in enumerate(apply(row)):
                     f = 3 * e + c
@@ -384,18 +400,55 @@
         shear = sums["lateral", row] + inverse * inverse * sums["upright", row]
         part[pl.ds((row - 2) * 8, 8), :] = -0.25 * shear
         part[pl.ds(64 + (row - 2) * 8, 8), :] = -sums["density", row]
-
-
-def gather(sums, field, wave, fwd, e, t, row):
+    if near:
+        mirror, sums = Mirror(), {}
+        for f in range(fields):
+            then[f, pl.ds(pl.multiple_of(mirror.row(1) * ROWS, ROWS), ROWS), :] = zeros
+        for e in range(events):
+            second = Event(lambda c, row, e=e: mirror.of(then, 3 * e + c, row))
+            wave = Event(lambda c, row, e=e: mirror.of(stored, 2 * (3 * e + c) + 1, row))
+            for row in (2, 3):
+                gather(sums, second, wave, fwd, e, 1, row, mirror.row(row) - 2)
+        for row in (2, 3):
+            mirror.add(part, sums, med, row)
+
+
+def gather(sums, field, wave, fwd, e, t, row, x=None):
+    x = row - 2 if x is None else x
     for c in range(3):
         ax, ay, az = field.slopes(c, row)
         ux, uy, uz = wave.slopes(c, row)
-        newer = fwd[(e * 4 + t) * 3 + c, row - 2].astype(F32)
-        older = fwd[(e * 4 + t + 2) * 3 + c, row - 2].astype(F32)
+        newer = fwd[(e * 4 + t) * 3 + c, x].astype(F32)
+        older = fwd[(e * 4 + t + 2) * 3 + c, x].astype(F32)
         bend = newer - 2.0 * wave.value(c, row)[:8] + older
         add_to(sums, ("lateral", row), ax * ux + ay * uy)
         add_to(sums, ("upright", row), az * uz)
         add_to(sums, ("density", row), field.value(c, row)[:8] * bend)
+
+
+def one_sided(x_rounds):
+    return x_rounds == "A" and lax.axis_size("gx") == 2
+
+
+class Mirror:
+    def __init__(self):
+        self.up = upward("gx", "A")
+        self.sign = jnp.where(self.up, 1.0, -1.0)
+        self.row = functools.cache(lambda r: jnp.where(self.up, r, 11 - r))
+
+    def of(self, ref, index, row):
+        start = pl.multiple_of(self.row(row) * ROWS, ROWS)
+        return ref[index, pl.ds(start, ROWS), :]
+
+    def tile(self, index, row):
+        return pl.ds(pl.multiple_of(index * 64 + (self.row(row) - 2) * 8, 8), 8)
+
+    def add(self, part, sums, med, row):
+        inverse = med[self.tile(INV, row), :]
+        more = sums["lateral", row] + inverse * inverse * sums["upright", row]
+        for index, value in ((0, -0.25 * more), (1, -sums["density", row])):
+            spot = self.tile(index, row)
+            part[spot, :] = part[spot, :] + value
 
 
 OUTER = (0, 1, 10, 11)
@@ -493,7 +546,10 @@
             density = density - sums["density", row]
         grads[0].append(shear)
         grads[1].append(density)
-    grads = grads[0] + grads[1]
+    cut(grads[0] + grads[1], shares, slabs, own_share, sent)
+
+
+def cut(grads, shares, slabs, own_share, sent):
     piece = 128 // shares
     quarter = lax.broadcasted_iota(jnp.int32, (8, 128), 1) // piece
     per = len(grads) // shares
@@ -509,6 +565,90 @@
     own_share[...] = slabs[me]
     for m in range(1, shares):
         sent[m - 1][...] = slabs[me ^ m]
+
+
+def near_kernel(events, x_rounds, y_rounds, shares, *refs):
+    fields = 3 * events
+    corners, refs = refs[: len(y_rounds)], refs[len(y_rounds) :]
+    (here, start, stored, medium, coef, then, part, fwd, med), refs = refs[:9], refs[9:]
+    edge, own_share, *sent = refs[: 1 + shares]
+    outer, outer_start, outer_medium, outer_coef, total, slabs = refs[1 + shares :]
+    mirror = Mirror()
+
+    height = 2 * ROWS
+    for f in range(fields):
+        outer_start[pl.ds(f * ROWS, ROWS), :] = mirror.of(start, f, 10)
+    for k, row in enumerate((10, 11)):
+        for f in range(fields):
+            outer[pl.ds(f * height + k * ROWS, ROWS), :] = mirror.of(here, f, row)
+        for m in range(4):
+            outer_medium[pl.ds(m * height + k * ROWS, ROWS), :] = mirror.of(medium, m, row)
+    for corner, name in zip(corners, y_rounds):
+        up_y, real = upward("gy", name), linked("gy", name)
+        for ring_x in (1, 2):
+            for ring_y in (1, 2):
+                place = y_place(up_y, ring_y)
+                spot = (ring_x - 1) * ROWS + place
+
+                def put(ref, spot, first, count, stride):
+                    values = corner[ring_x - 1, ring_y - 1, pl.ds(first, count), :]
+                    ref[pl.ds(spot, count, stride=stride), :] = jnp.where(real, values, 0.0)
+
+                put(outer, spot, 0, fields, height)
+                put(outer_medium, spot, fields, 4, height)
+                if ring_x == 1 and ring_y == 1:
+                    put(outer_start, place, fields + 4, fields, ROWS)
+
+    def row_with(ref, full):
+        def pick(index, row):
+            if row >= 10:
+                return ref[pl.ds(index * height + (row - 10) * ROWS, ROWS), :]
+            return mirror.of(full, index, row)
+
+        return pick
+
+    field_row, medium_row = row_with(outer, here), row_with(outer_medium, medium)
+    for k, row in enumerate((9, 10, 11)):
+        for name, value in coefficients(medium_row, row, row < 11).items():
+            if row > 9 or name in ("own_x", "other_x"):
+                outer_coef[COEFFICIENTS.index(name), pl.ds(k * ROWS, ROWS), :] = value
+
+    def faces(name, row):
+        if name == "inverse":
+            return medium_row(INV, row)
+        index = COEFFICIENTS.index(name)
+        along_x = name in ("own_x", "other_x")
+        if row >= (9 if along_x else 10):
+            return row_of(outer_coef, index, row - 9)
+        first = jnp.where(mirror.up, row, 10 - row) if along_x else mirror.row(row)
+        return coef[index, pl.ds(pl.multiple_of(first * ROWS, ROWS), ROWS), :]
+
+    def slot(row):
+        up, down = EDGES.index(row), EDGES.index(11 - row)
+        return pl.ds(pl.multiple_of(jnp.where(mirror.up, up, down) * ROWS, ROWS), ROWS)
+
+    def then_row(f, row):
+        return edge[f, slot(row), :] if row > 8 else mirror.of(then, f, row)
+
+    sums = {}
+    for e in range(events):
+        apply = Event(lambda c, row, e=e: field_row(3 * e + c, row)).operator(faces, mirror.sign)
+        for row in (9, 10):
+            scale = STEP_FACTOR * medium_row(BUOY, row)
+            for c, result in enumerate(apply(row)):
+                f = 3 * e + c
+                first = outer_start[pl.ds(f * ROWS, ROWS), :] if row == 10 else mirror.of(start, f, 9)
+                edge[f, slot(row), :] = first + scale * result
+                edge[f, slot(11 - row), :] = mirror.of(then, f, 11 - row)
+        second = Event(lambda c, row, e=e: then_row(3 * e + c, row))
+        wave = Event(lambda c, row, e=e: mirror.of(stored, 2 * (3 * e + c) + 1, row))
+        for row in (8, 9):
+            gather(sums, second, wave, fwd, e, 1, row, mirror.row(row) - 2)
+    total[...] = part[...]
+    for row in (8, 9):
+        mirror.add(total, sums, med, row)
+    grads = [total[pl.ds(8 * k, 8), :] for k in range(16)]
+    cut(grads, shares, slabs, own_share, sent)
 
 
 def second_kernel(events, now, med, cells, force, medium, coef, then, edge, mid, after):
@@ -645,15 +785,18 @@
     )(now, base, fwd, med, *x_messages, *y_messages, *arrival)
     slab = ((16 // shares * 8, depth), F32)
     outer = ((fields, len(OUTER) * ROWS, depth), F32)
+    if one_sided(x_rounds):
+        edge_step, scratch = near_kernel, (fields * 2, fields, 4 * 2, 3, ((2 * tile, depth), F32))
+    else:
+        edge_step, scratch = edge_kernel, (fields * 4, fields * 4, 4 * 4, 5)
     edge, own_share, *sent = call(
-        functools.partial(edge_kernel, events, x_rounds, y_rounds, shares),
+        functools.partial(edge_step, events, x_rounds, y_rounds, shares),
         [outer] + [slab] * shares,
         [pltpu.VMEM] * (9 + len(corners)),
         [
-            ((fields * len(OUTER) * ROWS, depth), F32),
-            ((fields * len(OUTER) * ROWS, depth), F32),
-            ((4 * len(OUTER) * ROWS, depth), F32),
-            ((len(COEFFICIENTS), 5 * ROWS, depth), F32),
+            *(((rows * ROWS, depth), F32) for rows in scratch[:3]),
+            ((len(COEFFICIENTS), scratch[3] * ROWS, depth), F32),
+            *scratch[4:],
             ((shares,) + slab[0], F32),
         ],
         "edges",

time: 17.6 us -> 17.3 us (0.983)
  waiting for transfers between devices: 3.1 us -> 2.86 us
    pallas_call x1, Pallas kernels: 0.67 us -> 0.42 us  [body(): call(functools.partial(edge_step, events, x_rounds, y_rounds, shares), [o...]
    pallas_call x1, Pallas kernels: 1.1 us -> 1.34 us  [body(): call(functools.partial(inner_kernel, events, x_rounds, y_rounds), [wide,...]
    ppermute x5, waiting for transfers between devices: 2.08 us -> 1.84 us  [swap(): return lax.ppermute(values, names, pairs)]
  transfers between devices with their start and end apart: 8 -> 8, of which waited for: 3 -> 3; matrix products, arithmetic and copies ran while one was open for 0% -> 0% of each run, Pallas kernels for 13% -> 14%
where the time goes in v7:
time: 17.3 us; the launch traced here: 17.2 us
  starting transfers between devices  8.54 us (49%)
  Pallas kernels  5.11 us (30%)
  waiting for transfers between devices  2.86 us (17%)
  between operations  0.68 us (4%)
    ppermute x5, starting transfers between devices, swap(): return lax.ppermute(values, names, pairs)  5.47 us
    ppermute x3, starting transfers between devices, body(): pieces.append(lax.ppermute(sent[m - 1], 'ev', pairs))  3.07 us
    ppermute x5, waiting for transfers between devices, swap(): return lax.ppermute(values, names, pairs)  1.84 us
    pallas_call x1, Pallas kernels, body(): call(functools.partial(pack_kernel, events, x_rounds, y_rounds), [(a.shap...  1.55 us
    pallas_call x1, Pallas kernels, body(): call(functools.partial(inner_kernel, events, x_rounds, y_rounds), [wide,...  1.34 us
    pallas_call x1, Pallas kernels, body(): call(functools.partial(second_kernel, events), [flat, flat], [pltpu.VMEM]...  1.1 us
    ppermute x3, waiting for transfers between devices, body(): pieces.append(lax.ppermute(sent[m - 1], 'ev', pairs))  1.02 us
    pallas_call x1, Pallas kernels, body(): call(functools.partial(finish_kernel, shares, 1.0 / (events * shares)), [...  0.7 us
  transfers between devices with their start and end apart: 8, of which 3 were waited for; matrix products, arithmetic and copies ran while one was open for 0% of the time, Pallas kernels for 14%

profile of v7, /device:TPU:9, one launch (start us, length us, event | category | flops | bytes accessed | tf_op | source)
XLA Modules:
  0.0 17.2 jit_solution(8523866774747389054)
XLA Ops:
  0.6 1.6 %pack.1 = (f32[384,128]{1,0:T(8,128)S(1)}, bf16[24,8,8,128]{3,2,1,0:T(8,128)(2,1)S(1)}, f32[256,128]{1,0:T(8,128)S(1)}, s32[1,1,128]{2,1,0:T(1,128)S(1)}, f32[2,...) custom-call(f32[384,128]{1,0:T(8,128)} %bitcast.9, ...), custom_call_target="tpu_custom_call" | custom-call | flops 8192000 | bytes 8192000 | tf_op jit(solution)/shard_map/pack/pallas_call | solution.py:744
  2.2 1.4 %collective-permute-start.2 = (bf16[28,16,128]{2,1,0:T(8,128)(2,1)S(1)}, bf16[28,16,128]{2,1,0:T(8,128)(2,1)S(1)}, u32[]{:S(2)}, u32[]{:S(2)}) collective-permute-start(bf16[28,16,128]{2,1,0:T(8,128)(2,1)S(1)} %get-tuple-element.39), channel_id=1, source_target_pairs={{0,4},{1,2},{2,1},{3,11},{4,0},{5,6},{6,5},{7,15},{8,12},{9,10},{1... | collective-permute-start | bytes 344072 | tf_op jit(solution)/shard_map/ppermute | solution.py:37
  3.6 0.1 collective-permute-start.1
  3.7 1.1 %collective-permute-start = (bf16[28,16,128]{2,1,0:T(8,128)(2,1)S(1)}, bf16[28,16,128]{2,1,0:T(8,128)(2,1)S(1)}, u32[]{:S(2)}, u32[]{:S(2)}) collective-permute-start(bf16[28,16,128]{2,1,0:T(8,128)(2,1)S(1)} %get-tuple-element.37), channel_id=1, source_target_pairs={{0,8},{1,5},{2,6},{3,7},{4,12},{5,1},{6,2},{7,3},{8,0},{9,13},{10,... | collective-permute-start | bytes 344072 | tf_op jit(solution)/shard_map/ppermute | solution.py:37
  4.8 2.4 %collective-permute-start.3 = (f32[2,2,16,128]{3,2,1,0:T(8,128)S(1)}, f32[2,2,16,128]{3,2,1,0:T(8,128)S(1)}, u32[]{:S(2)}, u32[]{:S(2)}) collective-permute-start(f32[2,2,16,128]{3,2,1,0:T(8,128)S(1)} %get-tuple-element.43), channel_id=1, source_target_pairs={{0,5},{1,4},{2,7},{3,6},{4,1},{5,0},{6,3},{7,2},{8,13},{9,12},{10,... | collective-permute-start | bytes 98312 | tf_op jit(solution)/shard_map/ppermute | solution.py:37
  7.2 0.5 %collective-permute-start.4 = (f32[2,2,16,128]{3,2,1,0:T(8,128)S(1)}, f32[2,2,16,128]{3,2,1,0:T(8,128)S(1)}, u32[]{:S(2)}, u32[]{:S(2)}) collective-permute-start(f32[2,2,16,128]{3,2,1,0:T(8,128)S(1)} %get-tuple-element.44), channel_id=1, source_target_pairs={{0,8},{1,6},{2,5},{3,11},{4,12},{5,2},{6,1},{7,15},{8,0},{9,14},{1... | collective-permute-start | bytes 98312 | tf_op jit(solution)/shard_map/ppermute | solution.py:37
  7.7 0.0 collective-permute-done.2.refs_0_.refs_2_
  7.7 0.0 collective-permute-done.1.refs_1_
  7.7 0.0 collective-permute-done.refs_0_
  7.7 1.3 %inner.1 = (f32[6,192,128]{2,1,0:T(8,128)S(1)}, f32[6,192,128]{2,1,0:T(8,128)S(1)}, f32[12,192,128]{2,1,0:T(8,128)S(1)}, f32[4,192,128]{2,1,0:T(8,128)S(1)}, f32...) custom-call(f32[384,128]{1,0:T(8,128)S(1)} %get-tuple-element.31.now, ...), custom_call_target="tpu_custom_call" | custom-call | flops 3072000 | bytes 3072000 | tf_op jit(solution)/shard_map/inner/pallas_call | solution.py:771
  9.0 0.0 collective-permute-done.3.refs_0_
  9.0 1.8 %collective-permute-done.4.refs_1_ = f32[2,2,16,128]{3,2,1,0:T(8,128)S(1)} collective-permute-done((f32[2,2,16,128]{3,2,1,0:T(8,128)S(1)}, f32[2,2,16,128]{3,2,1,0:T(8,128)S(1)}, u32[]{:S(2)}, u32[]{:S(2)}) %collective-permute-start.4) | collective-permute-done | bytes 32800 | tf_op jit(solution)/shard_map/ppermute | solution.py:37
  10.9 0.4 %edges.1 = (f32[6,64,128]{2,1,0:T(8,128)S(1)}, f32[32,128]{1,0:T(8,128)S(1)}, f32[32,128]{1,0:T(8,128)S(1)}, f32[32,128]{1,0:T(8,128)S(1)}, f32[32,128]{1,0:T(8,128)S(1)}) custom-call(f32[2,2,16,128]{3,2,1,0:T(8,128)S(1)} %collective-permute-done.3.refs_0_, f32[2,2,16,128]{3,2,1,0:T(8,128)S(1)} %collective-permute-done.4.refs_1_, ...), custom_call_target="tpu_custom_call" | custom-call | flops 1024000 | bytes 1024000 | tf_op jit(solution)/shard_map/edges/pallas_call | solution.py:792
  11.3 2.6 %collective-permute-start.5 = (f32[32,128]{1,0:T(8,128)S(1)}, f32[32,128]{1,0:T(8,128)S(1)}, u32[]{:S(2)}, u32[]{:S(2)}) collective-permute-start(f32[32,128]{1,0:T(8,128)S(1)} %get-tuple-element.53), channel_id=1, source_target_pairs={{0,24},{8,16},{16,8},{24,0},{1,25},{9,17},{17,9},{25,1},{2,26},{10... | collective-permute-start | bytes 49160 | tf_op jit(solution)/shard_map/ppermute | solution.py:807
  13.9 0.3 %collective-permute-start.6 = (f32[32,128]{1,0:T(8,128)S(1)}, f32[32,128]{1,0:T(8,128)S(1)}, u32[]{:S(2)}, u32[]{:S(2)}) collective-permute-start(f32[32,128]{1,0:T(8,128)S(1)} %get-tuple-element.54), channel_id=1, source_target_pairs={{0,16},{8,24},{16,0},{24,8},{1,17},{9,25},{17,1},{25,9},{2,18},{10... | collective-permute-start | bytes 49160 | tf_op jit(solution)/shard_map/ppermute | solution.py:807
  14.1 0.2 %collective-permute-start.7 = (f32[32,128]{1,0:T(8,128)S(1)}, f32[32,128]{1,0:T(8,128)S(1)}, u32[]{:S(2)}, u32[]{:S(2)}) collective-permute-start(f32[32,128]{1,0:T(8,128)S(1)} %get-tuple-element.55), channel_id=1, source_target_pairs={{0,8},{8,0},{16,24},{24,16},{1,9},{9,1},{17,25},{25,17},{2,10},{10... | collective-permute-start | bytes 49160 | tf_op jit(solution)/shard_map/ppermute | solution.py:807
  14.4 1.1 %second.1 = (f32[384,128]{1,0:T(8,128)}, f32[384,128]{1,0:T(8,128)}) custom-call(f32[384,128]{1,0:T(8,128)S(1)} %get-tuple-element.31.now, f32[256,128]{1,0:T(8,128)S(1)} %get-tuple-element.32.med.refs_10_, s32[1,1,128]{2,1,0:T(1,128)S(1)} %get-tuple-element.33.cells, f32[2,2,3,1,1,128]{5,4,3,2,1,0:T(1,128)S(1)} %get-tuple-element.34.force, ...), custom_call_target="tpu_custom_call" | custom-call | flops 1024000 | bytes 1024000 | tf_op jit(solution)/shard_map/second/pallas_call | solution.py:808
  15.5 0.2 %collective-permute-done.5.refs_1_ = f32[32,128]{1,0:T(8,128)S(1)} collective-permute-done((f32[32,128]{1,0:T(8,128)S(1)}, f32[32,128]{1,0:T(8,128)S(1)}, u32[]{:S(2)}, u32[]{:S(2)}) %collective-permute-start.5) | collective-permute-done | bytes 16416 | tf_op jit(solution)/shard_map/ppermute | solution.py:807
  15.7 0.8 %collective-permute-done.6.refs_2_ = f32[32,128]{1,0:T(8,128)S(1)} collective-permute-done((f32[32,128]{1,0:T(8,128)S(1)}, f32[32,128]{1,0:T(8,128)S(1)}, u32[]{:S(2)}, u32[]{:S(2)}) %collective-permute-start.6) | collective-permute-done | bytes 16416 | tf_op jit(solution)/shard_map/ppermute | solution.py:807
  16.5 0.0 collective-permute-done.7.refs_3_
  16.5 0.7 %finish.1 = (f32[64,32]{1,0:T(8,128)}, f32[64,32]{1,0:T(8,128)}) custom-call(f32[32,128]{1,0:T(8,128)S(1)} %get-tuple-element.52.refs_0_, f32[32,128]{1,0:T(8,128)S(1)} %collective-permute-done.5.refs_1_, f32[32,128]{1,0:T(8,128)S(1)} %collective-permute-done.6.refs_2_, f32[32,128]{1,0:T(8,128)S(1)} %collective-permute-done.7.refs_3_), custom_call_target="tpu_custom_call" | custom-call | flops 1024000 | bytes 1024000 | tf_op jit(solution)/shard_map/finish/pallas_call | solution.py:814
  (2 shorter events, 0.0 us)
Async XLA Ops:
  2.2 5.5 %collective-permute-start.2 = (bf16[28,16,128]{2,1,0:T(8,128)(2,1)S(1)}, bf16[28,16,128]{2,1,0:T(8,128)(2,1)S(1)}, u32[]{:S(2)}, u32[]{:S(2)}) collective-permute-start(bf16[28,16,128]{2,1,0:T(8,128)(2,1)S(1)} %get-tuple-element.39), channel_id=1, source_target_pairs={{0,4},{1,2},{2,1},{3,11},{4,0},{5,6},{6,5},{7,15},{8,12},{9,10},{1... | collective-permute-start | bytes 344072 | tf_op jit(solution)/shard_map/ppermute | solution.py:37
  3.6 4.1 %collective-permute-start.1 = (bf16[28,16,128]{2,1,0:T(8,128)(2,1)S(1)}, bf16[28,16,128]{2,1,0:T(8,128)(2,1)S(1)}, u32[]{:S(2)}, u32[]{:S(2)}) collective-permute-start(bf16[28,16,128]{2,1,0:T(8,128)(2,1)S(1)} %get-tuple-element.38), channel_id=1, source_target_pairs={{0,1},{1,0},{2,3},{3,2},{4,5},{5,4},{6,7},{7,6},{8,9},{9,8},{10,11... | collective-permute-start | bytes 344072 | tf_op jit(solution)/shard_map/ppermute | solution.py:37
  3.7 4.0 %collective-permute-start = (bf16[28,16,128]{2,1,0:T(8,128)(2,1)S(1)}, bf16[28,16,128]{2,1,0:T(8,128)(2,1)S(1)}, u32[]{:S(2)}, u32[]{:S(2)}) collective-permute-start(bf16[28,16,128]{2,1,0:T(8,128)(2,1)S(1)} %get-tuple-element.37), channel_id=1, source_target_pairs={{0,8},{1,5},{2,6},{3,7},{4,12},{5,1},{6,2},{7,3},{8,0},{9,13},{10,... | collective-permute-start | bytes 344072 | tf_op jit(solution)/shard_map/ppermute | solution.py:37
  4.8 4.2 %collective-permute-start.3 = (f32[2,2,16,128]{3,2,1,0:T(8,128)S(1)}, f32[2,2,16,128]{3,2,1,0:T(8,128)S(1)}, u32[]{:S(2)}, u32[]{:S(2)}) collective-permute-start(f32[2,2,16,128]{3,2,1,0:T(8,128)S(1)} %get-tuple-element.43), channel_id=1, source_target_pairs={{0,5},{1,4},{2,7},{3,6},{4,1},{5,0},{6,3},{7,2},{8,13},{9,12},{10,... | collective-permute-start | bytes 98312 | tf_op jit(solution)/shard_map/ppermute | solution.py:37
  7.2 3.7 %collective-permute-start.4 = (f32[2,2,16,128]{3,2,1,0:T(8,128)S(1)}, f32[2,2,16,128]{3,2,1,0:T(8,128)S(1)}, u32[]{:S(2)}, u32[]{:S(2)}) collective-permute-start(f32[2,2,16,128]{3,2,1,0:T(8,128)S(1)} %get-tuple-element.44), channel_id=1, source_target_pairs={{0,8},{1,6},{2,5},{3,11},{4,12},{5,2},{6,1},{7,15},{8,0},{9,14},{1... | collective-permute-start | bytes 98312 | tf_op jit(solution)/shard_map/ppermute | solution.py:37
  11.3 4.4 %collective-permute-start.5 = (f32[32,128]{1,0:T(8,128)S(1)}, f32[32,128]{1,0:T(8,128)S(1)}, u32[]{:S(2)}, u32[]{:S(2)}) collective-permute-start(f32[32,128]{1,0:T(8,128)S(1)} %get-tuple-element.53), channel_id=1, source_target_pairs={{0,24},{8,16},{16,8},{24,0},{1,25},{9,17},{17,9},{25,1},{2,26},{10... | collective-permute-start | bytes 49160 | tf_op jit(solution)/shard_map/ppermute | solution.py:807
  13.9 2.6 %collective-permute-start.6 = (f32[32,128]{1,0:T(8,128)S(1)}, f32[32,128]{1,0:T(8,128)S(1)}, u32[]{:S(2)}, u32[]{:S(2)}) collective-permute-start(f32[32,128]{1,0:T(8,128)S(1)} %get-tuple-element.54), channel_id=1, source_target_pairs={{0,16},{8,24},{16,0},{24,8},{1,17},{9,25},{17,1},{25,9},{2,18},{10... | collective-permute-start | bytes 49160 | tf_op jit(solution)/shard_map/ppermute | solution.py:807
  14.1 2.3 %collective-permute-start.7 = (f32[32,128]{1,0:T(8,128)S(1)}, f32[32,128]{1,0:T(8,128)S(1)}, u32[]{:S(2)}, u32[]{:S(2)}) collective-permute-start(f32[32,128]{1,0:T(8,128)S(1)} %get-tuple-element.55), channel_id=1, source_target_pairs={{0,8},{8,0},{16,24},{24,16},{1,9},{9,1},{17,25},{25,17},{2,10},{10... | collective-permute-start | bytes 49160 | tf_op jit(solution)/shard_map/ppermute | solution.py:807

commit v8 on v7

--- a/solution.py
+++ b/solution.py
@@ -55,15 +55,47 @@
     return even if name == "A" else jnp.logical_not(even)
 
 
-def split(values):
-    high = values.astype(BF16)
-    low = (values - high.astype(F32)).astype(BF16)
-    return jnp.concatenate([high, low], axis=0)
-
-
-def join(tile):
-    tile = tile.astype(F32)
-    return tile[:8] + tile[8:]
+def padded(count):
+    return -(-count // 8) * 8
+
+
+def face_parts(fields):
+    parts = []
+    for f in range(fields):
+        for kind in ("field", "base"):
+            parts += [(kind, f, 1, False)] + [(kind, f, 1, True)]
+    parts += [("field", f, 2, False) for f in range(fields)]
+    parts += [("wave", k, 1, False) for k in range(2 * fields)]
+    for m in (SHEAR, LAME, INV):
+        parts += [("medium", m, 1, False), ("medium", m, 2, False)]
+    parts.append(("medium", BUOY, 1, False))
+    return parts
+
+
+def corner_layout(fields):
+    layout, at = [], 0
+    for ring_x in (1, 2):
+        for ring_y in (1, 2):
+            layout.append(("field", ring_x, ring_y, at))
+            at += fields
+            if ring_x == 1 and ring_y == 1:
+                layout.append(("base", ring_x, ring_y, at))
+                at += fields
+            layout.append(("medium", ring_x, ring_y, at))
+            at += 4
+    return layout, -(-at // 16) * 16, -(-at // 16) * 16 + padded(fields) + 8
+
+
+def take_corner(fields, corner, real, spread, put):
+    layout, rows, _ = corner_layout(fields)
+    if corner is not None:
+        spread[pl.ds(0, rows), :] = jnp.where(real, corner[...].astype(F32), 0.0)
+    for kind, ring_x, ring_y, first in layout:
+        count = 8 if kind == "medium" else padded(fields)
+        values = jnp.zeros((count, 128), F32)
+        if corner is not None:
+            values = spread[pl.ds(first, count), :]
+        put(kind, ring_x, ring_y, values)
 
 
 def force_field(cells, force_rows, width):
@@ -87,16 +119,17 @@
     fields = 3 * events
     now_in, prev_in, fwd_in, med_in, cells_in, force_in = refs[:6]
     now, fwd, med, cells, force, base = refs[6:12]
-    messages, (prev, stored, arrived) = refs[12:-3], refs[-3:]
+    messages, (prev, stored, spread, arrived) = refs[12:-4], refs[-4:]
     pairs = [(cells_in, cells), (force_in, force), (now_in, now), (prev_in, prev), (med_in, med)]
     for first, count in ((3, 6), (0, 3), (9, 3)):
         for e in range(events):
             part = pl.ds(e * 12 + first, count)
             pairs.append((fwd_in.at[part], fwd.at[part]))
-    copies = [
-        pltpu.make_async_copy(source, target, arrived.at[k])
-        for k, (source, target) in enumerate(pairs)
-    ]
+    copies = []
+    for k, (source, target) in enumerate(pairs):
+        if target.shape != source.shape:
+            target = target.at[pl.ds(0, source.shape[0])]
+        copies.append(pltpu.make_async_copy(source, target, arrived.at[k]))
     for copy in copies:
         copy.start()
     for copy in copies[:2]:
@@ -114,20 +147,16 @@
             part = fwd[(e * 4 + t + 1) * 3 + c].astype(F32).reshape(64, 128)
             stored[pl.ds((f * 2 + t) * 64, 64), :] = part
 
+    sources = {"field": now, "base": base, "wave": stored, "medium": med}
+
     def fill(message, pick):
-        for f in range(fields):
-            message[2 * f] = split(pick(now, f, 1))
-            message[2 * f + 1] = split(pick(now, f, 2))
-            message[2 * fields + f] = split(pick(base, f, 1))
-            message[3 * fields + f] = jnp.concatenate(
-                [pick(stored, 2 * f, 1), pick(stored, 2 * f + 1, 1)], axis=0
-            ).astype(BF16)
-        for k, m in enumerate((SHEAR, LAME, INV)):
-            message[4 * fields + k] = jnp.concatenate(
-                [pick(med, m, 1), pick(med, m, 2)], axis=0
-            ).astype(BF16)
-        edge = pick(med, BUOY, 1)
-        message[4 * fields + 3] = jnp.concatenate([edge, edge], axis=0).astype(BF16)
+        halves = []
+        for kind, index, ring, remainder in face_parts(fields):
+            value = pick(sources[kind], index, ring)
+            halves.append(value - value.astype(BF16).astype(F32) if remainder else value)
+        halves += [halves[-1]] * (len(halves) % 2)
+        for k in range(0, len(halves), 2):
+            message[k // 2] = jnp.concatenate(halves[k : k + 2], axis=0).astype(BF16)
 
     def face(axis, name, ring):
         return jnp.where(upward(axis, name), 8 - ring, ring - 1)
@@ -156,14 +185,12 @@
     for name_x in x_rounds:
         for name_y in y_rounds:
             message = next(targets)
-            for ring_x in (1, 2):
-                for ring_y in (1, 2):
-                    cell = face("gx", name_x, ring_x) * 8 + face("gy", name_y, ring_y)
-                    target = message.at[ring_x - 1, ring_y - 1]
-                    target[pl.ds(0, fields), :] = now[pl.ds(cell, fields, stride=64), :]
-                    target[pl.ds(fields, 4), :] = med[pl.ds(cell, 4, stride=64), :]
-                    picked = base[pl.ds(cell, fields, stride=64), :]
-                    target[pl.ds(fields + 4, fields), :] = picked
+            layout, rows, _ = corner_layout(fields)
+            for kind, ring_x, ring_y, first in layout:
+                cell = face("gx", name_x, ring_x) * 8 + face("gy", name_y, ring_y)
+                count = 8 if kind == "medium" else padded(fields)
+                spread[pl.ds(first, count), :] = sources[kind][pl.ds(cell, count, stride=64), :]
+            message[...] = spread[pl.ds(0, rows), :].astype(BF16)
     for copy in copies[5 + events :]:
         copy.wait()
 
@@ -314,19 +341,18 @@
         for x in range(8):
             medium[m, pl.ds((x + 2) * ROWS, 8), :] = med[pl.ds(m * 64 + x * 8, 8), :]
 
+    targets = {"field": here, "base": start, "wave": stored, "medium": medium}
+    parts = face_parts(fields)
+
     def place(tile, put):
-        for f in range(fields):
-            put(here, f, 1, join(tile(2 * f)))
-            put(here, f, 2, join(tile(2 * f + 1)))
-            put(start, f, 1, join(tile(2 * fields + f)))
-            both = tile(3 * fields + f).astype(F32)
-            put(stored, 2 * f, 1, both[:8])
-            put(stored, 2 * f + 1, 1, both[8:])
-        for k, m in enumerate((SHEAR, LAME, INV)):
-            both = tile(4 * fields + k).astype(F32)
-            put(medium, m, 1, both[:8])
-            put(medium, m, 2, both[8:])
-        put(medium, BUOY, 1, tile(4 * fields + 3).astype(F32)[:8])
+        whole = functools.cache(lambda k: tile(k).astype(F32))
+        for k, (kind, index, ring, remainder) in enumerate(parts):
+            if remainder:
+                continue
+            value = whole(k // 2)[8 * (k % 2) :][:8]
+            if parts[k + 1 : k + 2] == [(kind, index, ring, True)]:
+                value = value + whole((k + 1) // 2)[8 * ((k + 1) % 2) :][:8]
+            put(targets[kind], index, ring, value)
 
     def nothing(_):
         return jnp.zeros((16, 128), BF16)
@@ -461,7 +487,7 @@
     corners, refs = refs[:count], refs[count:]
     (here, start, stored, medium, coef, then, part, fwd, med), refs = refs[:9], refs[9:]
     edge, own_share, *sent = refs[: 1 + shares]
-    outer, outer_start, outer_medium, outer_coef, slabs = refs[1 + shares :]
+    outer, outer_start, outer_medium, outer_coef, spread, slabs = refs[1 + shares :]
 
     height = len(OUTER) * ROWS
     for k, row in enumerate(OUTER):
@@ -479,22 +505,13 @@
                 corner = corners[kx * len(y_rounds) + ky]
             up_x, up_y = upward("gx", name_x), upward("gy", name_y)
             real = jnp.logical_and(linked("gx", name_x), linked("gy", name_y))
-            for ring_x in (1, 2):
-                for ring_y in (1, 2):
-                    place = jnp.where(up_x, 1 + ring_x, 2 - ring_x)
-                    spot = place * ROWS + y_place(up_y, ring_y)
-
-                    def put(ref, first, count):
-                        values = jnp.zeros((count, 128), F32)
-                        if corner is not None:
-                            values = corner[ring_x - 1, ring_y - 1, pl.ds(first, count), :]
-                            values = jnp.where(real, values, 0.0)
-                        ref[pl.ds(spot, count, stride=height), :] = values
-
-                    put(outer, 0, fields)
-                    put(outer_medium, fields, 4)
-                    if ring_x == 1 and ring_y == 1:
-                        put(outer_start, fields + 4, fields)
+
+            def put(kind, ring_x, ring_y, values):
+                place = jnp.where(up_x, 1 + ring_x, 2 - ring_x)
+                spot = pl.ds(place * ROWS + y_place(up_y, ring_y), values.shape[0], stride=height)
+                {"field": outer, "base": outer_start, "medium": outer_medium}[kind][spot, :] = values
+
+            take_corner(fields, corner, real, spread, put)
 
     def outer_or(ref, full):
         def pick(index, row):
@@ -572,7 +589,7 @@
     corners, refs = refs[: len(y_rounds)], refs[len(y_rounds) :]
     (here, start, stored, medium, coef, then, part, fwd, med), refs = refs[:9], refs[9:]
     edge, own_share, *sent = refs[: 1 + shares]
-    outer, outer_start, outer_medium, outer_coef, total, slabs = refs[1 + shares :]
+    outer, outer_start, outer_medium, outer_coef, spread, total, slabs = refs[1 + shares :]
     mirror = Mirror()
 
     height = 2 * ROWS
@@ -585,19 +602,17 @@
             outer_medium[pl.ds(m * height + k * ROWS, ROWS), :] = mirror.of(medium, m, row)
     for corner, name in zip(corners, y_rounds):
         up_y, real = upward("gy", name), linked("gy", name)
-        for ring_x in (1, 2):
-            for ring_y in (1, 2):
-                place = y_place(up_y, ring_y)
-                spot = (ring_x - 1) * ROWS + place
-
-                def put(ref, spot, first, count, stride):
-                    values = corner[ring_x - 1, ring_y - 1, pl.ds(first, count), :]
-                    ref[pl.ds(spot, count, stride=stride), :] = jnp.where(real, values, 0.0)
-
-                put(outer, spot, 0, fields, height)
-                put(outer_medium, spot, fields, 4, height)
-                if ring_x == 1 and ring_y == 1:
-                    put(outer_start, place, fields + 4, fields, ROWS)
+
+        def put(kind, ring_x, ring_y, values):
+            place = y_place(up_y, ring_y)
+            count = values.shape[0]
+            if kind == "base":
+                outer_start[pl.ds(place, count, stride=ROWS), :] = values
+            else:
+                target = outer if kind == "field" else outer_medium
+                target[pl.ds((ring_x - 1) * ROWS + place, count, stride=height), :] = values
+
+        take_corner(fields, corner, real, spread, put)
 
     def row_with(ref, full):
         def pick(index, row):
@@ -731,8 +746,11 @@
     flat = ((fields * tile, depth), F32)
     tall = 12 * ROWS
 
-    face = ((4 * fields + 4, 16, depth), BF16)
-    corner = ((2, 2, 2 * fields + 4, depth), F32)
+    face = (((len(face_parts(fields)) + 1) // 2, 16, depth), BF16)
+    wide_fields = padded(fields)
+    _, corner_rows, spread_rows = corner_layout(fields)
+    corner, spread = ((corner_rows, depth), BF16), ((spread_rows, depth), F32)
+    roomy = (((wide_fields + 1) * tile, depth), F32)
     inputs = [
         adjoint_now.reshape(flat[0]),
         adjoint_prev.reshape(flat[0]),
@@ -743,12 +761,18 @@
     ]
     now, fwd, med, cells, force, base, *messages = call(
         functools.partial(pack_kernel, events, x_rounds, y_rounds),
-        [(a.shape, a.dtype) for k, a in enumerate(inputs) if k != 1]
-        + [flat]
+        [roomy, (inputs[2].shape, BF16), ((9 * tile, depth), F32)]
+        + [(a.shape, a.dtype) for a in inputs[4:]]
+        + [roomy]
         + [face] * (len(y_rounds) + len(x_rounds))
         + [corner] * (len(x_rounds) * len(y_rounds)),
         [pltpu.HBM] * len(inputs),
-        [flat, ((2 * fields * tile, depth), F32), pltpu.SemaphoreType.DMA((5 + 3 * events,))],
+        [
+            flat,
+            (((2 * fields + 1) * tile, depth), F32),
+            spread,
+            pltpu.SemaphoreType.DMA((5 + 3 * events,)),
+        ],
         "pack",
         cost=8000,
         pinned=True,
@@ -786,17 +810,19 @@
     slab = ((16 // shares * 8, depth), F32)
     outer = ((fields, len(OUTER) * ROWS, depth), F32)
     if one_sided(x_rounds):
-        edge_step, scratch = near_kernel, (fields * 2, fields, 4 * 2, 3, ((2 * tile, depth), F32))
+        edge_step, each, fresh, more = near_kernel, (2, 1, 2), 3, [((2 * tile, depth), F32)]
     else:
-        edge_step, scratch = edge_kernel, (fields * 4, fields * 4, 4 * 4, 5)
+        edge_step, each, fresh, more = edge_kernel, (len(OUTER),) * 3, 5, []
+    room = [wide_fields + 1, wide_fields + 1, 9]
     edge, own_share, *sent = call(
         functools.partial(edge_step, events, x_rounds, y_rounds, shares),
         [outer] + [slab] * shares,
         [pltpu.VMEM] * (9 + len(corners)),
         [
-            *(((rows * ROWS, depth), F32) for rows in scratch[:3]),
-            ((len(COEFFICIENTS), scratch[3] * ROWS, depth), F32),
-            *scratch[4:],
+            *(((count * rows * ROWS, depth), F32) for count, rows in zip(room, each)),
+            ((len(COEFFICIENTS), fresh * ROWS, depth), F32),
+            spread,
+            *more,
             ((shares,) + slab[0], F32),
         ],
         "edges",

time: 17.3 us -> 17.2 us (level)
    ppermute x5, waiting for transfers between devices: 1.84 us -> 1.67 us  [swap(): return lax.ppermute(values, names, pairs)]
where the time goes in v8:
time: 17.2 us; the launch traced here: 17 us
  starting transfers between devices  8.54 us (50%)
  Pallas kernels  5.07 us (29%)
  waiting for transfers between devices  2.7 us (16%)
  between operations  0.68 us (4%)
    ppermute x5, starting transfers between devices, swap(): return lax.ppermute(values, names, pairs)  5.47 us
    ppermute x3, starting transfers between devices, body(): pieces.append(lax.ppermute(sent[m - 1], 'ev', pairs))  3.07 us
    ppermute x5, waiting for transfers between devices, swap(): return lax.ppermute(values, names, pairs)  1.67 us
    pallas_call x1, Pallas kernels, body(): call(functools.partial(pack_kernel, events, x_rounds, y_rounds), [roomy,...  1.58 us
    pallas_call x1, Pallas kernels, body(): call(functools.partial(inner_kernel, events, x_rounds, y_rounds), [wide,...  1.29 us
    pallas_call x1, Pallas kernels, body(): call(functools.partial(second_kernel, events), [flat, flat], [pltpu.VMEM]...  1.08 us
    ppermute x3, waiting for transfers between devices, body(): pieces.append(lax.ppermute(sent[m - 1], 'ev', pairs))  1.04 us
    pallas_call x1, Pallas kernels, body(): call(functools.partial(finish_kernel, shares, 1.0 / (events * shares)), [...  0.7 us
  transfers between devices with their start and end apart: 8, of which 3 were waited for; matrix products, arithmetic and copies ran while one was open for 0% of the time, Pallas kernels for 14%

profile of v8, /device:TPU:9, one launch (start us, length us, event | category | flops | bytes accessed | tf_op | source)
XLA Modules:
  0.0 17.0 jit_solution(13953447617757766595)
XLA Ops:
  0.6 1.6 %pack.1 = (f32[576,128]{1,0:T(8,128)S(1)}, bf16[24,8,8,128]{3,2,1,0:T(8,128)(2,1)S(1)}, f32[576,128]{1,0:T(8,128)S(1)}, s32[1,1,128]{2,1,0:T(1,128)S(1)}, f32[2,...) custom-call(f32[384,128]{1,0:T(8,128)} %bitcast.9, ...), custom_call_target="tpu_custom_call" | custom-call | flops 8192000 | bytes 8192000 | tf_op jit(solution)/shard_map/pack/pallas_call | solution.py:762
  2.2 1.4 %collective-permute-start.2 = (bf16[25,16,128]{2,1,0:T(8,128)(2,1)S(1)}, bf16[25,16,128]{2,1,0:T(8,128)(2,1)S(1)}, u32[]{:S(2)}, u32[]{:S(2)}) collective-permute-start(bf16[25,16,128]{2,1,0:T(8,128)(2,1)S(1)} %get-tuple-element.39), channel_id=1, source_target_pairs={{0,4},{1,2},{2,1},{3,11},{4,0},{5,6},{6,5},{7,15},{8,12},{9,10},{1... | collective-permute-start | bytes 307208 | tf_op jit(solution)/shard_map/ppermute | solution.py:37
  3.6 0.1 collective-permute-start.1
  3.7 1.1 %collective-permute-start = (bf16[25,16,128]{2,1,0:T(8,128)(2,1)S(1)}, bf16[25,16,128]{2,1,0:T(8,128)(2,1)S(1)}, u32[]{:S(2)}, u32[]{:S(2)}) collective-permute-start(bf16[25,16,128]{2,1,0:T(8,128)(2,1)S(1)} %get-tuple-element.37), channel_id=1, source_target_pairs={{0,8},{1,5},{2,6},{3,7},{4,12},{5,1},{6,2},{7,3},{8,0},{9,13},{10,... | collective-permute-start | bytes 307208 | tf_op jit(solution)/shard_map/ppermute | solution.py:37
  4.8 2.4 %collective-permute-start.3 = (bf16[48,128]{1,0:T(8,128)(2,1)S(1)}, bf16[48,128]{1,0:T(8,128)(2,1)S(1)}, u32[]{:S(2)}, u32[]{:S(2)}) collective-permute-start(bf16[48,128]{1,0:T(8,128)(2,1)S(1)} %get-tuple-element.43), channel_id=1, source_target_pairs={{0,5},{1,4},{2,7},{3,6},{4,1},{5,0},{6,3},{7,2},{8,13},{9,12},{10,... | collective-permute-start | bytes 36872 | tf_op jit(solution)/shard_map/ppermute | solution.py:37
  7.2 0.5 %collective-permute-start.4 = (bf16[48,128]{1,0:T(8,128)(2,1)S(1)}, bf16[48,128]{1,0:T(8,128)(2,1)S(1)}, u32[]{:S(2)}, u32[]{:S(2)}) collective-permute-start(bf16[48,128]{1,0:T(8,128)(2,1)S(1)} %get-tuple-element.44), channel_id=1, source_target_pairs={{0,8},{1,6},{2,5},{3,11},{4,12},{5,2},{6,1},{7,15},{8,0},{9,14},{1... | collective-permute-start | bytes 36872 | tf_op jit(solution)/shard_map/ppermute | solution.py:37
  7.7 0.0 collective-permute-done.2.refs_0_.refs_2_
  7.7 0.0 collective-permute-done.1.refs_1_
  7.7 0.0 collective-permute-done.refs_0_
  7.7 1.3 %inner.1 = (f32[6,192,128]{2,1,0:T(8,128)S(1)}, f32[6,192,128]{2,1,0:T(8,128)S(1)}, f32[12,192,128]{2,1,0:T(8,128)S(1)}, f32[4,192,128]{2,1,0:T(8,128)S(1)}, f32...) custom-call(f32[576,128]{1,0:T(8,128)S(1)} %get-tuple-element.31.now, ...), custom_call_target="tpu_custom_call" | custom-call | flops 3072000 | bytes 3072000 | tf_op jit(solution)/shard_map/inner/pallas_call | solution.py:795
  9.0 0.0 collective-permute-done.3.refs_0_
  9.0 1.7 %collective-permute-done.4.refs_1_ = bf16[48,128]{1,0:T(8,128)(2,1)S(1)} collective-permute-done((bf16[48,128]{1,0:T(8,128)(2,1)S(1)}, bf16[48,128]{1,0:T(8,128)(2,1)S(1)}, u32[]{:S(2)}, u32[]{:S(2)}) %collective-permute-start.4) | collective-permute-done | bytes 12320 | tf_op jit(solution)/shard_map/ppermute | solution.py:37
  10.7 0.4 %edges.1 = (f32[6,64,128]{2,1,0:T(8,128)S(1)}, f32[32,128]{1,0:T(8,128)S(1)}, f32[32,128]{1,0:T(8,128)S(1)}, f32[32,128]{1,0:T(8,128)S(1)}, f32[32,128]{1,0:T(8,128)S(1)}) custom-call(bf16[48,128]{1,0:T(8,128)(2,1)S(1)} %collective-permute-done.3.refs_0_, bf16[48,128]{1,0:T(8,128)(2,1)S(1)} %collective-permute-done.4.refs_1_, ...), custom_call_target="tpu_custom_call" | custom-call | flops 1024000 | bytes 1024000 | tf_op jit(solution)/shard_map/edges/pallas_call | solution.py:817
  11.1 2.6 %collective-permute-start.5 = (f32[32,128]{1,0:T(8,128)S(1)}, f32[32,128]{1,0:T(8,128)S(1)}, u32[]{:S(2)}, u32[]{:S(2)}) collective-permute-start(f32[32,128]{1,0:T(8,128)S(1)} %get-tuple-element.53), channel_id=1, source_target_pairs={{0,24},{8,16},{16,8},{24,0},{1,25},{9,17},{17,9},{25,1},{2,26},{10... | collective-permute-start | bytes 49160 | tf_op jit(solution)/shard_map/ppermute | solution.py:833
  13.7 0.3 %collective-permute-start.6 = (f32[32,128]{1,0:T(8,128)S(1)}, f32[32,128]{1,0:T(8,128)S(1)}, u32[]{:S(2)}, u32[]{:S(2)}) collective-permute-start(f32[32,128]{1,0:T(8,128)S(1)} %get-tuple-element.54), channel_id=1, source_target_pairs={{0,16},{8,24},{16,0},{24,8},{1,17},{9,25},{17,1},{25,9},{2,18},{10... | collective-permute-start | bytes 49160 | tf_op jit(solution)/shard_map/ppermute | solution.py:833
  14.0 0.2 %collective-permute-start.7 = (f32[32,128]{1,0:T(8,128)S(1)}, f32[32,128]{1,0:T(8,128)S(1)}, u32[]{:S(2)}, u32[]{:S(2)}) collective-permute-start(f32[32,128]{1,0:T(8,128)S(1)} %get-tuple-element.55), channel_id=1, source_target_pairs={{0,8},{8,0},{16,24},{24,16},{1,9},{9,1},{17,25},{25,17},{2,10},{10... | collective-permute-start | bytes 49160 | tf_op jit(solution)/shard_map/ppermute | solution.py:833
  14.2 1.1 %second.1 = (f32[384,128]{1,0:T(8,128)}, f32[384,128]{1,0:T(8,128)}) custom-call(f32[576,128]{1,0:T(8,128)S(1)} %get-tuple-element.31.now, f32[576,128]{1,0:T(8,128)S(1)} %get-tuple-element.32.med.refs_10_, s32[1,1,128]{2,1,0:T(1,128)S(1)} %get-tuple-element.33.cells, f32[2,2,3,1,1,128]{5,4,3,2,1,0:T(1,128)S(1)} %get-tuple-element.34.force, ...), custom_call_target="tpu_custom_call" | custom-call | flops 1024000 | bytes 1024000 | tf_op jit(solution)/shard_map/second/pallas_call | solution.py:834
  15.3 0.2 %collective-permute-done.5.refs_1_ = f32[32,128]{1,0:T(8,128)S(1)} collective-permute-done((f32[32,128]{1,0:T(8,128)S(1)}, f32[32,128]{1,0:T(8,128)S(1)}, u32[]{:S(2)}, u32[]{:S(2)}) %collective-permute-start.5) | collective-permute-done | bytes 16416 | tf_op jit(solution)/shard_map/ppermute | solution.py:833
  15.5 0.8 %collective-permute-done.6.refs_2_ = f32[32,128]{1,0:T(8,128)S(1)} collective-permute-done((f32[32,128]{1,0:T(8,128)S(1)}, f32[32,128]{1,0:T(8,128)S(1)}, u32[]{:S(2)}, u32[]{:S(2)}) %collective-permute-start.6) | collective-permute-done | bytes 16416 | tf_op jit(solution)/shard_map/ppermute | solution.py:833
  16.3 0.0 collective-permute-done.7.refs_3_
  16.3 0.7 %finish.1 = (f32[64,32]{1,0:T(8,128)}, f32[64,32]{1,0:T(8,128)}) custom-call(f32[32,128]{1,0:T(8,128)S(1)} %get-tuple-element.52.refs_0_, f32[32,128]{1,0:T(8,128)S(1)} %collective-permute-done.5.refs_1_, f32[32,128]{1,0:T(8,128)S(1)} %collective-permute-done.6.refs_2_, f32[32,128]{1,0:T(8,128)S(1)} %collective-permute-done.7.refs_3_), custom_call_target="tpu_custom_call" | custom-call | flops 1024000 | bytes 1024000 | tf_op jit(solution)/shard_map/finish/pallas_call | solution.py:840
  (2 shorter events, 0.0 us)
Async XLA Ops:
  2.2 5.5 %collective-permute-start.2 = (bf16[25,16,128]{2,1,0:T(8,128)(2,1)S(1)}, bf16[25,16,128]{2,1,0:T(8,128)(2,1)S(1)}, u32[]{:S(2)}, u32[]{:S(2)}) collective-permute-start(bf16[25,16,128]{2,1,0:T(8,128)(2,1)S(1)} %get-tuple-element.39), channel_id=1, source_target_pairs={{0,4},{1,2},{2,1},{3,11},{4,0},{5,6},{6,5},{7,15},{8,12},{9,10},{1... | collective-permute-start | bytes 307208 | tf_op jit(solution)/shard_map/ppermute | solution.py:37
  3.6 4.1 %collective-permute-start.1 = (bf16[25,16,128]{2,1,0:T(8,128)(2,1)S(1)}, bf16[25,16,128]{2,1,0:T(8,128)(2,1)S(1)}, u32[]{:S(2)}, u32[]{:S(2)}) collective-permute-start(bf16[25,16,128]{2,1,0:T(8,128)(2,1)S(1)} %get-tuple-element.38), channel_id=1, source_target_pairs={{0,1},{1,0},{2,3},{3,2},{4,5},{5,4},{6,7},{7,6},{8,9},{9,8},{10,11... | collective-permute-start | bytes 307208 | tf_op jit(solution)/shard_map/ppermute | solution.py:37
  3.7 4.0 %collective-permute-start = (bf16[25,16,128]{2,1,0:T(8,128)(2,1)S(1)}, bf16[25,16,128]{2,1,0:T(8,128)(2,1)S(1)}, u32[]{:S(2)}, u32[]{:S(2)}) collective-permute-start(bf16[25,16,128]{2,1,0:T(8,128)(2,1)S(1)} %get-tuple-element.37), channel_id=1, source_target_pairs={{0,8},{1,5},{2,6},{3,7},{4,12},{5,1},{6,2},{7,3},{8,0},{9,13},{10,... | collective-permute-start | bytes 307208 | tf_op jit(solution)/shard_map/ppermute | solution.py:37
  4.8 4.2 %collective-permute-start.3 = (bf16[48,128]{1,0:T(8,128)(2,1)S(1)}, bf16[48,128]{1,0:T(8,128)(2,1)S(1)}, u32[]{:S(2)}, u32[]{:S(2)}) collective-permute-start(bf16[48,128]{1,0:T(8,128)(2,1)S(1)} %get-tuple-element.43), channel_id=1, source_target_pairs={{0,5},{1,4},{2,7},{3,6},{4,1},{5,0},{6,3},{7,2},{8,13},{9,12},{10,... | collective-permute-start | bytes 36872 | tf_op jit(solution)/shard_map/ppermute | solution.py:37
  7.2 3.4 %collective-permute-start.4 = (bf16[48,128]{1,0:T(8,128)(2,1)S(1)}, bf16[48,128]{1,0:T(8,128)(2,1)S(1)}, u32[]{:S(2)}, u32[]{:S(2)}) collective-permute-start(bf16[48,128]{1,0:T(8,128)(2,1)S(1)} %get-tuple-element.44), channel_id=1, source_target_pairs={{0,8},{1,6},{2,5},{3,11},{4,12},{5,2},{6,1},{7,15},{8,0},{9,14},{1... | collective-permute-start | bytes 36872 | tf_op jit(solution)/shard_map/ppermute | solution.py:37
  11.1 4.4 %collective-permute-start.5 = (f32[32,128]{1,0:T(8,128)S(1)}, f32[32,128]{1,0:T(8,128)S(1)}, u32[]{:S(2)}, u32[]{:S(2)}) collective-permute-start(f32[32,128]{1,0:T(8,128)S(1)} %get-tuple-element.53), channel_id=1, source_target_pairs={{0,24},{8,16},{16,8},{24,0},{1,25},{9,17},{17,9},{25,1},{2,26},{10... | collective-permute-start | bytes 49160 | tf_op jit(solution)/shard_map/ppermute | solution.py:833
  13.7 2.6 %collective-permute-start.6 = (f32[32,128]{1,0:T(8,128)S(1)}, f32[32,128]{1,0:T(8,128)S(1)}, u32[]{:S(2)}, u32[]{:S(2)}) collective-permute-start(f32[32,128]{1,0:T(8,128)S(1)} %get-tuple-element.54), channel_id=1, source_target_pairs={{0,16},{8,24},{16,0},{24,8},{1,17},{9,25},{17,1},{25,9},{2,18},{10... | collective-permute-start | bytes 49160 | tf_op jit(solution)/shard_map/ppermute | solution.py:833
  14.0 2.3 %collective-permute-start.7 = (f32[32,128]{1,0:T(8,128)S(1)}, f32[32,128]{1,0:T(8,128)S(1)}, u32[]{:S(2)}, u32[]{:S(2)}) collective-permute-start(f32[32,128]{1,0:T(8,128)S(1)} %get-tuple-element.55), channel_id=1, source_target_pairs={{0,8},{8,0},{16,24},{24,16},{1,9},{9,1},{17,25},{25,17},{2,10},{10... | collective-permute-start | bytes 49160 | tf_op jit(solution)/shard_map/ppermute | solution.py:833

commit v9 on v8

--- a/solution.py
+++ b/solution.py
@@ -122,9 +122,8 @@
     messages, (prev, stored, spread, arrived) = refs[12:-4], refs[-4:]
     pairs = [(cells_in, cells), (force_in, force), (now_in, now), (prev_in, prev), (med_in, med)]
     for first, count in ((3, 6), (0, 3), (9, 3)):
-        for e in range(events):
-            part = pl.ds(e * 12 + first, count)
-            pairs.append((fwd_in.at[part], fwd.at[part]))
+        part = pl.ds(first, count)
+        pairs.append((fwd_in.at[:, part], fwd.at[:, part]))
     copies = []
     for k, (source, target) in enumerate(pairs):
         if target.shape != source.shape:
@@ -136,27 +135,27 @@
         copy.wait()
     rows = [force[e, 0, c, 0] for e in range(events) for c in range(3)]
     pushed = force_field(cells[0], rows, 64)
-    for copy in copies[2 : 5 + events]:
+    for copy in copies[2:5]:
         copy.wait()
     scale = STEP_FACTOR * med[pl.ds(BUOY * 64, 64), :]
     for f in range(fields):
         spot = pl.ds(f * 64, 64)
         base[spot, :] = 2.0 * now[spot, :] - prev[spot, :] + scale * pushed[f * 64 : (f + 1) * 64]
-        e, c = f // 3, f % 3
-        for t in range(2):
-            part = fwd[(e * 4 + t + 1) * 3 + c].astype(F32).reshape(64, 128)
-            stored[pl.ds((f * 2 + t) * 64, 64), :] = part
 
     sources = {"field": now, "base": base, "wave": stored, "medium": med}
 
-    def fill(message, pick):
-        halves = []
-        for kind, index, ring, remainder in face_parts(fields):
-            value = pick(sources[kind], index, ring)
-            halves.append(value - value.astype(BF16).astype(F32) if remainder else value)
-        halves += [halves[-1]] * (len(halves) % 2)
-        for k in range(0, len(halves), 2):
-            message[k // 2] = jnp.concatenate(halves[k : k + 2], axis=0).astype(BF16)
+    parts = face_parts(fields)
+    parts += parts[-1:] * (len(parts) % 2)
+
+    def fill(message, pick, waves):
+        for k in range(0, len(parts), 2):
+            if waves != any(kind == "wave" for kind, *_ in parts[k : k + 2]):
+                continue
+            halves = []
+            for kind, index, ring, remainder in parts[k : k + 2]:
+                value = pick(sources[kind], index, ring)
+                halves.append(value - value.astype(BF16).astype(F32) if remainder else value)
+            message[k // 2] = jnp.concatenate(halves, axis=0).astype(BF16)
 
     def face(axis, name, ring):
         return jnp.where(upward(axis, name), 8 - ring, ring - 1)
@@ -168,30 +167,42 @@
 
         return pick
 
-    targets = iter(messages)
-    for name in y_rounds:
-
-        def pick_y(ref, index, ring, name=name):
+    def pick_y(name):
+        def pick(ref, index, ring):
             return ref[pl.ds(index * 64 + face("gy", name, ring), 8, stride=8), :]
 
-        if name == "B" and their_turn(x_rounds, y_rounds):
-            message = next(targets)
-            pl.when(is_first())(functools.partial(fill, message, pick_x("A")))
-            pl.when(jnp.logical_not(is_first()))(functools.partial(fill, message, pick_y))
-        else:
-            fill(next(targets), pick_y)
-    for name in x_rounds:
-        fill(next(targets), pick_x(name))
+        return pick
+
+    def fill_faces(waves):
+        for message, name in zip(messages, y_rounds):
+            if name == "B" and their_turn(x_rounds, y_rounds):
+                pl.when(is_first())(functools.partial(fill, message, pick_x("A"), waves))
+                other = functools.partial(fill, message, pick_y(name), waves)
+                pl.when(jnp.logical_not(is_first()))(other)
+            else:
+                fill(message, pick_y(name), waves)
+        for message, name in zip(messages[len(y_rounds) :], x_rounds):
+            fill(message, pick_x(name), waves)
+
+    fill_faces(False)
+    corners = iter(messages[len(y_rounds) + len(x_rounds) :])
     for name_x in x_rounds:
         for name_y in y_rounds:
-            message = next(targets)
+            message = next(corners)
             layout, rows, _ = corner_layout(fields)
             for kind, ring_x, ring_y, first in layout:
                 cell = face("gx", name_x, ring_x) * 8 + face("gy", name_y, ring_y)
                 count = 8 if kind == "medium" else padded(fields)
                 spread[pl.ds(first, count), :] = sources[kind][pl.ds(cell, count, stride=64), :]
             message[...] = spread[pl.ds(0, rows), :].astype(BF16)
-    for copy in copies[5 + events :]:
+    copies[5].wait()
+    for f in range(fields):
+        e, c = f // 3, f % 3
+        for t in range(2):
+            part = fwd[e, (t + 1) * 3 + c].astype(F32).reshape(64, 128)
+            stored[pl.ds((f * 2 + t) * 64, 64), :] = part
+    fill_faces(True)
+    for copy in copies[6:]:
         copy.wait()
 
 
@@ -754,7 +765,7 @@
     inputs = [
         adjoint_now.reshape(flat[0]),
         adjoint_prev.reshape(flat[0]),
-        forward.reshape(events * 12, width_x, width_y, depth),
+        forward.reshape(events, 12, width_x, width_y, depth),
         medium.reshape(4 * tile, depth),
         drm_cells,
         drm_force,
@@ -771,7 +782,7 @@
             flat,
             (((2 * fields + 1) * tile, depth), F32),
             spread,
-            pltpu.SemaphoreType.DMA((5 + 3 * events,)),
+            pltpu.SemaphoreType.DMA((8,)),
         ],
         "pack",
         cost=8000,
@@ -779,6 +790,7 @@
     )(*(pltpu.with_memory_space_constraint(a, pltpu.HBM) for a in inputs))
     kinds = [{"gy": r} for r in y_rounds] + [{"gx": r} for r in x_rounds]
     kinds += [{"gx": x, "gy": y} for x in x_rounds for y in y_rounds]
+    fwd = fwd.reshape(events * 12, width_x, width_y, depth)
     turn = their_turn(x_rounds, y_rounds)
     received = [
         swap(message, kind, turn and kind == {"gy": "B"}, turn and kind == {"gx": "A"})

time: 17.2 us -> 17.1 us (level)
  no operation moved by 1% of the time
where the time goes in v9:
time: 17.1 us; the launch traced here: 16.9 us
  starting transfers between devices  8.54 us (50%)
  Pallas kernels  4.98 us (29%)
  waiting for transfers between devices  2.7 us (16%)
  between operations  0.68 us (4%)
    ppermute x5, starting transfers between devices, swap(): return lax.ppermute(values, names, pairs)  5.47 us
    ppermute x3, starting transfers between devices, body(): pieces.append(lax.ppermute(sent[m - 1], 'ev', pairs))  3.07 us
    ppermute x5, waiting for transfers between devices, swap(): return lax.ppermute(values, names, pairs)  1.67 us
    pallas_call x1, Pallas kernels, body(): call(functools.partial(pack_kernel, events, x_rounds, y_rounds), [roomy,...  1.48 us
    pallas_call x1, Pallas kernels, body(): call(functools.partial(inner_kernel, events, x_rounds, y_rounds), [wide,...  1.29 us
    pallas_call x1, Pallas kernels, body(): call(functools.partial(second_kernel, events), [flat, flat], [pltpu.VMEM]...  1.08 us
    ppermute x3, waiting for transfers between devices, body(): pieces.append(lax.ppermute(sent[m - 1], 'ev', pairs))  1.04 us
    pallas_call x1, Pallas kernels, body(): call(functools.partial(finish_kernel, shares, 1.0 / (events * shares)), [...  0.7 us
  transfers between devices with their start and end apart: 8, of which 3 were waited for; matrix products, arithmetic and copies ran while one was open for 0% of the time, Pallas kernels for 14%

profile of v9, /device:TPU:9, one launch (start us, length us, event | category | flops | bytes accessed | tf_op | source)
XLA Modules:
  0.0 16.9 jit_solution(9414576208164564662)
XLA Ops:
  0.6 1.5 %pack.1 = (f32[576,128]{1,0:T(8,128)S(1)}, bf16[2,12,8,8,128]{4,3,2,1,0:T(8,128)(2,1)S(1)}, f32[576,128]{1,0:T(8,128)S(1)}, s32[1,1,128]{2,1,0:T(1,128)S(1)}, f3...) custom-call(f32[384,128]{1,0:T(8,128)} %bitcast.12, ...), custom_call_target="tpu_custom_call" | custom-call | flops 8192000 | bytes 8192000 | tf_op jit(solution)/shard_map/pack/pallas_call | solution.py:773
  2.1 1.4 %collective-permute-start.2 = (bf16[25,16,128]{2,1,0:T(8,128)(2,1)S(1)}, bf16[25,16,128]{2,1,0:T(8,128)(2,1)S(1)}, u32[]{:S(2)}, u32[]{:S(2)}) collective-permute-start(bf16[25,16,128]{2,1,0:T(8,128)(2,1)S(1)} %get-tuple-element.39), channel_id=1, source_target_pairs={{0,4},{1,2},{2,1},{3,11},{4,0},{5,6},{6,5},{7,15},{8,12},{9,10},{1... | collective-permute-start | bytes 307208 | tf_op jit(solution)/shard_map/ppermute | solution.py:37
  3.5 0.1 collective-permute-start.1
  3.6 1.1 %collective-permute-start = (bf16[25,16,128]{2,1,0:T(8,128)(2,1)S(1)}, bf16[25,16,128]{2,1,0:T(8,128)(2,1)S(1)}, u32[]{:S(2)}, u32[]{:S(2)}) collective-permute-start(bf16[25,16,128]{2,1,0:T(8,128)(2,1)S(1)} %get-tuple-element.37), channel_id=1, source_target_pairs={{0,8},{1,5},{2,6},{3,7},{4,12},{5,1},{6,2},{7,3},{8,0},{9,13},{10,... | collective-permute-start | bytes 307208 | tf_op jit(solution)/shard_map/ppermute | solution.py:37
  4.7 2.4 %collective-permute-start.3 = (bf16[48,128]{1,0:T(8,128)(2,1)S(1)}, bf16[48,128]{1,0:T(8,128)(2,1)S(1)}, u32[]{:S(2)}, u32[]{:S(2)}) collective-permute-start(bf16[48,128]{1,0:T(8,128)(2,1)S(1)} %get-tuple-element.43), channel_id=1, source_target_pairs={{0,5},{1,4},{2,7},{3,6},{4,1},{5,0},{6,3},{7,2},{8,13},{9,12},{10,... | collective-permute-start | bytes 36872 | tf_op jit(solution)/shard_map/ppermute | solution.py:37
  7.1 0.5 %collective-permute-start.4 = (bf16[48,128]{1,0:T(8,128)(2,1)S(1)}, bf16[48,128]{1,0:T(8,128)(2,1)S(1)}, u32[]{:S(2)}, u32[]{:S(2)}) collective-permute-start(bf16[48,128]{1,0:T(8,128)(2,1)S(1)} %get-tuple-element.44), channel_id=1, source_target_pairs={{0,8},{1,6},{2,5},{3,11},{4,12},{5,2},{6,1},{7,15},{8,0},{9,14},{1... | collective-permute-start | bytes 36872 | tf_op jit(solution)/shard_map/ppermute | solution.py:37
  7.6 0.0 collective-permute-done.2.refs_0_.refs_2_
  7.6 0.0 collective-permute-done.1.refs_1_
  7.6 0.0 collective-permute-done.refs_0_
  7.6 1.3 %inner.1 = (f32[6,192,128]{2,1,0:T(8,128)S(1)}, f32[6,192,128]{2,1,0:T(8,128)S(1)}, f32[12,192,128]{2,1,0:T(8,128)S(1)}, f32[4,192,128]{2,1,0:T(8,128)S(1)}, f32...) custom-call(f32[576,128]{1,0:T(8,128)S(1)} %get-tuple-element.31.now, ...), custom_call_target="tpu_custom_call" | custom-call | flops 3072000 | bytes 3072000 | tf_op jit(solution)/shard_map/inner/pallas_call | solution.py:807
  8.9 0.0 collective-permute-done.3.refs_0_
  8.9 1.7 %collective-permute-done.4.refs_1_ = bf16[48,128]{1,0:T(8,128)(2,1)S(1)} collective-permute-done((bf16[48,128]{1,0:T(8,128)(2,1)S(1)}, bf16[48,128]{1,0:T(8,128)(2,1)S(1)}, u32[]{:S(2)}, u32[]{:S(2)}) %collective-permute-start.4) | collective-permute-done | bytes 12320 | tf_op jit(solution)/shard_map/ppermute | solution.py:37
  10.6 0.4 %edges.1 = (f32[6,64,128]{2,1,0:T(8,128)S(1)}, f32[32,128]{1,0:T(8,128)S(1)}, f32[32,128]{1,0:T(8,128)S(1)}, f32[32,128]{1,0:T(8,128)S(1)}, f32[32,128]{1,0:T(8,128)S(1)}) custom-call(bf16[48,128]{1,0:T(8,128)(2,1)S(1)} %collective-permute-done.3.refs_0_, bf16[48,128]{1,0:T(8,128)(2,1)S(1)} %collective-permute-done.4.refs_1_, ...), custom_call_target="tpu_custom_call" | custom-call | flops 1024000 | bytes 1024000 | tf_op jit(solution)/shard_map/edges/pallas_call | solution.py:829
  11.0 2.6 %collective-permute-start.5 = (f32[32,128]{1,0:T(8,128)S(1)}, f32[32,128]{1,0:T(8,128)S(1)}, u32[]{:S(2)}, u32[]{:S(2)}) collective-permute-start(f32[32,128]{1,0:T(8,128)S(1)} %get-tuple-element.53), channel_id=1, source_target_pairs={{0,24},{8,16},{16,8},{24,0},{1,25},{9,17},{17,9},{25,1},{2,26},{10... | collective-permute-start | bytes 49160 | tf_op jit(solution)/shard_map/ppermute | solution.py:845
  13.6 0.3 %collective-permute-start.6 = (f32[32,128]{1,0:T(8,128)S(1)}, f32[32,128]{1,0:T(8,128)S(1)}, u32[]{:S(2)}, u32[]{:S(2)}) collective-permute-start(f32[32,128]{1,0:T(8,128)S(1)} %get-tuple-element.54), channel_id=1, source_target_pairs={{0,16},{8,24},{16,0},{24,8},{1,17},{9,25},{17,1},{25,9},{2,18},{10... | collective-permute-start | bytes 49160 | tf_op jit(solution)/shard_map/ppermute | solution.py:845
  13.9 0.2 %collective-permute-start.7 = (f32[32,128]{1,0:T(8,128)S(1)}, f32[32,128]{1,0:T(8,128)S(1)}, u32[]{:S(2)}, u32[]{:S(2)}) collective-permute-start(f32[32,128]{1,0:T(8,128)S(1)} %get-tuple-element.55), channel_id=1, source_target_pairs={{0,8},{8,0},{16,24},{24,16},{1,9},{9,1},{17,25},{25,17},{2,10},{10... | collective-permute-start | bytes 49160 | tf_op jit(solution)/shard_map/ppermute | solution.py:845
  14.1 1.1 %second.1 = (f32[384,128]{1,0:T(8,128)}, f32[384,128]{1,0:T(8,128)}) custom-call(f32[576,128]{1,0:T(8,128)S(1)} %get-tuple-element.31.now, f32[576,128]{1,0:T(8,128)S(1)} %get-tuple-element.32.med.refs_10_, s32[1,1,128]{2,1,0:T(1,128)S(1)} %get-tuple-element.33.cells, f32[2,2,3,1,1,128]{5,4,3,2,1,0:T(1,128)S(1)} %get-tuple-element.34.force, ...), custom_call_target="tpu_custom_call" | custom-call | flops 1024000 | bytes 1024000 | tf_op jit(solution)/shard_map/second/pallas_call | solution.py:846
  15.2 0.2 %collective-permute-done.5.refs_1_ = f32[32,128]{1,0:T(8,128)S(1)} collective-permute-done((f32[32,128]{1,0:T(8,128)S(1)}, f32[32,128]{1,0:T(8,128)S(1)}, u32[]{:S(2)}, u32[]{:S(2)}) %collective-permute-start.5) | collective-permute-done | bytes 16416 | tf_op jit(solution)/shard_map/ppermute | solution.py:845
  15.4 0.8 %collective-permute-done.6.refs_2_ = f32[32,128]{1,0:T(8,128)S(1)} collective-permute-done((f32[32,128]{1,0:T(8,128)S(1)}, f32[32,128]{1,0:T(8,128)S(1)}, u32[]{:S(2)}, u32[]{:S(2)}) %collective-permute-start.6) | collective-permute-done | bytes 16416 | tf_op jit(solution)/shard_map/ppermute | solution.py:845
  16.2 0.0 collective-permute-done.7.refs_3_
  16.2 0.7 %finish.1 = (f32[64,32]{1,0:T(8,128)}, f32[64,32]{1,0:T(8,128)}) custom-call(f32[32,128]{1,0:T(8,128)S(1)} %get-tuple-element.52.refs_0_, f32[32,128]{1,0:T(8,128)S(1)} %collective-permute-done.5.refs_1_, f32[32,128]{1,0:T(8,128)S(1)} %collective-permute-done.6.refs_2_, f32[32,128]{1,0:T(8,128)S(1)} %collective-permute-done.7.refs_3_), custom_call_target="tpu_custom_call" | custom-call | flops 1024000 | bytes 1024000 | tf_op jit(solution)/shard_map/finish/pallas_call | solution.py:852
  (2 shorter events, 0.0 us)
Async XLA Ops:
  2.1 5.5 %collective-permute-start.2 = (bf16[25,16,128]{2,1,0:T(8,128)(2,1)S(1)}, bf16[25,16,128]{2,1,0:T(8,128)(2,1)S(1)}, u32[]{:S(2)}, u32[]{:S(2)}) collective-permute-start(bf16[25,16,128]{2,1,0:T(8,128)(2,1)S(1)} %get-tuple-element.39), channel_id=1, source_target_pairs={{0,4},{1,2},{2,1},{3,11},{4,0},{5,6},{6,5},{7,15},{8,12},{9,10},{1... | collective-permute-start | bytes 307208 | tf_op jit(solution)/shard_map/ppermute | solution.py:37
  3.5 4.1 %collective-permute-start.1 = (bf16[25,16,128]{2,1,0:T(8,128)(2,1)S(1)}, bf16[25,16,128]{2,1,0:T(8,128)(2,1)S(1)}, u32[]{:S(2)}, u32[]{:S(2)}) collective-permute-start(bf16[25,16,128]{2,1,0:T(8,128)(2,1)S(1)} %get-tuple-element.38), channel_id=1, source_target_pairs={{0,1},{1,0},{2,3},{3,2},{4,5},{5,4},{6,7},{7,6},{8,9},{9,8},{10,11... | collective-permute-start | bytes 307208 | tf_op jit(solution)/shard_map/ppermute | solution.py:37
  3.6 4.0 %collective-permute-start = (bf16[25,16,128]{2,1,0:T(8,128)(2,1)S(1)}, bf16[25,16,128]{2,1,0:T(8,128)(2,1)S(1)}, u32[]{:S(2)}, u32[]{:S(2)}) collective-permute-start(bf16[25,16,128]{2,1,0:T(8,128)(2,1)S(1)} %get-tuple-element.37), channel_id=1, source_target_pairs={{0,8},{1,5},{2,6},{3,7},{4,12},{5,1},{6,2},{7,3},{8,0},{9,13},{10,... | collective-permute-start | bytes 307208 | tf_op jit(solution)/shard_map/ppermute | solution.py:37
  4.7 4.2 %collective-permute-start.3 = (bf16[48,128]{1,0:T(8,128)(2,1)S(1)}, bf16[48,128]{1,0:T(8,128)(2,1)S(1)}, u32[]{:S(2)}, u32[]{:S(2)}) collective-permute-start(bf16[48,128]{1,0:T(8,128)(2,1)S(1)} %get-tuple-element.43), channel_id=1, source_target_pairs={{0,5},{1,4},{2,7},{3,6},{4,1},{5,0},{6,3},{7,2},{8,13},{9,12},{10,... | collective-permute-start | bytes 36872 | tf_op jit(solution)/shard_map/ppermute | solution.py:37
  7.1 3.4 %collective-permute-start.4 = (bf16[48,128]{1,0:T(8,128)(2,1)S(1)}, bf16[48,128]{1,0:T(8,128)(2,1)S(1)}, u32[]{:S(2)}, u32[]{:S(2)}) collective-permute-start(bf16[48,128]{1,0:T(8,128)(2,1)S(1)} %get-tuple-element.44), channel_id=1, source_target_pairs={{0,8},{1,6},{2,5},{3,11},{4,12},{5,2},{6,1},{7,15},{8,0},{9,14},{1... | collective-permute-start | bytes 36872 | tf_op jit(solution)/shard_map/ppermute | solution.py:37
  11.0 4.4 %collective-permute-start.5 = (f32[32,128]{1,0:T(8,128)S(1)}, f32[32,128]{1,0:T(8,128)S(1)}, u32[]{:S(2)}, u32[]{:S(2)}) collective-permute-start(f32[32,128]{1,0:T(8,128)S(1)} %get-tuple-element.53), channel_id=1, source_target_pairs={{0,24},{8,16},{16,8},{24,0},{1,25},{9,17},{17,9},{25,1},{2,26},{10... | collective-permute-start | bytes 49160 | tf_op jit(solution)/shard_map/ppermute | solution.py:845
  13.6 2.6 %collective-permute-start.6 = (f32[32,128]{1,0:T(8,128)S(1)}, f32[32,128]{1,0:T(8,128)S(1)}, u32[]{:S(2)}, u32[]{:S(2)}) collective-permute-start(f32[32,128]{1,0:T(8,128)S(1)} %get-tuple-element.54), channel_id=1, source_target_pairs={{0,16},{8,24},{16,0},{24,8},{1,17},{9,25},{17,1},{25,9},{2,18},{10... | collective-permute-start | bytes 49160 | tf_op jit(solution)/shard_map/ppermute | solution.py:845
  13.9 2.3 %collective-permute-start.7 = (f32[32,128]{1,0:T(8,128)S(1)}, f32[32,128]{1,0:T(8,128)S(1)}, u32[]{:S(2)}, u32[]{:S(2)}) collective-permute-start(f32[32,128]{1,0:T(8,128)S(1)} %get-tuple-element.55), channel_id=1, source_target_pairs={{0,8},{8,0},{16,24},{24,16},{1,9},{9,1},{17,25},{25,17},{2,10},{10... | collective-permute-start | bytes 49160 | tf_op jit(solution)/shard_map/ppermute | solution.py:845

commit v10 on v9

--- a/solution.py
+++ b/solution.py
@@ -334,11 +334,15 @@
     sums[key] = sums[key] + value if key in sums else value
 
 
-def inner_kernel(events, x_rounds, y_rounds, now, base, fwd, med, *refs):
+def inner_kernel(events, x_rounds, y_rounds, shares, now, base, fwd, med, *refs):
     fields = 3 * events
     x_messages, refs = refs[: len(x_rounds)], refs[len(x_rounds) :]
     y_messages, refs = refs[: len(y_rounds)], refs[len(y_rounds) :]
-    here, start, stored, medium, coef, then, part = refs[-7:]
+    near = one_sided(x_rounds)
+    if near:
+        here, start, medium, coef, then, slabs, slopes, stored, part = refs[-9:]
+    else:
+        here, start, stored, medium, coef, then, part = refs[-7:]
 
     for f in range(fields):
         e, c = f // 3, f % 3
@@ -368,7 +372,6 @@
     def nothing(_):
         return jnp.zeros((16, 128), BF16)
 
-    near = one_sided(x_rounds)
     if near:
         zeros = jnp.zeros((ROWS, 128), F32)
         for row in (0, 1, 10, 11):
@@ -446,21 +449,39 @@
             wave = Event(lambda c, row, e=e: mirror.of(stored, 2 * (3 * e + c) + 1, row))
             for row in (2, 3):
                 gather(sums, second, wave, fwd, e, 1, row, mirror.row(row) - 2)
+            for row in (8, 9):
+                for c in range(3):
+                    terms = (*wave.slopes(c, row), bend_of(wave, fwd, e, 1, c, row, mirror.row(row) - 2))
+                    for k, term in enumerate(terms):
+                        slopes[slope_place(events, e, c, row, k), :] = term
         for row in (2, 3):
             mirror.add(part, sums, med, row)
+        cut([part[pl.ds(8 * k, 8), :] for k in range(16)], shares, slabs)
+
+
+def bend_of(wave, fwd, e, t, c, row, x):
+    newer = fwd[(e * 4 + t) * 3 + c, x].astype(F32)
+    older = fwd[(e * 4 + t + 2) * 3 + c, x].astype(F32)
+    return newer - 2.0 * wave.value(c, row)[:8] + older
+
+
+def slope_place(events, e, c, row, k):
+    return pl.ds((((row - 8) * events + e) * 3 + c) * 32 + k * 8, 8)
 
 
 def gather(sums, field, wave, fwd, e, t, row, x=None):
     x = row - 2 if x is None else x
     for c in range(3):
-        ax, ay, az = field.slopes(c, row)
-        ux, uy, uz = wave.slopes(c, row)
-        newer = fwd[(e * 4 + t) * 3 + c, x].astype(F32)
-        older = fwd[(e * 4 + t + 2) * 3 + c, x].astype(F32)
-        bend = newer - 2.0 * wave.value(c, row)[:8] + older
-        add_to(sums, ("lateral", row), ax * ux + ay * uy)
-        add_to(sums, ("upright", row), az * uz)
-        add_to(sums, ("density", row), field.value(c, row)[:8] * bend)
+        terms = (*wave.slopes(c, row), bend_of(wave, fwd, e, t, c, row, x))
+        gather_terms(sums, field, terms, c, row)
+
+
+def gather_terms(sums, field, terms, c, row):
+    ax, ay, az = field.slopes(c, row)
+    ux, uy, uz, bend = terms
+    add_to(sums, ("lateral", row), ax * ux + ay * uy)
+    add_to(sums, ("upright", row), az * uz)
+    add_to(sums, ("density", row), field.value(c, row)[:8] * bend)
 
 
 def one_sided(x_rounds):
@@ -480,10 +501,13 @@
     def tile(self, index, row):
         return pl.ds(pl.multiple_of(index * 64 + (self.row(row) - 2) * 8, 8), 8)
 
-    def add(self, part, sums, med, row):
+    def terms(self, sums, med, row):
         inverse = med[self.tile(INV, row), :]
         more = sums["lateral", row] + inverse * inverse * sums["upright", row]
-        for index, value in ((0, -0.25 * more), (1, -sums["density", row])):
+        return -0.25 * more, -sums["density", row]
+
+    def add(self, part, sums, med, row):
+        for index, value in enumerate(self.terms(sums, med, row)):
             spot = self.tile(index, row)
             part[spot, :] = part[spot, :] + value
 
@@ -574,10 +598,11 @@
             density = density - sums["density", row]
         grads[0].append(shear)
         grads[1].append(density)
-    cut(grads[0] + grads[1], shares, slabs, own_share, sent)
-
-
-def cut(grads, shares, slabs, own_share, sent):
+    cut(grads[0] + grads[1], shares, slabs)
+    deal(shares, slabs, own_share, sent)
+
+
+def cut(grads, shares, slabs):
     piece = 128 // shares
     quarter = lax.broadcasted_iota(jnp.int32, (8, 128), 1) // piece
     per = len(grads) // shares
@@ -589,6 +614,9 @@
                 moved = pltpu.roll(source, ((g - j) * piece) % 128, axis=1) if g != j else source
                 tile = moved if tile is None else jnp.where(quarter == g, moved, tile)
             slabs[j, pl.ds(r * 8, 8), :] = tile
+
+
+def deal(shares, slabs, own_share, sent):
     me = lax.axis_index("ev")
     own_share[...] = slabs[me]
     for m in range(1, shares):
@@ -598,9 +626,9 @@
 def near_kernel(events, x_rounds, y_rounds, shares, *refs):
     fields = 3 * events
     corners, refs = refs[: len(y_rounds)], refs[len(y_rounds) :]
-    (here, start, stored, medium, coef, then, part, fwd, med), refs = refs[:9], refs[9:]
+    (here, start, medium, coef, then, ready, slopes, med), refs = refs[:8], refs[8:]
     edge, own_share, *sent = refs[: 1 + shares]
-    outer, outer_start, outer_medium, outer_coef, spread, total, slabs = refs[1 + shares :]
+    outer, outer_start, outer_medium, outer_coef, spread, slabs = refs[1 + shares :]
     mirror = Mirror()
 
     height = 2 * ROWS
@@ -667,14 +695,25 @@
                 edge[f, slot(row), :] = first + scale * result
                 edge[f, slot(11 - row), :] = mirror.of(then, f, 11 - row)
         second = Event(lambda c, row, e=e: then_row(3 * e + c, row))
-        wave = Event(lambda c, row, e=e: mirror.of(stored, 2 * (3 * e + c) + 1, row))
         for row in (8, 9):
-            gather(sums, second, wave, fwd, e, 1, row, mirror.row(row) - 2)
-    total[...] = part[...]
-    for row in (8, 9):
-        mirror.add(total, sums, med, row)
-    grads = [total[pl.ds(8 * k, 8), :] for k in range(16)]
-    cut(grads, shares, slabs, own_share, sent)
+            for c in range(3):
+                terms = [slopes[slope_place(events, e, c, row, k), :] for k in range(4)]
+                gather_terms(sums, second, terms, c, row)
+    piece = 128 // shares
+    quarter = lax.broadcasted_iota(jnp.int32, (8, 128), 1) // piece
+    slabs[...] = ready[...]
+    rows = {row: mirror.terms(sums, med, row) for row in (8, 9)}
+    for index in range(2):
+        tile = index * (8 // shares) + (mirror.row(9) - 2) // shares
+        spot = pl.ds(pl.multiple_of(tile * 8, 8), 8)
+        for j in range(shares):
+            values = slabs[j, spot, :]
+            for row in (8, 9):
+                g = lax.rem(mirror.row(row) - 2, shares)
+                moved = pltpu.roll(rows[row][index], lax.rem((g - j + shares) * piece, 128), axis=1)
+                values = values + jnp.where(quarter == g, moved, 0.0)
+            slabs[j, spot, :] = values
+    deal(shares, slabs, own_share, sent)
 
 
 def second_kernel(events, now, med, cells, force, medium, coef, then, edge, mid, after):
@@ -804,41 +843,40 @@
         arrival = wait_for(arrival, [message])
 
     wide = ((fields, tall, depth), F32)
-    here, start, stored, tall_medium, coef, then, part = call(
-        functools.partial(inner_kernel, events, x_rounds, y_rounds),
-        [
-            wide,
-            wide,
-            ((2 * fields, tall, depth), F32),
-            ((4, tall, depth), F32),
-            ((len(COEFFICIENTS), tall, depth), F32),
-            wide,
-            ((2 * tile, depth), F32),
-        ],
+    slab = ((16 // shares * 8, depth), F32)
+    whole, near = ((2 * tile, depth), F32), one_sided(x_rounds)
+    waves = ((2 * fields, tall, depth), F32)
+    results = call(
+        functools.partial(inner_kernel, events, x_rounds, y_rounds, shares),
+        [wide, wide]
+        + ([] if near else [waves])
+        + [((4, tall, depth), F32), ((len(COEFFICIENTS), tall, depth), F32), wide]
+        + ([((shares,) + slab[0], F32), ((fields * 64, depth), F32)] if near else [whole]),
         [pltpu.VMEM] * (4 + len(x_messages) + len(y_messages)) + [pl.ANY] * len(arrival),
+        [waves, whole] if near else (),
         name="inner",
         cost=3000,
     )(now, base, fwd, med, *x_messages, *y_messages, *arrival)
-    slab = ((16 // shares * 8, depth), F32)
     outer = ((fields, len(OUTER) * ROWS, depth), F32)
-    if one_sided(x_rounds):
-        edge_step, each, fresh, more = near_kernel, (2, 1, 2), 3, [((2 * tile, depth), F32)]
+    if near:
+        edge_step, each, fresh, operands = near_kernel, (2, 1, 2), 3, [*results, med]
+        _, _, tall_medium, coef, then, *_ = results
     else:
-        edge_step, each, fresh, more = edge_kernel, (len(OUTER),) * 3, 5, []
+        edge_step, each, fresh, operands = edge_kernel, (len(OUTER),) * 3, 5, [*results, fwd, med]
+        _, _, _, tall_medium, coef, then, _ = results
     room = [wide_fields + 1, wide_fields + 1, 9]
     edge, own_share, *sent = call(
         functools.partial(edge_step, events, x_rounds, y_rounds, shares),
         [outer] + [slab] * shares,
-        [pltpu.VMEM] * (9 + len(corners)),
+        [pltpu.VMEM] * (len(operands) + len(corners)),
         [
             *(((count * rows * ROWS, depth), F32) for count, rows in zip(room, each)),
             ((len(COEFFICIENTS), fresh * ROWS, depth), F32),
             spread,
-            *more,
             ((shares,) + slab[0], F32),
         ],
         "edges",
-    )(*corners, here, start, stored, tall_medium, coef, then, part, fwd, med)
+    )(*corners, *operands)
     pieces = [own_share]
     for m in reversed(range(1, shares)):
         pairs = [(i, i ^ m) for i in range(shares)]

time: 17.1 us -> 17 us (level)
  waiting for transfers between devices: 2.7 us -> 2.49 us
    ppermute x5, waiting for transfers between devices: 1.67 us -> 1.48 us  [swap(): return lax.ppermute(values, names, pairs)]
    pallas_call x1, Pallas kernels: 1.29 us -> 1.48 us  [body(): call(functools.partial(inner_kernel, events, x_rounds, y_rounds, shares),...]
  transfers between devices with their start and end apart: 8 -> 8, of which waited for: 3 -> 3; matrix products, arithmetic and copies ran while one was open for 0% -> 0% of each run, Pallas kernels for 14% -> 15%
where the time goes in v10:
time: 17 us; the launch traced here: 16.8 us
  starting transfers between devices  8.54 us (50%)
  Pallas kernels  5.11 us (30%)
  waiting for transfers between devices  2.49 us (15%)
  between operations  0.68 us (4%)
    ppermute x5, starting transfers between devices, swap(): return lax.ppermute(values, names, pairs)  5.47 us
    ppermute x3, starting transfers between devices, body(): pieces.append(lax.ppermute(sent[m - 1], 'ev', pairs))  3.07 us
    pallas_call x1, Pallas kernels, body(): call(functools.partial(pack_kernel, events, x_rounds, y_rounds), [roomy,...  1.48 us
    pallas_call x1, Pallas kernels, body(): call(functools.partial(inner_kernel, events, x_rounds, y_rounds, shares),...  1.48 us
    ppermute x5, waiting for transfers between devices, swap(): return lax.ppermute(values, names, pairs)  1.48 us
    pallas_call x1, Pallas kernels, body(): call(functools.partial(second_kernel, events), [flat, flat], [pltpu.VMEM]...  1.1 us
    ppermute x3, waiting for transfers between devices, body(): pieces.append(lax.ppermute(sent[m - 1], 'ev', pairs))  1.02 us
    pallas_call x1, Pallas kernels, body(): call(functools.partial(finish_kernel, shares, 1.0 / (events * shares)), [...  0.7 us
  transfers between devices with their start and end apart: 8, of which 3 were waited for; matrix products, arithmetic and copies ran while one was open for 0% of the time, Pallas kernels for 15%

profile of v10, /device:TPU:9, one launch (start us, length us, event | category | flops | bytes accessed | tf_op | source)
XLA Modules:
  0.0 16.8 jit_solution(6069812104256845251)
XLA Ops:
  0.6 1.5 %pack.1 = (f32[576,128]{1,0:T(8,128)S(1)}, bf16[2,12,8,8,128]{4,3,2,1,0:T(8,128)(2,1)S(1)}, f32[576,128]{1,0:T(8,128)S(1)}, s32[1,1,128]{2,1,0:T(1,128)S(1)}, f3...) custom-call(f32[384,128]{1,0:T(8,128)} %bitcast.11, ...), custom_call_target="tpu_custom_call" | custom-call | flops 8192000 | bytes 8192000 | tf_op jit(solution)/shard_map/pack/pallas_call | solution.py:812
  2.1 1.4 %collective-permute-start.2 = (bf16[25,16,128]{2,1,0:T(8,128)(2,1)S(1)}, bf16[25,16,128]{2,1,0:T(8,128)(2,1)S(1)}, u32[]{:S(2)}, u32[]{:S(2)}) collective-permute-start(bf16[25,16,128]{2,1,0:T(8,128)(2,1)S(1)} %get-tuple-element.39), channel_id=1, source_target_pairs={{0,4},{1,2},{2,1},{3,11},{4,0},{5,6},{6,5},{7,15},{8,12},{9,10},{1... | collective-permute-start | bytes 307208 | tf_op jit(solution)/shard_map/ppermute | solution.py:37
  3.5 0.1 collective-permute-start.1
  3.6 1.1 %collective-permute-start = (bf16[25,16,128]{2,1,0:T(8,128)(2,1)S(1)}, bf16[25,16,128]{2,1,0:T(8,128)(2,1)S(1)}, u32[]{:S(2)}, u32[]{:S(2)}) collective-permute-start(bf16[25,16,128]{2,1,0:T(8,128)(2,1)S(1)} %get-tuple-element.37), channel_id=1, source_target_pairs={{0,8},{1,5},{2,6},{3,7},{4,12},{5,1},{6,2},{7,3},{8,0},{9,13},{10,... | collective-permute-start | bytes 307208 | tf_op jit(solution)/shard_map/ppermute | solution.py:37
  4.7 2.4 %collective-permute-start.3 = (bf16[48,128]{1,0:T(8,128)(2,1)S(1)}, bf16[48,128]{1,0:T(8,128)(2,1)S(1)}, u32[]{:S(2)}, u32[]{:S(2)}) collective-permute-start(bf16[48,128]{1,0:T(8,128)(2,1)S(1)} %get-tuple-element.43), channel_id=1, source_target_pairs={{0,5},{1,4},{2,7},{3,6},{4,1},{5,0},{6,3},{7,2},{8,13},{9,12},{10,... | collective-permute-start | bytes 36872 | tf_op jit(solution)/shard_map/ppermute | solution.py:37
  7.1 0.5 %collective-permute-start.4 = (bf16[48,128]{1,0:T(8,128)(2,1)S(1)}, bf16[48,128]{1,0:T(8,128)(2,1)S(1)}, u32[]{:S(2)}, u32[]{:S(2)}) collective-permute-start(bf16[48,128]{1,0:T(8,128)(2,1)S(1)} %get-tuple-element.44), channel_id=1, source_target_pairs={{0,8},{1,6},{2,5},{3,11},{4,12},{5,2},{6,1},{7,15},{8,0},{9,14},{1... | collective-permute-start | bytes 36872 | tf_op jit(solution)/shard_map/ppermute | solution.py:37
  7.6 0.0 collective-permute-done.2.refs_0_.refs_2_
  7.6 0.0 collective-permute-done.1.refs_1_
  7.6 0.0 collective-permute-done.refs_0_
  7.6 1.5 %inner.1 = (f32[6,192,128]{2,1,0:T(8,128)S(1)}, f32[6,192,128]{2,1,0:T(8,128)S(1)}, f32[4,192,128]{2,1,0:T(8,128)S(1)}, f32[12,192,128]{2,1,0:T(8,128)S(1)}, f32...) custom-call(f32[576,128]{1,0:T(8,128)S(1)} %get-tuple-element.31.now, ...), custom_call_target="tpu_custom_call" | custom-call | flops 3072000 | bytes 3072000 | tf_op jit(solution)/shard_map/inner/pallas_call | solution.py:849
  9.1 0.0 collective-permute-done.3.refs_0_
  9.1 1.5 %collective-permute-done.4.refs_1_ = bf16[48,128]{1,0:T(8,128)(2,1)S(1)} collective-permute-done((bf16[48,128]{1,0:T(8,128)(2,1)S(1)}, bf16[48,128]{1,0:T(8,128)(2,1)S(1)}, u32[]{:S(2)}, u32[]{:S(2)}) %collective-permute-start.4) | collective-permute-done | bytes 12320 | tf_op jit(solution)/shard_map/ppermute | solution.py:37
  10.6 0.3 %edges.1 = (f32[6,64,128]{2,1,0:T(8,128)S(1)}, f32[32,128]{1,0:T(8,128)S(1)}, f32[32,128]{1,0:T(8,128)S(1)}, f32[32,128]{1,0:T(8,128)S(1)}, f32[32,128]{1,0:T(8,128)S(1)}) custom-call(bf16[48,128]{1,0:T(8,128)(2,1)S(1)} %collective-permute-done.3.refs_0_, bf16[48,128]{1,0:T(8,128)(2,1)S(1)} %collective-permute-done.4.refs_1_, ...), custom_call_target="tpu_custom_call" | custom-call | flops 1024000 | bytes 1024000 | tf_op jit(solution)/shard_map/edges/pallas_call | solution.py:868
  10.9 2.6 %collective-permute-start.5 = (f32[32,128]{1,0:T(8,128)S(1)}, f32[32,128]{1,0:T(8,128)S(1)}, u32[]{:S(2)}, u32[]{:S(2)}) collective-permute-start(f32[32,128]{1,0:T(8,128)S(1)} %get-tuple-element.53), channel_id=1, source_target_pairs={{0,24},{8,16},{16,8},{24,0},{1,25},{9,17},{17,9},{25,1},{2,26},{10... | collective-permute-start | bytes 49160 | tf_op jit(solution)/shard_map/ppermute | solution.py:883
  13.5 0.3 %collective-permute-start.6 = (f32[32,128]{1,0:T(8,128)S(1)}, f32[32,128]{1,0:T(8,128)S(1)}, u32[]{:S(2)}, u32[]{:S(2)}) collective-permute-start(f32[32,128]{1,0:T(8,128)S(1)} %get-tuple-element.54), channel_id=1, source_target_pairs={{0,16},{8,24},{16,0},{24,8},{1,17},{9,25},{17,1},{25,9},{2,18},{10... | collective-permute-start | bytes 49160 | tf_op jit(solution)/shard_map/ppermute | solution.py:883
  13.8 0.2 %collective-permute-start.7 = (f32[32,128]{1,0:T(8,128)S(1)}, f32[32,128]{1,0:T(8,128)S(1)}, u32[]{:S(2)}, u32[]{:S(2)}) collective-permute-start(f32[32,128]{1,0:T(8,128)S(1)} %get-tuple-element.55), channel_id=1, source_target_pairs={{0,8},{8,0},{16,24},{24,16},{1,9},{9,1},{17,25},{25,17},{2,10},{10... | collective-permute-start | bytes 49160 | tf_op jit(solution)/shard_map/ppermute | solution.py:883
  14.0 1.1 %second.1 = (f32[384,128]{1,0:T(8,128)}, f32[384,128]{1,0:T(8,128)}) custom-call(f32[576,128]{1,0:T(8,128)S(1)} %get-tuple-element.31.now, f32[576,128]{1,0:T(8,128)S(1)} %get-tuple-element.32.med.refs_9_, s32[1,1,128]{2,1,0:T(1,128)S(1)} %get-tuple-element.33.cells, f32[2,2,3,1,1,128]{5,4,3,2,1,0:T(1,128)S(1)} %get-tuple-element.34.force, ...), custom_call_target="tpu_custom_call" | custom-call | flops 1024000 | bytes 1024000 | tf_op jit(solution)/shard_map/second/pallas_call | solution.py:884
  15.1 0.2 %collective-permute-done.5.refs_1_ = f32[32,128]{1,0:T(8,128)S(1)} collective-permute-done((f32[32,128]{1,0:T(8,128)S(1)}, f32[32,128]{1,0:T(8,128)S(1)}, u32[]{:S(2)}, u32[]{:S(2)}) %collective-permute-start.5) | collective-permute-done | bytes 16416 | tf_op jit(solution)/shard_map/ppermute | solution.py:883
  15.3 0.8 %collective-permute-done.6.refs_2_ = f32[32,128]{1,0:T(8,128)S(1)} collective-permute-done((f32[32,128]{1,0:T(8,128)S(1)}, f32[32,128]{1,0:T(8,128)S(1)}, u32[]{:S(2)}, u32[]{:S(2)}) %collective-permute-start.6) | collective-permute-done | bytes 16416 | tf_op jit(solution)/shard_map/ppermute | solution.py:883
  16.1 0.0 collective-permute-done.7.refs_3_
  16.1 0.7 %finish.1 = (f32[64,32]{1,0:T(8,128)}, f32[64,32]{1,0:T(8,128)}) custom-call(f32[32,128]{1,0:T(8,128)S(1)} %get-tuple-element.52.refs_0_, f32[32,128]{1,0:T(8,128)S(1)} %collective-permute-done.5.refs_1_, f32[32,128]{1,0:T(8,128)S(1)} %collective-permute-done.6.refs_2_, f32[32,128]{1,0:T(8,128)S(1)} %collective-permute-done.7.refs_3_), custom_call_target="tpu_custom_call" | custom-call | flops 1024000 | bytes 1024000 | tf_op jit(solution)/shard_map/finish/pallas_call | solution.py:890
  (2 shorter events, 0.0 us)
Async XLA Ops:
  2.1 5.5 %collective-permute-start.2 = (bf16[25,16,128]{2,1,0:T(8,128)(2,1)S(1)}, bf16[25,16,128]{2,1,0:T(8,128)(2,1)S(1)}, u32[]{:S(2)}, u32[]{:S(2)}) collective-permute-start(bf16[25,16,128]{2,1,0:T(8,128)(2,1)S(1)} %get-tuple-element.39), channel_id=1, source_target_pairs={{0,4},{1,2},{2,1},{3,11},{4,0},{5,6},{6,5},{7,15},{8,12},{9,10},{1... | collective-permute-start | bytes 307208 | tf_op jit(solution)/shard_map/ppermute | solution.py:37
  3.5 4.1 %collective-permute-start.1 = (bf16[25,16,128]{2,1,0:T(8,128)(2,1)S(1)}, bf16[25,16,128]{2,1,0:T(8,128)(2,1)S(1)}, u32[]{:S(2)}, u32[]{:S(2)}) collective-permute-start(bf16[25,16,128]{2,1,0:T(8,128)(2,1)S(1)} %get-tuple-element.38), channel_id=1, source_target_pairs={{0,1},{1,0},{2,3},{3,2},{4,5},{5,4},{6,7},{7,6},{8,9},{9,8},{10,11... | collective-permute-start | bytes 307208 | tf_op jit(solution)/shard_map/ppermute | solution.py:37
  3.6 4.0 %collective-permute-start = (bf16[25,16,128]{2,1,0:T(8,128)(2,1)S(1)}, bf16[25,16,128]{2,1,0:T(8,128)(2,1)S(1)}, u32[]{:S(2)}, u32[]{:S(2)}) collective-permute-start(bf16[25,16,128]{2,1,0:T(8,128)(2,1)S(1)} %get-tuple-element.37), channel_id=1, source_target_pairs={{0,8},{1,5},{2,6},{3,7},{4,12},{5,1},{6,2},{7,3},{8,0},{9,13},{10,... | collective-permute-start | bytes 307208 | tf_op jit(solution)/shard_map/ppermute | solution.py:37
  4.7 4.4 %collective-permute-start.3 = (bf16[48,128]{1,0:T(8,128)(2,1)S(1)}, bf16[48,128]{1,0:T(8,128)(2,1)S(1)}, u32[]{:S(2)}, u32[]{:S(2)}) collective-permute-start(bf16[48,128]{1,0:T(8,128)(2,1)S(1)} %get-tuple-element.43), channel_id=1, source_target_pairs={{0,5},{1,4},{2,7},{3,6},{4,1},{5,0},{6,3},{7,2},{8,13},{9,12},{10,... | collective-permute-start | bytes 36872 | tf_op jit(solution)/shard_map/ppermute | solution.py:37
  7.1 3.4 %collective-permute-start.4 = (bf16[48,128]{1,0:T(8,128)(2,1)S(1)}, bf16[48,128]{1,0:T(8,128)(2,1)S(1)}, u32[]{:S(2)}, u32[]{:S(2)}) collective-permute-start(bf16[48,128]{1,0:T(8,128)(2,1)S(1)} %get-tuple-element.44), channel_id=1, source_target_pairs={{0,8},{1,6},{2,5},{3,11},{4,12},{5,2},{6,1},{7,15},{8,0},{9,14},{1... | collective-permute-start | bytes 36872 | tf_op jit(solution)/shard_map/ppermute | solution.py:37
  10.9 4.4 %collective-permute-start.5 = (f32[32,128]{1,0:T(8,128)S(1)}, f32[32,128]{1,0:T(8,128)S(1)}, u32[]{:S(2)}, u32[]{:S(2)}) collective-permute-start(f32[32,128]{1,0:T(8,128)S(1)} %get-tuple-element.53), channel_id=1, source_target_pairs={{0,24},{8,16},{16,8},{24,0},{1,25},{9,17},{17,9},{25,1},{2,26},{10... | collective-permute-start | bytes 49160 | tf_op jit(solution)/shard_map/ppermute | solution.py:883
  13.5 2.6 %collective-permute-start.6 = (f32[32,128]{1,0:T(8,128)S(1)}, f32[32,128]{1,0:T(8,128)S(1)}, u32[]{:S(2)}, u32[]{:S(2)}) collective-permute-start(f32[32,128]{1,0:T(8,128)S(1)} %get-tuple-element.54), channel_id=1, source_target_pairs={{0,16},{8,24},{16,0},{24,8},{1,17},{9,25},{17,1},{25,9},{2,18},{10... | collective-permute-start | bytes 49160 | tf_op jit(solution)/shard_map/ppermute | solution.py:883
  13.8 2.3 %collective-permute-start.7 = (f32[32,128]{1,0:T(8,128)S(1)}, f32[32,128]{1,0:T(8,128)S(1)}, u32[]{:S(2)}, u32[]{:S(2)}) collective-permute-start(f32[32,128]{1,0:T(8,128)S(1)} %get-tuple-element.55), channel_id=1, source_target_pairs={{0,8},{8,0},{16,24},{24,16},{1,9},{9,1},{17,25},{25,17},{2,10},{10... | collective-permute-start | bytes 49160 | tf_op jit(solution)/shard_map/ppermute | solution.py:883

commit v11 on v10

--- a/solution.py
+++ b/solution.py
@@ -410,7 +410,8 @@
     for row in range(1, 11):
         values = coefficients(lambda m, r: row_of(medium, m, r), row, row < 10)
         for name, value in values.items():
-            coef[COEFFICIENTS.index(name), pl.ds(row * ROWS, ROWS), :] = value
+            if 1 < row < 10 or name in ("own_x", "other_x", "cross", "cross_z"):
+                coef[COEFFICIENTS.index(name), pl.ds(row * ROWS, ROWS), :] = value
 
     def faces(name, row):
         if name == "inverse":
@@ -664,7 +665,7 @@
     field_row, medium_row = row_with(outer, here), row_with(outer_medium, medium)
     for k, row in enumerate((9, 10, 11)):
         for name, value in coefficients(medium_row, row, row < 11).items():
-            if row > 9 or name in ("own_x", "other_x"):
+            if row == 10 or name in (("own_x", "other_x") if row == 9 else ("cross", "cross_z")):
                 outer_coef[COEFFICIENTS.index(name), pl.ds(k * ROWS, ROWS), :] = value
 
     def faces(name, row):

time: 17 us -> 17 us (level)
  no operation moved by 1% of the time
where the time goes in v11:
time: 17 us; the launch traced here: 16.8 us
  starting transfers between devices  8.54 us (50%)
  Pallas kernels  5.09 us (30%)
  waiting for transfers between devices  2.51 us (15%)
  between operations  0.68 us (4%)
    ppermute x5, starting transfers between devices, swap(): return lax.ppermute(values, names, pairs)  5.47 us
    ppermute x3, starting transfers between devices, body(): pieces.append(lax.ppermute(sent[m - 1], 'ev', pairs))  3.07 us
    ppermute x5, waiting for transfers between devices, swap(): return lax.ppermute(values, names, pairs)  1.49 us
    pallas_call x1, Pallas kernels, body(): call(functools.partial(pack_kernel, events, x_rounds, y_rounds), [roomy,...  1.48 us
    pallas_call x1, Pallas kernels, body(): call(functools.partial(inner_kernel, events, x_rounds, y_rounds, shares),...  1.47 us
    pallas_call x1, Pallas kernels, body(): call(functools.partial(second_kernel, events), [flat, flat], [pltpu.VMEM]...  1.1 us
    ppermute x3, waiting for transfers between devices, body(): pieces.append(lax.ppermute(sent[m - 1], 'ev', pairs))  1.02 us
    pallas_call x1, Pallas kernels, body(): call(functools.partial(finish_kernel, shares, 1.0 / (events * shares)), [...  0.7 us
  transfers between devices with their start and end apart: 8, of which 3 were waited for; matrix products, arithmetic and copies ran while one was open for 0% of the time, Pallas kernels for 15%

profile of v11, /device:TPU:9, one launch (start us, length us, event | category | flops | bytes accessed | tf_op | source)
XLA Modules:
  0.0 16.8 jit_solution(6865550107690618279)
XLA Ops:
  0.6 1.5 %pack.1 = (f32[576,128]{1,0:T(8,128)S(1)}, bf16[2,12,8,8,128]{4,3,2,1,0:T(8,128)(2,1)S(1)}, f32[576,128]{1,0:T(8,128)S(1)}, s32[1,1,128]{2,1,0:T(1,128)S(1)}, f3...) custom-call(f32[384,128]{1,0:T(8,128)} %bitcast.11, ...), custom_call_target="tpu_custom_call" | custom-call | flops 8192000 | bytes 8192000 | tf_op jit(solution)/shard_map/pack/pallas_call | solution.py:813
  2.1 1.4 %collective-permute-start.2 = (bf16[25,16,128]{2,1,0:T(8,128)(2,1)S(1)}, bf16[25,16,128]{2,1,0:T(8,128)(2,1)S(1)}, u32[]{:S(2)}, u32[]{:S(2)}) collective-permute-start(bf16[25,16,128]{2,1,0:T(8,128)(2,1)S(1)} %get-tuple-element.39), channel_id=1, source_target_pairs={{0,4},{1,2},{2,1},{3,11},{4,0},{5,6},{6,5},{7,15},{8,12},{9,10},{1... | collective-permute-start | bytes 307208 | tf_op jit(solution)/shard_map/ppermute | solution.py:37
  3.5 0.1 collective-permute-start.1
  3.6 1.1 %collective-permute-start = (bf16[25,16,128]{2,1,0:T(8,128)(2,1)S(1)}, bf16[25,16,128]{2,1,0:T(8,128)(2,1)S(1)}, u32[]{:S(2)}, u32[]{:S(2)}) collective-permute-start(bf16[25,16,128]{2,1,0:T(8,128)(2,1)S(1)} %get-tuple-element.37), channel_id=1, source_target_pairs={{0,8},{1,5},{2,6},{3,7},{4,12},{5,1},{6,2},{7,3},{8,0},{9,13},{10,... | collective-permute-start | bytes 307208 | tf_op jit(solution)/shard_map/ppermute | solution.py:37
  4.7 2.4 %collective-permute-start.3 = (bf16[48,128]{1,0:T(8,128)(2,1)S(1)}, bf16[48,128]{1,0:T(8,128)(2,1)S(1)}, u32[]{:S(2)}, u32[]{:S(2)}) collective-permute-start(bf16[48,128]{1,0:T(8,128)(2,1)S(1)} %get-tuple-element.43), channel_id=1, source_target_pairs={{0,5},{1,4},{2,7},{3,6},{4,1},{5,0},{6,3},{7,2},{8,13},{9,12},{10,... | collective-permute-start | bytes 36872 | tf_op jit(solution)/shard_map/ppermute | solution.py:37
  7.1 0.5 %collective-permute-start.4 = (bf16[48,128]{1,0:T(8,128)(2,1)S(1)}, bf16[48,128]{1,0:T(8,128)(2,1)S(1)}, u32[]{:S(2)}, u32[]{:S(2)}) collective-permute-start(bf16[48,128]{1,0:T(8,128)(2,1)S(1)} %get-tuple-element.44), channel_id=1, source_target_pairs={{0,8},{1,6},{2,5},{3,11},{4,12},{5,2},{6,1},{7,15},{8,0},{9,14},{1... | collective-permute-start | bytes 36872 | tf_op jit(solution)/shard_map/ppermute | solution.py:37
  7.6 0.0 collective-permute-done.2.refs_0_.refs_2_
  7.6 0.0 collective-permute-done.1.refs_1_
  7.6 0.0 collective-permute-done.refs_0_
  7.6 1.5 %inner.1 = (f32[6,192,128]{2,1,0:T(8,128)S(1)}, f32[6,192,128]{2,1,0:T(8,128)S(1)}, f32[4,192,128]{2,1,0:T(8,128)S(1)}, f32[12,192,128]{2,1,0:T(8,128)S(1)}, f32...) custom-call(f32[576,128]{1,0:T(8,128)S(1)} %get-tuple-element.31.now, ...), custom_call_target="tpu_custom_call" | custom-call | flops 3072000 | bytes 3072000 | tf_op jit(solution)/shard_map/inner/pallas_call | solution.py:850
  9.1 0.0 collective-permute-done.3.refs_0_
  9.1 1.5 %collective-permute-done.4.refs_1_ = bf16[48,128]{1,0:T(8,128)(2,1)S(1)} collective-permute-done((bf16[48,128]{1,0:T(8,128)(2,1)S(1)}, bf16[48,128]{1,0:T(8,128)(2,1)S(1)}, u32[]{:S(2)}, u32[]{:S(2)}) %collective-permute-start.4) | collective-permute-done | bytes 12320 | tf_op jit(solution)/shard_map/ppermute | solution.py:37
  10.6 0.3 %edges.1 = (f32[6,64,128]{2,1,0:T(8,128)S(1)}, f32[32,128]{1,0:T(8,128)S(1)}, f32[32,128]{1,0:T(8,128)S(1)}, f32[32,128]{1,0:T(8,128)S(1)}, f32[32,128]{1,0:T(8,128)S(1)}) custom-call(bf16[48,128]{1,0:T(8,128)(2,1)S(1)} %collective-permute-done.3.refs_0_, bf16[48,128]{1,0:T(8,128)(2,1)S(1)} %collective-permute-done.4.refs_1_, ...), custom_call_target="tpu_custom_call" | custom-call | flops 1024000 | bytes 1024000 | tf_op jit(solution)/shard_map/edges/pallas_call | solution.py:869
  10.9 2.6 %collective-permute-start.5 = (f32[32,128]{1,0:T(8,128)S(1)}, f32[32,128]{1,0:T(8,128)S(1)}, u32[]{:S(2)}, u32[]{:S(2)}) collective-permute-start(f32[32,128]{1,0:T(8,128)S(1)} %get-tuple-element.53), channel_id=1, source_target_pairs={{0,24},{8,16},{16,8},{24,0},{1,25},{9,17},{17,9},{25,1},{2,26},{10... | collective-permute-start | bytes 49160 | tf_op jit(solution)/shard_map/ppermute | solution.py:884
  13.5 0.3 %collective-permute-start.6 = (f32[32,128]{1,0:T(8,128)S(1)}, f32[32,128]{1,0:T(8,128)S(1)}, u32[]{:S(2)}, u32[]{:S(2)}) collective-permute-start(f32[32,128]{1,0:T(8,128)S(1)} %get-tuple-element.54), channel_id=1, source_target_pairs={{0,16},{8,24},{16,0},{24,8},{1,17},{9,25},{17,1},{25,9},{2,18},{10... | collective-permute-start | bytes 49160 | tf_op jit(solution)/shard_map/ppermute | solution.py:884
  13.8 0.2 %collective-permute-start.7 = (f32[32,128]{1,0:T(8,128)S(1)}, f32[32,128]{1,0:T(8,128)S(1)}, u32[]{:S(2)}, u32[]{:S(2)}) collective-permute-start(f32[32,128]{1,0:T(8,128)S(1)} %get-tuple-element.55), channel_id=1, source_target_pairs={{0,8},{8,0},{16,24},{24,16},{1,9},{9,1},{17,25},{25,17},{2,10},{10... | collective-permute-start | bytes 49160 | tf_op jit(solution)/shard_map/ppermute | solution.py:884
  14.0 1.1 %second.1 = (f32[384,128]{1,0:T(8,128)}, f32[384,128]{1,0:T(8,128)}) custom-call(f32[576,128]{1,0:T(8,128)S(1)} %get-tuple-element.31.now, f32[576,128]{1,0:T(8,128)S(1)} %get-tuple-element.32.med.refs_9_, s32[1,1,128]{2,1,0:T(1,128)S(1)} %get-tuple-element.33.cells, f32[2,2,3,1,1,128]{5,4,3,2,1,0:T(1,128)S(1)} %get-tuple-element.34.force, ...), custom_call_target="tpu_custom_call" | custom-call | flops 1024000 | bytes 1024000 | tf_op jit(solution)/shard_map/second/pallas_call | solution.py:885
  15.1 0.2 %collective-permute-done.5.refs_1_ = f32[32,128]{1,0:T(8,128)S(1)} collective-permute-done((f32[32,128]{1,0:T(8,128)S(1)}, f32[32,128]{1,0:T(8,128)S(1)}, u32[]{:S(2)}, u32[]{:S(2)}) %collective-permute-start.5) | collective-permute-done | bytes 16416 | tf_op jit(solution)/shard_map/ppermute | solution.py:884
  15.3 0.8 %collective-permute-done.6.refs_2_ = f32[32,128]{1,0:T(8,128)S(1)} collective-permute-done((f32[32,128]{1,0:T(8,128)S(1)}, f32[32,128]{1,0:T(8,128)S(1)}, u32[]{:S(2)}, u32[]{:S(2)}) %collective-permute-start.6) | collective-permute-done | bytes 16416 | tf_op jit(solution)/shard_map/ppermute | solution.py:884
  16.1 0.0 collective-permute-done.7.refs_3_
  16.1 0.7 %finish.1 = (f32[64,32]{1,0:T(8,128)}, f32[64,32]{1,0:T(8,128)}) custom-call(f32[32,128]{1,0:T(8,128)S(1)} %get-tuple-element.52.refs_0_, f32[32,128]{1,0:T(8,128)S(1)} %collective-permute-done.5.refs_1_, f32[32,128]{1,0:T(8,128)S(1)} %collective-permute-done.6.refs_2_, f32[32,128]{1,0:T(8,128)S(1)} %collective-permute-done.7.refs_3_), custom_call_target="tpu_custom_call" | custom-call | flops 1024000 | bytes 1024000 | tf_op jit(solution)/shard_map/finish/pallas_call | solution.py:891
  (2 shorter events, 0.0 us)
Async XLA Ops:
  2.1 5.5 %collective-permute-start.2 = (bf16[25,16,128]{2,1,0:T(8,128)(2,1)S(1)}, bf16[25,16,128]{2,1,0:T(8,128)(2,1)S(1)}, u32[]{:S(2)}, u32[]{:S(2)}) collective-permute-start(bf16[25,16,128]{2,1,0:T(8,128)(2,1)S(1)} %get-tuple-element.39), channel_id=1, source_target_pairs={{0,4},{1,2},{2,1},{3,11},{4,0},{5,6},{6,5},{7,15},{8,12},{9,10},{1... | collective-permute-start | bytes 307208 | tf_op jit(solution)/shard_map/ppermute | solution.py:37
  3.5 4.1 %collective-permute-start.1 = (bf16[25,16,128]{2,1,0:T(8,128)(2,1)S(1)}, bf16[25,16,128]{2,1,0:T(8,128)(2,1)S(1)}, u32[]{:S(2)}, u32[]{:S(2)}) collective-permute-start(bf16[25,16,128]{2,1,0:T(8,128)(2,1)S(1)} %get-tuple-element.38), channel_id=1, source_target_pairs={{0,1},{1,0},{2,3},{3,2},{4,5},{5,4},{6,7},{7,6},{8,9},{9,8},{10,11... | collective-permute-start | bytes 307208 | tf_op jit(solution)/shard_map/ppermute | solution.py:37
  3.6 4.0 %collective-permute-start = (bf16[25,16,128]{2,1,0:T(8,128)(2,1)S(1)}, bf16[25,16,128]{2,1,0:T(8,128)(2,1)S(1)}, u32[]{:S(2)}, u32[]{:S(2)}) collective-permute-start(bf16[25,16,128]{2,1,0:T(8,128)(2,1)S(1)} %get-tuple-element.37), channel_id=1, source_target_pairs={{0,8},{1,5},{2,6},{3,7},{4,12},{5,1},{6,2},{7,3},{8,0},{9,13},{10,... | collective-permute-start | bytes 307208 | tf_op jit(solution)/shard_map/ppermute | solution.py:37
  4.7 4.4 %collective-permute-start.3 = (bf16[48,128]{1,0:T(8,128)(2,1)S(1)}, bf16[48,128]{1,0:T(8,128)(2,1)S(1)}, u32[]{:S(2)}, u32[]{:S(2)}) collective-permute-start(bf16[48,128]{1,0:T(8,128)(2,1)S(1)} %get-tuple-element.43), channel_id=1, source_target_pairs={{0,5},{1,4},{2,7},{3,6},{4,1},{5,0},{6,3},{7,2},{8,13},{9,12},{10,... | collective-permute-start | bytes 36872 | tf_op jit(solution)/shard_map/ppermute | solution.py:37
  7.1 3.4 %collective-permute-start.4 = (bf16[48,128]{1,0:T(8,128)(2,1)S(1)}, bf16[48,128]{1,0:T(8,128)(2,1)S(1)}, u32[]{:S(2)}, u32[]{:S(2)}) collective-permute-start(bf16[48,128]{1,0:T(8,128)(2,1)S(1)} %get-tuple-element.44), channel_id=1, source_target_pairs={{0,8},{1,6},{2,5},{3,11},{4,12},{5,2},{6,1},{7,15},{8,0},{9,14},{1... | collective-permute-start | bytes 36872 | tf_op jit(solution)/shard_map/ppermute | solution.py:37
  10.9 4.4 %collective-permute-start.5 = (f32[32,128]{1,0:T(8,128)S(1)}, f32[32,128]{1,0:T(8,128)S(1)}, u32[]{:S(2)}, u32[]{:S(2)}) collective-permute-start(f32[32,128]{1,0:T(8,128)S(1)} %get-tuple-element.53), channel_id=1, source_target_pairs={{0,24},{8,16},{16,8},{24,0},{1,25},{9,17},{17,9},{25,1},{2,26},{10... | collective-permute-start | bytes 49160 | tf_op jit(solution)/shard_map/ppermute | solution.py:884
  13.5 2.6 %collective-permute-start.6 = (f32[32,128]{1,0:T(8,128)S(1)}, f32[32,128]{1,0:T(8,128)S(1)}, u32[]{:S(2)}, u32[]{:S(2)}) collective-permute-start(f32[32,128]{1,0:T(8,128)S(1)} %get-tuple-element.54), channel_id=1, source_target_pairs={{0,16},{8,24},{16,0},{24,8},{1,17},{9,25},{17,1},{25,9},{2,18},{10... | collective-permute-start | bytes 49160 | tf_op jit(solution)/shard_map/ppermute | solution.py:884
  13.8 2.3 %collective-permute-start.7 = (f32[32,128]{1,0:T(8,128)S(1)}, f32[32,128]{1,0:T(8,128)S(1)}, u32[]{:S(2)}, u32[]{:S(2)}) collective-permute-start(f32[32,128]{1,0:T(8,128)S(1)} %get-tuple-element.55), channel_id=1, source_target_pairs={{0,8},{8,0},{16,24},{24,16},{1,9},{9,1},{17,25},{25,17},{2,10},{10... | collective-permute-start | bytes 49160 | tf_op jit(solution)/shard_map/ppermute | solution.py:884
